TPU v7x, 32 devices: a whole 2x2x4 slice. The times are simulated.
32 devices in a mesh: dp: 16 (over z, y, x), seq: 2 (over core).
Axes of the slice: x: 2, y: 2, z: 4, core: 2. Of those that a mesh axis runs over, the one named last changes fastest.
Arguments:
- layer_input: bfloat16 [16, 512, 768], P('dp', 'seq'), may hold values from -6 to 6
- encoder_states: bfloat16 [16, 3, 1500, 768], P('dp', None, 'seq'), may hold values from -6 to 6
- clip_lengths: int32 [16, 3], P('dp'), may hold values from 1 to 448, as said below
- out_grad: bfloat16 [16, 512, 768], P('dp', 'seq'), may hold values from -6 to 6
- self_weights: bfloat16 [768, 3072], P(('dp', 'seq')), may hold values from -2 to 2
- cross_weights: bfloat16 [768, 3072], P(('dp', 'seq')), may hold values from -2 to 2
- up_weights: bfloat16 [768, 3072], P(('dp', 'seq')), may hold values from -0.21875 to 0.21875
- down_weights: bfloat16 [3072, 768], P(('dp', 'seq')), may hold values from -0.15625 to 0.15625
- up_bias: bfloat16 [3072], P(('dp', 'seq')), may hold values from -3 to 3
- down_bias: bfloat16 [768], P(('dp', 'seq')), may hold values from -3 to 3
- vectors: bfloat16 [768, 12], P(('dp', 'seq')), may hold values from -2 to 2
Outputs:
- layer_output: bfloat16 [16, 512, 768], P('dp', 'seq')
- input_grad: float32 [16, 512, 768], P('dp', 'seq')
- encoder_grad: float32 [16, 3, 1500, 768], P('dp', None, 'seq')
- self_weights_grad: float32 [768, 3072], P(('dp', 'seq'))
- cross_weights_grad: float32 [768, 3072], P(('dp', 'seq'))
- up_weights_grad: float32 [768, 3072], P(('dp', 'seq'))
- down_weights_grad: float32 [3072, 768], P(('dp', 'seq'))
- up_bias_grad: float32 [3072], P(('dp', 'seq'))
- down_bias_grad: float32 [768], P(('dp', 'seq'))
- vectors_grad: float32 [768, 12], P(('dp', 'seq'))
Inputs may be any that keep to these rules, and one draw needn't show every extreme that they name: `clip_lengths`: each row's 3 clips lie end to end from the row's first token, in order, and take at most 512 tokens together; the rest of the row is padding. Every row has a clip of exactly 448 tokens.
All inputs are finite; a program needn't handle non-finite values.
Results may differ from a plain program's by a relative error of at most 0.019.
Values may be sent and summed in bfloat16 or wider, within the bound.
A program may use at most 192 MiB of HBM per device.

v0:
```python
import functools

import jax
import jax.numpy as jnp
from jax import lax
from jax.experimental import pallas as pl
from jax.experimental.pallas import tpu as pltpu
from jax.sharding import PartitionSpec as P

HEAD_DIM = 64
CLIPS = 3
MESH = pl.DeviceIdType.MESH
NT = (((1,), (1,)), ((), ()))
NN = (((1,), (0,)), ((), ()))


def dot(left, right, dims):
    return lax.dot_general(left, right, dims, preferred_element_type=jnp.float32)


def one_head(values, h):
    lane = lax.broadcasted_iota(jnp.int32, values.shape, 1)
    return jnp.where((lane >= 64) == (h == 1), values, jnp.zeros_like(values))


def self_forward_kernel(q_ref, k_ref, v_ref, bias_ref, out_ref, lse_ref):
    keys = k_ref[...]
    values_t = v_ref[...].T
    halves = []
    for h in range(2):
        scores = dot(keys, one_head(q_ref[...], h), NT) + bias_ref[...]
        peak = jnp.max(scores, 0, keepdims=True)
        terms = jnp.exp(scores - peak)
        total = jnp.sum(terms, 0, keepdims=True)
        result = dot(values_t[h * 64:(h + 1) * 64], terms.astype(jnp.bfloat16), NN)
        halves.append(result / total)
        lse_ref[0, h:h + 1] = peak + jnp.log(total)
    out_ref[...] = jnp.concatenate(halves, 0).T.astype(out_ref.dtype)


def self_forward(q, kv, bias):
    toks, width = q.shape
    keys, pairs = kv.shape[0], width // 128
    return pl.pallas_call(
        self_forward_kernel,
        grid=(width // 128,),
        in_specs=[
            pl.BlockSpec((toks, 128), lambda j: (0, j)),
            pl.BlockSpec((keys, 128), lambda j: (0, j)),
            pl.BlockSpec((keys, 128), lambda j: (0, j + pairs)),
            pl.BlockSpec((keys, toks), lambda j: (0, 0)),
        ],
        out_specs=[
            pl.BlockSpec((toks, 128), lambda j: (0, j)),
            pl.BlockSpec((1, 2, toks), lambda j: (j, 0, 0)),
        ],
        out_shape=[
            jax.ShapeDtypeStruct((toks, width), jnp.float32),
            jax.ShapeDtypeStruct((width // 128, 2, toks), jnp.float32),
        ],
        compiler_params=pltpu.CompilerParams(vmem_limit_bytes=48 * 2**20),
        name="self_forward",
    )(q, kv, kv, bias)


def self_backward_kernel(q_ref, k_ref, v_ref, bias_ref, lse_ref, inner_ref, g_ref, dq_ref, dk_ref, dv_ref):
    keys, values = k_ref[...], v_ref[...]
    keys_t = keys.T
    grad_k = grad_v = None
    halves = []
    for h in range(2):
        query, grad = one_head(q_ref[...], h), one_head(g_ref[...], h)
        weights = jnp.exp(dot(keys, query, NT) + bias_ref[...] - lse_ref[0, h:h + 1])
        part = dot(weights.astype(jnp.bfloat16), grad, NN)
        grad_v = part if grad_v is None else grad_v + part
        grad_s = (weights * (dot(values, grad, NT) - inner_ref[0, h:h + 1])).astype(jnp.bfloat16)
        part = dot(grad_s, query, NN)
        grad_k = part if grad_k is None else grad_k + part
        halves.append(dot(keys_t[h * 64:(h + 1) * 64], grad_s, NN))
    dq_ref[...] = (jnp.concatenate(halves, 0) * 0.125).T
    dk_ref[...] = grad_k
    dv_ref[...] = grad_v


def self_backward(q, kv, bias, lse, inner, grad):
    toks, width = q.shape
    keys, pairs = kv.shape[0], width // 128
    tok_spec = pl.BlockSpec((toks, 128), lambda j: (0, j))
    key_spec = pl.BlockSpec((keys, 128), lambda j: (0, j))
    row_spec = pl.BlockSpec((1, 2, toks), lambda j: (j, 0, 0))
    return pl.pallas_call(
        self_backward_kernel,
        grid=(width // 128,),
        in_specs=[tok_spec, key_spec, pl.BlockSpec((keys, 128), lambda j: (0, j + pairs)), pl.BlockSpec((keys, toks), lambda j: (0, 0)), row_spec, row_spec, tok_spec],
        out_specs=[tok_spec, key_spec, key_spec],
        out_shape=[
            jax.ShapeDtypeStruct((toks, width), jnp.float32),
            jax.ShapeDtypeStruct((keys, width), jnp.float32),
            jax.ShapeDtypeStruct((keys, width), jnp.float32),
        ],
        compiler_params=pltpu.CompilerParams(vmem_limit_bytes=48 * 2**20),
        name="self_backward",
    )(q, kv, kv, bias, lse, inner, grad)


def cross_forward_kernel(which, q_ref, k_ref, v_ref, seg_ref, out_ref, stat_ref, acc_ref):
    def attend(clip, values_t, query, h):
        scores = dot(k_ref[clip], query, NT)
        peak = jnp.max(scores, 0, keepdims=True)
        terms = jnp.exp(scores - peak)
        total = jnp.sum(terms, 0, keepdims=True)
        result = dot(values_t[h * 64:(h + 1) * 64], terms.astype(jnp.bfloat16), NN)
        return result / total, peak, total

    values_t = v_ref[0].T
    for h in range(2):
        mine = seg_ref[...] == 0
        result, peak, total = attend(0, values_t, one_head(q_ref[...], h), h)
        acc_ref[h * 64:(h + 1) * 64] = jnp.where(mine, result, 0.0)
        stat_ref[0, h:h + 1] = jnp.where(mine, peak, 0.0)
        stat_ref[0, 2 + h:3 + h] = jnp.where(mine, total, 1.0)
    for clip in (1, 2):
        cols = pl.ds(pl.multiple_of(which[clip - 1] * 128, 128), 128)
        values_t = v_ref[clip].T
        mine = seg_ref[:, cols] == clip
        for h in range(2):
            result, peak, total = attend(clip, values_t, one_head(q_ref[cols], h), h)
            rows = slice(h * 64, (h + 1) * 64)
            acc_ref[rows, cols] = jnp.where(mine, result, acc_ref[rows, cols])
            stat_ref[0, h:h + 1, cols] = jnp.where(mine, peak, stat_ref[0, h:h + 1, cols])
            stat_ref[0, 2 + h:3 + h, cols] = jnp.where(mine, total, stat_ref[0, 2 + h:3 + h, cols])
    out_ref[...] = acc_ref[...].T


def cross_forward(which, q, kv, seg):
    toks, width = q.shape
    clips, frames = kv.shape[:2]
    pairs = width // 128
    kv_spec = pl.BlockSpec((clips, frames, 128), lambda j, w: (0, 0, j))
    v_spec = pl.BlockSpec((clips, frames, 128), lambda j, w: (0, 0, j + pairs))
    tok_spec = pl.BlockSpec((toks, 128), lambda j, w: (0, j))
    return pl.pallas_call(
        cross_forward_kernel,
        grid_spec=pltpu.PrefetchScalarGridSpec(
            num_scalar_prefetch=1,
            grid=(width // 128,),
            in_specs=[tok_spec, kv_spec, v_spec, pl.BlockSpec((1, toks), lambda j, w: (0, 0))],
            out_specs=[tok_spec, pl.BlockSpec((1, 4, toks), lambda j, w: (j, 0, 0))],
            scratch_shapes=[pltpu.VMEM((128, toks), jnp.float32)],
        ),
        out_shape=[
            jax.ShapeDtypeStruct((toks, width), jnp.float32),
            jax.ShapeDtypeStruct((width // 128, 4, toks), jnp.float32),
        ],
        compiler_params=pltpu.CompilerParams(vmem_limit_bytes=48 * 2**20),
        name="cross_forward",
    )(which, q, kv, kv, seg)


def cross_backward_kernel(which, q_ref, k_ref, v_ref, seg_ref, lse_ref, inner_ref, g_ref, dq_ref, dk_ref, dv_ref, acc_ref):
    def back(clip, keys_t, cols, h):
        query, grad = one_head(q_ref[cols], h), one_head(g_ref[cols], h)
        lse = jnp.where(seg_ref[:, cols] == clip, lse_ref[0, h:h + 1, cols], 1e30)
        weights = jnp.exp(dot(k_ref[clip], query, NT) - lse)
        grad_v = dot(weights.astype(jnp.bfloat16), grad, NN)
        grad_s = (weights * (dot(v_ref[clip], grad, NT) - inner_ref[0, h:h + 1, cols])).astype(jnp.bfloat16)
        grad_k = dot(grad_s, query, NN)
        return dot(keys_t[h * 64:(h + 1) * 64], grad_s, NN), grad_k, grad_v

    for clip in range(3):
        cols = slice(None) if clip == 0 else pl.ds(pl.multiple_of(which[clip - 1] * 128, 128), 128)
        keys_t = k_ref[clip].T
        grad_q, grad_k, grad_v = zip(*(back(clip, keys_t, cols, h) for h in range(2)))
        grad_q = jnp.concatenate(grad_q, 0)
        if clip == 0:
            acc_ref[...] = grad_q
        else:
            acc_ref[:, cols] += grad_q
        dk_ref[clip] = (grad_k[0] + grad_k[1]).astype(jnp.bfloat16)
        dv_ref[clip] = (grad_v[0] + grad_v[1]).astype(jnp.bfloat16)
    dq_ref[...] = (acc_ref[...] * 0.125).T


def cross_backward(which, q, kv, seg, lse, inner, grad):
    toks, width = q.shape
    clips, frames = kv.shape[:2]
    pairs = width // 128
    kv_spec = pl.BlockSpec((clips, frames, 128), lambda j, w: (0, 0, j))
    v_spec = pl.BlockSpec((clips, frames, 128), lambda j, w: (0, 0, j + pairs))
    tok_spec = pl.BlockSpec((toks, 128), lambda j, w: (0, j))
    row_spec = pl.BlockSpec((1, 2, toks), lambda j, w: (j, 0, 0))
    return pl.pallas_call(
        cross_backward_kernel,
        grid_spec=pltpu.PrefetchScalarGridSpec(
            num_scalar_prefetch=1,
            grid=(width // 128,),
            in_specs=[tok_spec, kv_spec, v_spec, pl.BlockSpec((1, toks), lambda j, w: (0, 0)), row_spec, row_spec, tok_spec],
            out_specs=[tok_spec, kv_spec, kv_spec],
            scratch_shapes=[pltpu.VMEM((128, toks), jnp.float32)],
        ),
        out_shape=[
            jax.ShapeDtypeStruct((toks, width), jnp.float32),
            jax.ShapeDtypeStruct((clips, frames, width), jnp.bfloat16),
            jax.ShapeDtypeStruct((clips, frames, width), jnp.bfloat16),
        ],
        compiler_params=pltpu.CompilerParams(vmem_limit_bytes=48 * 2**20),
        name="cross_backward",
    )(which, q, kv, kv, seg, lse, inner, grad)


Z = 4


class Place:
    def __init__(self):
        self.dp = lax.axis_index("dp")
        self.core = lax.axis_index("seq")
        self.z = self.dp // 4
        self.p = self.dp % 4
        x, y = self.p % 2, self.p // 2
        px, py = self.p + 1 - 2 * x, self.p + 2 - 4 * y
        self.p_first = px * (1 - self.core) + py * self.core
        self.p_second = py * (1 - self.core) + px * self.core
        self.p_diag = 3 - self.p
        base = self.z * 4
        self.first = (base + self.p_first, self.core)
        self.second = (base + self.p_second, self.core)
        self.up = (lax.rem(self.dp + 4, 16), self.core)
        self.down = (lax.rem(self.dp + 12, 16), self.core)
        self.mate = (self.dp, 1 - self.core)
        self.has_up = self.z < Z - 1
        self.has_down = self.z > 0

    def greet(self):
        barrier = pltpu.get_barrier_semaphore()
        for target in (self.mate, self.first, self.second):
            pl.semaphore_signal(barrier, inc=1, device_id=target, device_id_type=MESH)

        @pl.when(self.has_up)
        def _():
            pl.semaphore_signal(barrier, inc=1, device_id=self.up, device_id_type=MESH)

        @pl.when(self.has_down)
        def _():
            pl.semaphore_signal(barrier, inc=1, device_id=self.down, device_id_type=MESH)

        pl.semaphore_wait(barrier, 3 + (self.z + 3) // 4 + (6 - self.z) // 4)


def when(cond, fn):
    if cond is None:
        fn()
    else:
        pl.when(cond)(fn)


def both(a, b):
    if a is None:
        return b
    if b is None:
        return a
    return jnp.logical_and(a, b)


HALF_COLS = {1: 768, 2: 1536, 3: 768, 4: 1536}


class Gather:
    def __init__(self, me, srcs, outs, send_sem, recv_sem, own_sem):
        self.me, self.srcs, self.outs = me, srcs, outs
        self.send_sem, self.recv_sem, self.own_sem = send_sem, recv_sem, own_sem
        self.sends = []
        self.tasks = []
        for m, times in enumerate(GATHER_TIMES):
            for time, task in zip(times, self.steps(m)):
                self.tasks.append((time, m, task))
        self.tasks.sort(key=lambda entry: entry[:2])

    def piece(self, m, chip, core):
        if m == 0:
            return self.outs[m].at[chip * 2 + core]
        if m == 5:
            return self.outs[m].at[pl.ds(pl.multiple_of(chip * 192 + core * 96, 96), 96)]
        rows = pl.ds(pl.multiple_of(chip * 48, 48), 48)
        return self.outs[m].at[rows, columns(core, HALF_COLS[m])]

    def sender(self, m, src, chip, target, cond):
        copy = pltpu.make_async_remote_copy(
            src_ref=src, dst_ref=self.piece(m, chip, self.me.core), send_sem=self.send_sem.at[len(self.sends)],
            recv_sem=self.recv_sem.at[m, chip * 2 + self.me.core], device_id=target, device_id_type=MESH)
        self.sends.append((cond, copy))
        return lambda: when(cond, copy.start)

    def arrival(self, m, chip, core, cond=None):
        piece = self.piece(m, chip, core)
        copy = pltpu.make_async_remote_copy(
            src_ref=piece, dst_ref=piece, send_sem=self.send_sem.at[0],
            recv_sem=self.recv_sem.at[m, chip * 2 + core], device_id=self.me.mate, device_id_type=MESH)
        return lambda: when(cond, copy.wait_recv)

    def forward(self, m, z, p, targets, cond=None):
        chip = z * 4 + p
        return [self.arrival(m, chip, self.me.core, cond)] + [
            self.sender(m, self.piece(m, chip, self.me.core), chip, target, both(cond, extra))
            for target, extra in targets
        ]

    def steps(self, m):
        me = self.me
        up, down, mate = (me.up, me.has_up), (me.down, me.has_down), (me.mate, None)
        first, second = (me.first, None), (me.second, None)

        def at(d, p, below_to, above_to):
            if d == 0:
                return self.forward(m, me.z, p, below_to)
            return self.forward(m, me.z - d, p, below_to, me.z - d >= 0) + self.forward(
                m, me.z + d, p, above_to, me.z + d < Z)

        begin = [self.sender(m, self.srcs[m], me.dp, *target) for target in (up, down, first, second, mate)]
        begin.append(pltpu.make_async_copy(self.srcs[m], self.piece(m, me.dp, me.core), self.own_sem.at[m]).start)
        steps = [begin]
        for d in range(1, Z + 1):
            line = at(d, me.p, [up, first, second, mate], [down, first, second, mate]) if d < Z else []
            steps.append(line + at(d - 1, me.p_first, [second, mate], [second, mate]))
        steps.append([act for p in (me.p_second, me.p_diag) for d in range(Z) for act in at(d, p, [mate], [mate])])
        return steps

    def run(self, entry):
        for act in entry[2]:
            act()

    def run_until(self, time):
        while self.tasks and self.tasks[0][0] <= time:
            self.run(self.tasks.pop(0))

    def take_until(self, time):
        taken = []
        while self.tasks and self.tasks[0][0] <= time:
            taken.append(self.tasks.pop(0))
        return taken

    def need(self, m):
        for entry in [e for e in self.tasks if e[1] == m]:
            self.run(entry)
        self.tasks = [e for e in self.tasks if e[1] != m]
        pltpu.make_async_copy(self.srcs[m], self.piece(m, self.me.dp, self.me.core), self.own_sem.at[m]).wait()
        for chip in range(16):
            self.arrival(m, chip, 1 - self.me.core)()

    def finish(self):
        for cond, copy in self.sends:
            when(cond, copy.wait_send)


GATHER_TIMES = (
    (1, 4.5, 8.5, 12.5, 16.5, 18.5),
    (0, 4, 8, 12, 16, 18),
    (2, 9, 14, 19, 24, 27),
    (10, 20, 25, 29, 33, 36),
    (20, 31, 38, 45, 51, 55),
    (32, 50, 58, 66, 73, 78),
)


def loop_with(gather, count, begin, length, body):
    due = [gather.take_until(begin + length * i) for i in range(count)]

    def turn(i, carry):
        for k, tasks in enumerate(due):
            if tasks:

                def run(tasks=tasks):
                    for task in tasks:
                        gather.run(task)

                pl.when(i == k)(run)
        body(i)
        return carry

    lax.fori_loop(0, count, turn, 0)


def norm_rows(values, gain, shift):
    average = jnp.mean(values, -1, keepdims=True)
    centred = values - average
    spread = jnp.mean(centred * centred, -1, keepdims=True)
    return centred * lax.rsqrt(spread + 1e-05) * gain + shift


def columns(j, size=128):
    return pl.ds(pl.multiple_of(j * size, size), size)


def forward_kernel(*refs):
    (group_ref, x_ref, frames_ref, bias_ref, seg_ref, small_in, self_in, cross_in, up_in, down_in) = refs[:10]
    (small_out, ckv_out, self_out, cqo_out, up_out, down_out, kv_out, vec_ref, normed_one_ref, query_ref, kv_row_ref,
     attended_ref, self_lse_ref, after_self_ref, normed_two_ref, row_query_ref, cross_lse_ref, mixed_ref,
     after_cross_ref, normed_three_ref) = refs[10:30]
    (half_wide, half_narrow, pair_wide, pair_narrow, small_vm, ckv_vm, self_vm, cqo_vm, kv_vm, acc_ref, stat_ref, part_ref, part_stat_ref, give_ref,
     give_stat_ref, take_ref, take_stat_ref, send_sem, recv_sem, own_sem, half_sems, mate_sems, load_sem) = refs[30:]
    me = Place()
    core = me.core
    width = x_ref.shape[1]
    toks = x_ref.shape[0]
    me.greet()

    def to_mate(src, dst, k):
        return pltpu.make_async_remote_copy(
            src_ref=src, dst_ref=dst, send_sem=mate_sems.at[0, k], recv_sem=mate_sems.at[1, k], device_id=me.mate,
            device_id_type=MESH)

    def half_of(m, which):
        shard = (None, cross_in, self_in, cross_in, up_in)[m]
        size = HALF_COLS[m]
        begin = (0, width, 0, 0, 0)[m] + which * (0, width, size, 3 * width, size)[m]
        return shard.at[:, pl.ds(pl.multiple_of(begin, size), size)]

    buffers = {1: (half_narrow.at[0], pair_narrow.at[0]), 2: (half_wide.at[0], pair_wide.at[0]),
               3: (half_narrow.at[1], pair_narrow.at[1]), 4: (half_wide.at[1], pair_wide.at[1])}
    halves = {
        m: pltpu.make_async_remote_copy(
            src_ref=half_of(m, 1 - core), dst_ref=buffers[m][0], send_sem=half_sems.at[0, m],
            recv_sem=half_sems.at[1, m], device_id=me.mate, device_id_type=MESH)
        for m in buffers
    }
    for copy in halves.values():
        copy.start()
    sources = (small_in,) + tuple(buffers[m][1] for m in buffers) + (down_in,)
    gather = Gather(me, sources, (small_out, ckv_out, self_out, cqo_out, up_out, down_out), send_sem, recv_sem, own_sem)
    for m, (came_ref, both_ref) in buffers.items():
        halves[m].wait()
        own = half_of(m, core)[...].astype(jnp.float32)
        came = came_ref[...].astype(jnp.float32)
        both_ref[...] = jnp.concatenate(
            [jnp.where(core == 0, own, came), jnp.where(core == 0, came, own)], 0).astype(jnp.bfloat16)
        gather.run_until((0, 1, 2, 2, 4.5)[m])

    def fetch(src, dst, k):
        copy = pltpu.make_async_copy(src, dst, load_sem.at[k])
        copy.start()
        copy.wait()

    gather.run_until(18.5)
    gather.need(0)
    fetch(small_out, small_vm, 0)
    row = lax.broadcasted_iota(jnp.int32, (128, width), 0)
    spot = lax.broadcasted_iota(jnp.int32, (128, width), 1) - row

    def place_small(d, total):
        chosen = jnp.where((spot == d * 24) & (row < 24), 1.0, 0.0).astype(jnp.bfloat16)
        return total + dot(small_vm[d], chosen, NN)

    vec_ref[...] = lax.fori_loop(0, 32, place_small, jnp.zeros(vec_ref.shape, jnp.float32))

    def vec(k):
        return vec_ref[k:k + 1]

    source = x_ref[...].astype(jnp.float32)
    normed_one_ref[...] = norm_rows(source, vec(0), vec(1)).astype(jnp.bfloat16)
    gather.need(1)
    fetch(ckv_out, ckv_vm, 0)
    clips = frames_ref.shape[0]
    tiles = 2 * width // 256

    def project(t):
        clip, tile = t // tiles, t % tiles
        result = dot(frames_ref[clip], ckv_vm[:, columns(tile, 256)], NN)
        is_value = (tile >= 3).astype(jnp.float32)
        shift = vec_ref[10:11, columns(tile % 3, 256)] * is_value
        kv_vm[clip, :, columns(tile, 256)] = (result + shift).astype(jnp.bfloat16)

    loop_with(gather, clips * tiles, 20, 0.65, project)
    kv_store = pltpu.make_async_copy(kv_vm, kv_out, load_sem.at[1])
    kv_store.start()
    gather.run_until(31)
    gather.need(2)
    fetch(self_out, self_vm, 0)

    normed = normed_one_ref[...]
    own_rows = slice(toks, 2 * toks)
    kv_row_ref[own_rows, :width] = dot(normed, self_vm[:, width:2 * width], NN).astype(jnp.bfloat16)
    kv_row_ref[own_rows, width:] = (dot(normed, self_vm[:, 2 * width:3 * width], NN) + vec(7)).astype(jnp.bfloat16)
    kv_copy = to_mate(kv_row_ref.at[own_rows], kv_row_ref.at[slice(0, toks)], 0)
    kv_copy.start()
    query = (dot(normed, self_vm[:, :width], NN) + vec(6)).astype(jnp.bfloat16)
    query_ref[...] = query * jnp.bfloat16(0.125)
    gather.run_until(35)
    kv_copy.wait()

    def self_pair(j):
        cols = columns(j)
        keys = kv_row_ref[:, cols]
        values_t = kv_row_ref[:, columns(j + 6)].T
        parts = []
        for h in range(2):
            scores = dot(keys, one_head(query_ref[:, cols], h), NT) + bias_ref[...]
            peak = jnp.max(scores, 0, keepdims=True)
            terms = jnp.exp(scores - peak)
            total = jnp.sum(terms, 0, keepdims=True)
            parts.append(dot(values_t[h * 64:(h + 1) * 64], terms.astype(jnp.bfloat16), NN) / total)
            self_lse_ref[j, h:h + 1] = peak + jnp.log(total)
        attended_ref[:, cols] = jnp.concatenate(parts, 0).T

    loop_with(gather, 6, 35, 1.2, self_pair)
    after_self = source + dot(attended_ref[...].astype(jnp.bfloat16), self_vm[:, 3 * width:], NN) + vec(8)
    after_self_ref[...] = after_self
    normed_two = norm_rows(after_self, vec(2), vec(3)).astype(jnp.bfloat16)
    normed_two_ref[...] = normed_two
    gather.run_until(44)
    gather.need(3)
    fetch(cqo_out, cqo_vm, 0)
    my_rows = pl.ds(pl.multiple_of(core * toks, toks), toks)
    cross_query = (dot(normed_two, cqo_vm[:, :width], NN) + vec(9)).astype(jnp.bfloat16)
    row_query_ref[my_rows] = cross_query * jnp.bfloat16(0.125)
    query_copy = to_mate(row_query_ref.at[my_rows], row_query_ref.at[my_rows], 1)
    query_copy.start()
    gather.run_until(48)
    query_copy.wait()

    def attend(clip, values_t, query, j, h):
        scores = dot(kv_vm[clip, :, columns(j)], query, NT)
        peak = jnp.max(scores, 0, keepdims=True)
        terms = jnp.exp(scores - peak)
        total = jnp.sum(terms, 0, keepdims=True)
        result = dot(values_t[h * 64:(h + 1) * 64], terms.astype(jnp.bfloat16), NN)
        return result / total, peak, total

    def cross_pair(j):
        values_t = kv_vm[0, :, columns(j + 6)].T
        mine = seg_ref[...] == 0
        for h in range(2):
            result, peak, total = attend(0, values_t, one_head(row_query_ref[:, columns(j)], h), j, h)
            acc_ref[h * 64:(h + 1) * 64] = jnp.where(mine, result, 0.0)
            stat_ref[h:h + 1] = jnp.where(mine, peak, 0.0)
            stat_ref[2 + h:3 + h] = jnp.where(mine, total, 1.0)
        for clip in (1, 2):
            values_t = kv_vm[clip, :, columns(j + 6)].T
            query_rows = jnp.where(
                group_ref[clip - 1:clip] == 0, row_query_ref[:128, columns(j)], row_query_ref[384:, columns(j)])
            for h in range(2):
                result, peak, total = attend(clip, values_t, one_head(query_rows, h), j, h)
                for spot in (0, 3):
                    cols = slice(spot * 128, (spot + 1) * 128)
                    mine = seg_ref[:, cols] == clip
                    rows = slice(h * 64, (h + 1) * 64)
                    acc_ref[rows, cols] = jnp.where(mine, result, acc_ref[rows, cols])
                    stat_ref[h:h + 1, cols] = jnp.where(mine, peak, stat_ref[h:h + 1, cols])
                    stat_ref[2 + h:3 + h, cols] = jnp.where(mine, total, stat_ref[2 + h:3 + h, cols])
        my_cols, mate_cols = columns(core, toks), columns(1 - core, toks)
        part_ref[j] = acc_ref[:, my_cols]
        part_stat_ref[j] = stat_ref[:, my_cols]
        give_ref[j] = acc_ref[:, mate_cols].astype(jnp.bfloat16)
        give_stat_ref[j] = stat_ref[:, mate_cols]

    loop_with(gather, 6, 48, 3.8, cross_pair)
    give_copy = to_mate(give_ref, take_ref, 2)
    give_copy.start()
    give_stat_copy = to_mate(give_stat_ref, take_stat_ref, 3)
    give_stat_copy.start()
    gather.run_until(1000)
    give_copy.wait()
    give_stat_copy.wait()

    def combine(j, carry):
        parts = []
        for h in range(2):
            rows = slice(h * 64, (h + 1) * 64)
            peak_a, peak_b = part_stat_ref[j, h:h + 1], take_stat_ref[j, h:h + 1]
            peak = jnp.maximum(peak_a, peak_b)
            share_a = part_stat_ref[j, 2 + h:3 + h] * jnp.exp(peak_a - peak)
            share_b = take_stat_ref[j, 2 + h:3 + h] * jnp.exp(peak_b - peak)
            total = share_a + share_b
            cross_lse_ref[j, h:h + 1] = peak + jnp.log(total)
            parts.append(part_ref[j, rows] * (share_a / total)
                         + take_ref[j, rows].astype(jnp.float32) * (share_b / total))
        mixed_ref[:, columns(j)] = jnp.concatenate(parts, 0).T
        return carry

    lax.fori_loop(0, 6, combine, 0)
    after_cross = after_self_ref[...] + dot(mixed_ref[...].astype(jnp.bfloat16), cqo_vm[:, width:], NN) + vec(11)
    after_cross_ref[...] = after_cross
    normed_three_ref[...] = norm_rows(after_cross, vec(4), vec(5)).astype(jnp.bfloat16)
    gather.need(4)
    gather.need(5)
    kv_store.wait()
    gather.finish()


def fused_forward(group, x, frames, bias, seg, small, self_w, cross_w, up_w, down_w):
    toks, width = x.shape
    clips, count = frames.shape[:2]
    low, full = jnp.bfloat16, jnp.float32
    pairs = width // 128
    vmem, hbm = pl.BlockSpec(memory_space=pltpu.VMEM), pl.BlockSpec(memory_space=pl.ANY)
    shape = jax.ShapeDtypeStruct
    outs = [
        (hbm, shape((32, 16, 128), low)), (hbm, shape((width, 2 * width), low)), (hbm, shape((width, 4 * width), low)),
        (hbm, shape((width, 2 * width), low)), (hbm, shape((width, 4 * width), low)),
        (hbm, shape((4 * width, width), low)),
        (hbm, shape((clips, count, 2 * width), low)),
        (vmem, shape((16, width), full)), (vmem, shape((toks, width), low)), (vmem, shape((toks, width), low)),
        (vmem, shape((2 * toks, 2 * width), low)), (vmem, shape((toks, width), full)),
        (vmem, shape((pairs, 2, toks), full)), (vmem, shape((toks, width), full)), (vmem, shape((toks, width), low)),
        (vmem, shape((2 * toks, width), low)), (vmem, shape((pairs, 2, toks), full)), (vmem, shape((toks, width), full)),
        (vmem, shape((toks, width), full)), (vmem, shape((toks, width), low)),
    ]
    return pl.pallas_call(
        forward_kernel,
        in_specs=[vmem] * 5 + [hbm] + [vmem] * 3 + [hbm],
        out_specs=tuple(spec for spec, _ in outs),
        out_shape=tuple(s for _, s in outs),
        scratch_shapes=[
            pltpu.VMEM((2, 24, 2 * width), low), pltpu.VMEM((2, 24, width), low), pltpu.VMEM((2, 48, 2 * width), low),
            pltpu.VMEM((2, 48, width), low), pltpu.VMEM((32, 16, 128), low),
            pltpu.VMEM((width, 2 * width), low), pltpu.VMEM((width, 4 * width), low), pltpu.VMEM((width, 2 * width), low),
            pltpu.VMEM((clips, count, 2 * width), low), pltpu.VMEM((128, 2 * toks), full), pltpu.VMEM((4, 2 * toks), full),
            pltpu.VMEM((pairs, 128, toks), full), pltpu.VMEM((pairs, 4, toks), full),
            pltpu.VMEM((pairs, 128, toks), low), pltpu.VMEM((pairs, 4, toks), full),
            pltpu.VMEM((pairs, 128, toks), low), pltpu.VMEM((pairs, 4, toks), full),
            pltpu.SemaphoreType.DMA((400,)), pltpu.SemaphoreType.DMA((6, 32)), pltpu.SemaphoreType.DMA((6,)),
            pltpu.SemaphoreType.DMA((2, 5)), pltpu.SemaphoreType.DMA((2, 4)), pltpu.SemaphoreType.DMA((2,)),
        ],
        compiler_params=pltpu.CompilerParams(collective_id=0, has_side_effects=True, vmem_limit_bytes=60 * 2**20),
        name="fused_forward",
    )(group, x, frames, bias, seg, small, self_w, cross_w, up_w, down_w)


class Scatter:
    def __init__(self, me, grads, outs, buffers, sems, times):
        self.me, self.grads, self.outs = me, grads, outs
        self.buffers = buffers
        self.send_sem, self.own_sem, self.pair_sem, self.plane_sem, self.line_sem = sems
        self.sends = []
        half = me.z // 2
        near = me.z + half * (3 - 2 * me.z)
        self.order = [base + half * (3 - 2 * base) for base in (3, 2, 1 - near, near)]
        self.tasks = []
        for m, (begin, ats) in enumerate(times):
            for at, acts in zip(ats, self.steps(m)):
                self.tasks.append((begin + at, m, acts))
        self.tasks.sort(key=lambda entry: entry[:2])

    def sender(self, src, dst, sem, target):
        copy = pltpu.make_async_remote_copy(
            src_ref=src, dst_ref=dst, send_sem=self.send_sem.at[len(self.sends)], recv_sem=sem, device_id=target,
            device_id_type=MESH)
        self.sends.append(copy)
        return copy.start

    def arrival(self, dst, sem):
        return pltpu.make_async_remote_copy(
            src_ref=dst, dst_ref=dst, send_sem=self.send_sem.at[0], recv_sem=sem, device_id=self.me.mate,
            device_id_type=MESH).wait_recv

    def steps(self, m):
        me, order = self.me, self.order
        grad, out = self.grads[m], self.outs[m]
        own, pair, plane_a, plane_b, plane_c, line = self.buffers[m]

        def own_at(z, p):
            return grad.at[z, p, me.core] if own is None else own.at[z, p]

        own_sem, pair_sem, plane_sem, line_sem = self.own_sem, self.pair_sem, self.plane_sem, self.line_sem

        def adder(dst, *others):
            def act():
                total = dst[...].astype(jnp.float32)
                for other in others:
                    total = total + other[...].astype(jnp.float32)
                dst[...] = total.astype(dst.dtype)
            return act

        loads = {}
        begin = []
        for k, p in enumerate((me.p_diag, me.p_second, me.p_first, me.p)):
            if own is not None:
                loads[k] = pltpu.make_async_copy(grad.at[:, p, me.core], own.at[:, p], own_sem.at[m, p])
                begin.append(loads[k].start)
        for p in (me.p_diag, me.p_first, me.p_second, me.p):
            begin.append(self.sender(grad.at[:, p, 1 - me.core], pair.at[:, p], pair_sem.at[m, p], me.mate))

        def paired(k, p):
            return ([loads[k].wait] if loads else []) + [self.arrival(pair.at[:, p], pair_sem.at[m, p])]

        diag = paired(0, me.p_diag)
        second = paired(1, me.p_second)
        first = paired(2, me.p_first)
        for z in order:
            diag += [adder(own_at(z, me.p_diag), pair.at[z, me.p_diag]),
                     self.sender(own_at(z, me.p_diag), plane_a.at[z], plane_sem.at[m, 0, z], me.second)]
            second += [adder(own_at(z, me.p_second), pair.at[z, me.p_second]),
                       self.sender(own_at(z, me.p_second), plane_c.at[z], plane_sem.at[m, 2, z], me.second)]
            first += [self.arrival(plane_a.at[z], plane_sem.at[m, 0, z]),
                      adder(own_at(z, me.p_first), pair.at[z, me.p_first], plane_a.at[z]),
                      self.sender(own_at(z, me.p_first), plane_b.at[z], plane_sem.at[m, 1, z], me.first)]
        steps = [begin, diag, second, first]
        for k, z in enumerate(order):
            acts = paired(3, me.p) if k == 0 else []
            acts += [self.arrival(plane_b.at[z], plane_sem.at[m, 1, z]),
                     self.arrival(plane_c.at[z], plane_sem.at[m, 2, z])]
            if k < 3:
                acts.append(adder(own_at(z, me.p), pair.at[z, me.p], plane_b.at[z], plane_c.at[z]))
                upward = (z - me.z + 3) // 4
                source = me.z + 1 - 2 * upward
                came = jnp.logical_and(source >= 0, source < Z)
                slot = line.at[upward, z]
                arrival, add = self.arrival(slot, line_sem.at[m, upward, z]), adder(own_at(z, me.p), slot)

                def join(came=came, arrival=arrival, add=add):
                    def go():
                        arrival()
                        add()
                    pl.when(came)(go)

                target = (lax.rem(me.dp + 12 + 8 * upward, 16), me.core)
                acts += [join, self.sender(own_at(z, me.p), slot, line_sem.at[m, upward, z], target)]
            else:
                def total():
                    part = own_at(me.z, me.p)[...].astype(jnp.float32) + pair[me.z, me.p].astype(jnp.float32)
                    out[...] = part + plane_b[me.z].astype(jnp.float32) + plane_c[me.z].astype(jnp.float32)

                acts.append(total)
                for upward, cond in ((0, me.has_up), (1, me.has_down)):
                    arrival = self.arrival(line.at[upward, me.z], line_sem.at[m, upward, me.z])

                    def last(upward=upward, cond=cond, arrival=arrival):
                        def go():
                            arrival()
                            out[...] += line[upward, me.z].astype(jnp.float32)
                        pl.when(cond)(go)

                    acts.append(last)
            steps.append(acts)
        return steps

    def run(self, entry):
        for act in entry[2]:
            act()

    def run_until(self, time):
        while self.tasks and self.tasks[0][0] <= time:
            self.run(self.tasks.pop(0))

    def take_until(self, time):
        taken = []
        while self.tasks and self.tasks[0][0] <= time:
            taken.append(self.tasks.pop(0))
        return taken

    def finish(self):
        self.run_until(10**6)
        for copy in self.sends:
            copy.wait_send()


def scatter_scratch(grads):
    shapes = []
    for g in grads:
        for lead in ((4, 4), (4, 4), (4,), (4,), (4,), (2, 4)):
            shapes.append(pltpu.VMEM(lead + g.shape[1:], g.dtype))
    count = len(grads)
    return shapes + [
        pltpu.SemaphoreType.DMA((20 * count,)),
        pltpu.SemaphoreType.DMA((count, 4)),
        pltpu.SemaphoreType.DMA((count, 4)),
        pltpu.SemaphoreType.DMA((count, 3, 4)),
        pltpu.SemaphoreType.DMA((count, 2, 4)),
    ]


def scatter_view(grad):
    return grad.reshape((4, 4, 2) + grad.shape[1:])


BACK_TIMES = ((0, (0, 4, 6, 12, 22, 27, 32, 38)), (1, (0, 14, 16, 22, 34, 39, 44, 50)))


def norm_rows_back(values, gain, grad):
    average = jnp.mean(values, -1, keepdims=True)
    centred = values - average
    scale = lax.rsqrt(jnp.mean(centred * centred, -1, keepdims=True) + 1e-05)
    normed = centred * scale
    inner = grad * gain
    mean_inner = jnp.mean(inner, -1, keepdims=True)
    mean_both = jnp.mean(inner * normed, -1, keepdims=True)
    result = scale * (inner - mean_inner - normed * mean_both)
    return result, jnp.sum(grad * normed, 0, keepdims=True), jnp.sum(grad, 0, keepdims=True)


def backward_kernel(*refs):
    (group_ref, x_ref, bias_ref, seg_ref, vec_ref, gac_ref, mixed_ref, cross_lse_ref, row_query_ref, after_self_ref,
     attended_ref, self_lse_ref, query_ref, kv_row_ref, cqo_hbm, self_hbm, kv_hbm, up_hbm, down_hbm) = refs[:19]
    (input_grad_ref, cq_ref, self_low_ref, qkv_ref, vec_grad_ref, dkv_hbm, up_out, down_out) = refs[19:27]
    scratch = refs[27:]
    scatter_refs, scratch = scratch[:17], scratch[17:]
    (cross_vm, self_vm, kv_vm, row_grad_ref, row_stat_ref, acc_ref, own_ref, give_ref, take_ref,
     take_query_ref, load_sem, mate_sems) = scratch
    me = Place()
    core = me.core
    toks, width = x_ref.shape
    loads = [
        pltpu.make_async_copy(cqo_hbm.at[:, pl.ds(0, width)], cross_vm.at[0], load_sem.at[0]),
        pltpu.make_async_copy(cqo_hbm.at[:, pl.ds(width, width)], cross_vm.at[1], load_sem.at[1]),
        pltpu.make_async_copy(kv_hbm, kv_vm, load_sem.at[2]),
        pltpu.make_async_copy(self_hbm, self_vm, load_sem.at[3]),
    ]
    for copy in (loads[1], loads[0], loads[2], loads[3]):
        copy.start()
    me.greet()
    scatter = Scatter(me, (up_hbm, down_hbm), (up_out, down_out), (scatter_refs[:6], scatter_refs[6:12]),
                      scatter_refs[12:], BACK_TIMES)
    scatter.run_until(1)

    def to_mate(src, dst, k):
        return pltpu.make_async_remote_copy(
            src_ref=src, dst_ref=dst, send_sem=mate_sems.at[0, k], recv_sem=mate_sems.at[1, k], device_id=me.mate,
            device_id_type=MESH)

    my_rows = pl.ds(pl.multiple_of(core * toks, toks), toks)
    my_cols = columns(core, toks)

    def head_rows(product, store):
        turned = product.T
        for h in range(2):
            store(h, jnp.sum(turned[h * 64:(h + 1) * 64], 0, keepdims=True))

    loads[1].wait()
    grad_mixed = dot(gac_ref[...].astype(jnp.bfloat16), cross_vm[1], NT).astype(jnp.bfloat16)
    row_grad_ref[my_rows] = grad_mixed
    grad_copy = to_mate(row_grad_ref.at[my_rows], row_grad_ref.at[my_rows], 0)
    grad_copy.start()
    for j in range(6):
        cols = slice(j * 128, (j + 1) * 128)
        product = grad_mixed[:, cols].astype(jnp.float32) * mixed_ref[:, cols]
        row_stat_ref[j, 0:2, my_cols] = cross_lse_ref[j]

        def keep(h, row, j=j):
            row_stat_ref[j, 2 + h:3 + h, my_cols] = row

        head_rows(product, keep)
    stat_copy = to_mate(row_stat_ref.at[:, :, my_cols], row_stat_ref.at[:, :, my_cols], 1)
    stat_copy.start()
    loads[2].wait()
    scatter.run_until(5)
    grad_copy.wait()
    stat_copy.wait()

    def cross_pair(j):
        def back(clip, keys_t, query, grad, lse, inner, h):
            weights = jnp.exp(dot(kv_vm[clip, :, columns(j)], query, NT) - lse)
            grad_v = dot(weights.astype(jnp.bfloat16), grad, NN)
            grad_s = (weights * (dot(kv_vm[clip, :, columns(j + 6)], grad, NT) - inner)).astype(jnp.bfloat16)
            return dot(keys_t[h * 64:(h + 1) * 64], grad_s, NN), dot(grad_s, query, NN), grad_v

        for clip in range(3):
            keys_t = kv_vm[clip, :, columns(j)].T
            grads = []
            for h in range(2):
                if clip == 0:
                    query, grad = row_query_ref[:, columns(j)], row_grad_ref[:, columns(j)]
                    mine = seg_ref[...] == 0
                    lse, inner = row_stat_ref[j, h:h + 1], row_stat_ref[j, 2 + h:3 + h]
                else:
                    low = group_ref[clip - 1:clip] == 0

                    def chosen(ref):
                        return jnp.where(low, ref[:128, columns(j)], ref[384:, columns(j)])

                    def chosen_row(row):
                        return jnp.where(low, row_stat_ref[j, row:row + 1, :128], row_stat_ref[j, row:row + 1, 384:])

                    query, grad = chosen(row_query_ref), chosen(row_grad_ref)
                    mine = jnp.where(low, seg_ref[:, :128], seg_ref[:, 384:]) == clip
                    lse, inner = chosen_row(h), chosen_row(2 + h)
                grads.append(back(clip, keys_t, one_head(query, h), one_head(grad, h), jnp.where(mine, lse, 1e30),
                                  inner, h))
            grad_q, grad_k, grad_v = zip(*grads)
            grad_q = jnp.concatenate(grad_q, 0)
            if clip == 0:
                acc_ref[...] = grad_q
            else:
                for spot in (0, 3):
                    cols = slice(spot * 128, (spot + 1) * 128)
                    acc_ref[:, cols] += jnp.where(low == (spot == 0), grad_q, 0.0)
            kv_vm[clip, :, columns(j)] = (grad_k[0] + grad_k[1]).astype(jnp.bfloat16)
            kv_vm[clip, :, columns(j + 6)] = (grad_v[0] + grad_v[1]).astype(jnp.bfloat16)
        own_ref[:, columns(j)] = (acc_ref[:, my_cols] * 0.125).T
        give_ref[:, columns(j)] = (acc_ref[:, columns(1 - core, toks)] * 0.125).T.astype(jnp.bfloat16)

    loop_with(scatter, 6, 6, 4.7, cross_pair)
    query_copy = to_mate(give_ref.at[:, pl.ds(0, width)], take_query_ref, 2)
    query_copy.start()
    dkv_store = pltpu.make_async_copy(kv_vm, dkv_hbm, load_sem.at[2])
    dkv_store.start()
    vec_grad_ref[...] = jnp.zeros_like(vec_grad_ref)
    cv_bias = sum(jnp.sum(kv_vm[clip, :, width:].astype(jnp.float32), 0, keepdims=True) for clip in range(3))
    vec_grad_ref[10:11] = cv_bias
    loads[0].wait()
    loads[3].wait()
    scatter.run_until(35)
    query_copy.wait()
    grad_query = (own_ref[:, :width] + take_query_ref[...].astype(jnp.float32)).astype(jnp.bfloat16)
    cq_ref[...] = grad_query
    vec_grad_ref[9:10] = jnp.sum(grad_query.astype(jnp.float32), 0, keepdims=True)
    grad_part, gain, shift = norm_rows_back(after_self_ref[...], vec_ref[2:3], dot(grad_query, cross_vm[0], NT))
    vec_grad_ref[2:3] = gain
    vec_grad_ref[3:4] = shift
    grad_after_self = gac_ref[...] + grad_part
    input_grad_ref[...] = grad_after_self
    grad_low = grad_after_self.astype(jnp.bfloat16)
    self_low_ref[...] = grad_low
    vec_grad_ref[8:9] = jnp.sum(grad_low.astype(jnp.float32), 0, keepdims=True)
    grad_attended = dot(grad_low, self_vm[:, 3 * width:], NT).astype(jnp.bfloat16)
    row_grad_ref[:toks] = grad_attended
    for j in range(6):
        cols = slice(j * 128, (j + 1) * 128)

        def keep_self(h, row, j=j):
            row_stat_ref[j, h:h + 1, :toks] = row

        head_rows(grad_attended[:, cols].astype(jnp.float32) * attended_ref[:, cols], keep_self)

    def self_pair(j):
        cols, value_cols = columns(j), columns(j + 6)
        keys, values = kv_row_ref[:, cols], kv_row_ref[:, value_cols]
        keys_t = keys.T
        grad_k = grad_v = None
        parts = []
        for h in range(2):
            query, grad = one_head(query_ref[:, cols], h), one_head(row_grad_ref[:toks, cols], h)
            weights = jnp.exp(dot(keys, query, NT) + bias_ref[...] - self_lse_ref[j, h:h + 1])
            part = dot(weights.astype(jnp.bfloat16), grad, NN)
            grad_v = part if grad_v is None else grad_v + part
            inner = row_stat_ref[j, h:h + 1, :toks]
            grad_s = (weights * (dot(values, grad, NT) - inner)).astype(jnp.bfloat16)
            part = dot(grad_s, query, NN)
            grad_k = part if grad_k is None else grad_k + part
            parts.append(dot(keys_t[h * 64:(h + 1) * 64], grad_s, NN))
        qkv_ref[:, cols] = (jnp.concatenate(parts, 0) * 0.125).T.astype(jnp.bfloat16)
        own_ref[:, cols] = grad_k[toks:]
        own_ref[:, value_cols] = grad_v[toks:]
        give_ref[:, cols] = grad_k[:toks].astype(jnp.bfloat16)
        give_ref[:, value_cols] = grad_v[:toks].astype(jnp.bfloat16)

    loop_with(scatter, 6, 42, 1.3, self_pair)
    row_copy = to_mate(give_ref, take_ref, 3)
    row_copy.start()
    scatter.run_until(51)
    row_copy.wait()
    qkv_ref[:, width:] = (own_ref[...] + take_ref[...].astype(jnp.float32)).astype(jnp.bfloat16)
    sums = jnp.sum(qkv_ref[...].astype(jnp.float32), 0, keepdims=True)
    vec_grad_ref[6:7] = sums[:, :width]
    vec_grad_ref[7:8] = sums[:, 2 * width:]
    grad_normed = dot(qkv_ref[...], self_vm[:, :3 * width], NT)
    grad_part, gain, shift = norm_rows_back(x_ref[...].astype(jnp.float32), vec_ref[0:1], grad_normed)
    vec_grad_ref[0:1] = gain
    vec_grad_ref[1:2] = shift
    input_grad_ref[...] += grad_part
    scatter.finish()
    dkv_store.wait()


def fused_backward(group, x, bias, seg, vec, gac, mixed, cross_lse, row_query, after_self, attended, self_lse, query,
                   kv_row, cqo_full, self_full, kv, grad_up, grad_down):
    toks, width = x.shape
    low, full = jnp.bfloat16, jnp.float32
    pairs = width // 128
    vmem, hbm = pl.BlockSpec(memory_space=pltpu.VMEM), pl.BlockSpec(memory_space=pl.ANY)
    shape = jax.ShapeDtypeStruct
    outs = [
        (vmem, shape((toks, width), full)), (vmem, shape((toks, width), low)), (vmem, shape((toks, width), low)),
        (vmem, shape((toks, 3 * width), low)), (vmem, shape((16, width), full)), (hbm, shape(kv.shape, low)),
        (vmem, shape(grad_up.shape[1:], full)), (vmem, shape(grad_down.shape[1:], full)),
    ]
    return pl.pallas_call(
        backward_kernel,
        in_specs=[vmem] * 14 + [hbm] * 5,
        out_specs=tuple(spec for spec, _ in outs),
        out_shape=tuple(s for _, s in outs),
        scratch_shapes=scatter_scratch((grad_up, grad_down)) + [
            pltpu.VMEM((2, width, width), low), pltpu.VMEM((width, 4 * width), low), pltpu.VMEM(kv.shape, low),
            pltpu.VMEM((2 * toks, width), low), pltpu.VMEM((pairs, 4, 2 * toks), full),
            pltpu.VMEM((128, 2 * toks), full), pltpu.VMEM((toks, 2 * width), full), pltpu.VMEM((toks, 2 * width), low),
            pltpu.VMEM((toks, 2 * width), low), pltpu.VMEM((toks, width), low), pltpu.SemaphoreType.DMA((4,)), pltpu.SemaphoreType.DMA((2, 4)),
        ],
        compiler_params=pltpu.CompilerParams(collective_id=2, has_side_effects=True, vmem_limit_bytes=63 * 2**20),
        name="fused_backward",
    )(group, x, bias, seg, vec, gac, mixed, cross_lse, row_query, after_self, attended, self_lse, query, kv_row,
      cqo_full, self_full, kv, scatter_view(grad_up), scatter_view(grad_down))


def ffn_kernel(normed_ref, grad_ref, after_ref, vec_ref, up_ref, bias_ref, down_ref, out_ref, back_ref, grad_up_ref,
               grad_down_ref, grad_bias_ref, rows_ref, turned_ref, sum_ref, back_sum_ref):
    t = pl.program_id(0)

    @pl.when(t == 0)
    def _():
        turned_ref[...] = normed_ref[...].T
        sum_ref[...] = jnp.zeros_like(sum_ref)
        back_sum_ref[...] = jnp.zeros_like(back_sum_ref)

    grad = grad_ref[...]
    pre = dot(normed_ref[...], up_ref[...], NN) + bias_ref[...]
    below = 0.5 * (1.0 + lax.erf(pre * 0.7071067811865476))
    activated = (pre * below).astype(jnp.bfloat16)
    sum_ref[...] += dot(activated, down_ref[...], NN)
    grad_act = dot(grad, down_ref[...], NT).astype(jnp.bfloat16).astype(jnp.float32)
    density = jnp.exp(-0.5 * pre * pre) * 0.3989422804014327
    grad_pre = (grad_act * (below + pre * density)).astype(jnp.bfloat16)
    back_sum_ref[...] += dot(grad_pre, up_ref[...], NT)
    grad_up_ref[...] = dot(turned_ref[...], grad_pre, NN).astype(jnp.bfloat16)
    grad_down_ref[...] = dot(activated.T, grad, NN).astype(jnp.bfloat16)
    grad_bias_ref[...] = jnp.sum(grad_pre.astype(jnp.float32), 0, keepdims=True)

    @pl.when(t == pl.num_programs(0) - 1)
    def _():
        out_ref[...] = (after_ref[...] + sum_ref[...] + vec_ref[12:13]).astype(jnp.bfloat16)
        grad_rows = grad_ref[...].astype(jnp.float32)
        part, gain, shift = norm_rows_back(after_ref[...], vec_ref[4:5], back_sum_ref[...])
        back = grad_rows + part
        back_ref[...] = back
        rows_ref[...] = jnp.zeros_like(rows_ref)
        rows_ref[4:5] = gain
        rows_ref[5:6] = shift
        rows_ref[11:12] = jnp.sum(back.astype(jnp.bfloat16).astype(jnp.float32), 0, keepdims=True)
        rows_ref[12:13] = jnp.sum(grad_rows, 0, keepdims=True)


def ffn(normed, grad, after, vec, up_full, bias, down_full):
    toks, width = normed.shape
    hidden = up_full.shape[1]
    size = 256
    low, full = jnp.bfloat16, jnp.float32
    shape = jax.ShapeDtypeStruct
    rows = pl.BlockSpec((toks, width), lambda t: (0, 0))
    vecs = pl.BlockSpec((16, width), lambda t: (0, 0))
    up_spec = pl.BlockSpec((width, size), lambda t: (0, t))
    down_spec = pl.BlockSpec((size, width), lambda t: (t, 0))
    bias_spec = pl.BlockSpec((1, size), lambda t: (0, t))
    return pl.pallas_call(
        ffn_kernel,
        grid=(hidden // size,),
        in_specs=[rows, rows, rows, vecs, up_spec, bias_spec, down_spec],
        out_specs=[rows, rows, up_spec, down_spec, bias_spec, vecs],
        out_shape=[
            shape((toks, width), low), shape((toks, width), full), shape(up_full.shape, low),
            shape(down_full.shape, low), shape((1, hidden), full), shape((16, width), full),
        ],
        scratch_shapes=[pltpu.VMEM((width, toks), low), pltpu.VMEM((toks, width), full), pltpu.VMEM((toks, width), full)],
        compiler_params=pltpu.CompilerParams(vmem_limit_bytes=48 * 2**20),
        name="ffn",
    )(normed, grad, after, vec, up_full, bias, down_full)


def place_clips_kernel(order, in_ref, out_ref):
    frames, width = in_ref.shape[1:]
    blocks = width // 128
    for k in range(blocks):
        out_ref[pl.ds(k, frames, stride=blocks), 0] = in_ref[0, :, k * 128:(k + 1) * 128]


def place_clips(order, values):
    clips, frames, width = values.shape
    rows = frames * width // 128
    flat = pl.pallas_call(
        place_clips_kernel,
        grid_spec=pltpu.PrefetchScalarGridSpec(
            num_scalar_prefetch=1,
            grid=(clips,),
            in_specs=[pl.BlockSpec((1, frames, width), lambda k, order: (k, 0, 0))],
            out_specs=pl.BlockSpec((rows, 1, 128), lambda k, order: (order[k], 0, 0)),
        ),
        out_shape=jax.ShapeDtypeStruct((clips * rows, 1, 128), values.dtype),
        compiler_params=pltpu.CompilerParams(vmem_limit_bytes=48 * 2**20),
        name="place_clips",
    )(order, values)
    return flat.reshape(1, clips, frames, width)


FINISH_TIMES = ((3, (0, 4, 6, 12, 22, 27, 32, 38)), (12, (0, 6, 8, 14, 26, 31, 36, 42)), (13, (0, 6, 8, 14, 26, 31, 36, 42)))


def finish_kernel(*refs):
    (normed_one_ref, qkv_ref, attended_ref, self_low_ref, normed_two_ref, cq_ref, mixed_ref, cross_low_ref, frames_ref,
     dkv_ref, ckv_hbm, small_hbm) = refs[:12]
    encoder_hbm, self_out, cross_out, small_out = refs[12:16]
    scratch = refs[16:]
    scatter_refs, scratch = scratch[:18], scratch[18:]
    sems, (turned_ref, weight_ref, stage_ref, load_sem, store_sem) = scratch[:5], scratch[5:]
    self_grad, cross_grad = scatter_refs[0], scatter_refs[6]
    width = normed_one_ref.shape[1]
    load = pltpu.make_async_copy(ckv_hbm, weight_ref, load_sem.at[0])
    load.start()
    me = Place()
    me.greet()
    scatter = Scatter(
        me, (self_grad, cross_grad, small_hbm), (self_out, cross_out, small_out),
        ((None,) + tuple(scatter_refs[1:6]), (None,) + tuple(scatter_refs[7:12]), tuple(scatter_refs[12:18])), sems,
        FINISH_TIMES)

    def store(grad, cols, value):
        grad[..., cols] = value.reshape(4, 4, 2, 24, value.shape[1]).astype(jnp.bfloat16)

    def weight_grad(grad, left_ref, right_ref, first_tile):
        left = left_ref[...].T

        def tile(t, carry):
            store(grad, columns(first_tile + t, 256), dot(left, right_ref[:, columns(t, 256)], NN))
            return carry

        lax.fori_loop(0, right_ref.shape[1] // 256, tile, 0)

    weight_grad(self_grad, normed_one_ref, qkv_ref, 0)
    weight_grad(self_grad, attended_ref, self_low_ref, 9)
    scatter.run_until(3)
    weight_grad(cross_grad, normed_two_ref, cq_ref, 0)
    weight_grad(cross_grad, mixed_ref, cross_low_ref, 9)
    clips = frames_ref.shape[0]
    for clip in range(clips):
        turned_ref[clip] = frames_ref[clip].T
    scatter.run_until(5)

    def frames_tile(t):
        cols = columns(t, 256)
        total = dot(turned_ref[0], dkv_ref[0, :, cols], NN)
        for clip in range(1, clips):
            total = total + dot(turned_ref[clip], dkv_ref[clip, :, cols], NN)
        store(cross_grad, columns(t + 3, 256), total)

    loop_with(scatter, 6, 6, 1, frames_tile)
    scatter.run_until(13)
    load.wait()
    stores = []
    for clip in range(clips):
        slot = clip % 2
        if clip >= 2:
            stores[clip - 2].wait()

        def encoder_tile(t, clip=clip, slot=slot):
            rows = columns(t, 256)
            stage_ref[slot, :, rows] = dot(dkv_ref[clip], weight_ref[rows], NT)

        loop_with(scatter, width // 256, 14 + 4 * clip, 1.3, encoder_tile)
        stores.append(pltpu.make_async_copy(stage_ref.at[slot], encoder_hbm.at[clip], store_sem.at[slot]))
        stores[clip].start()
    scatter.finish()
    for clip in range(max(0, clips - 2), clips):
        stores[clip].wait()


def fused_finish(normed_one, qkv, attended, self_low, normed_two, cq, mixed, cross_low, frames, dkv, ckv_full, small):
    width = normed_one.shape[1]
    clips, count = frames.shape[:2]
    low, full = jnp.bfloat16, jnp.float32
    vmem, hbm = pl.BlockSpec(memory_space=pltpu.VMEM), pl.BlockSpec(memory_space=pl.ANY)
    shape = jax.ShapeDtypeStruct
    large = shape((32, width // 32, 4 * width), low)
    scratch = scatter_scratch((large, large, small))
    for m in range(2):
        scratch[6 * m] = pltpu.VMEM((4, 4, 2) + large.shape[1:], low)
    outs = [
        (hbm, shape(frames.shape, full)), (vmem, shape(large.shape[1:], full)), (vmem, shape(large.shape[1:], full)),
        (vmem, shape(small.shape[1:], full)),
    ]
    return pl.pallas_call(
        finish_kernel,
        in_specs=[vmem] * 10 + [hbm] * 2,
        out_specs=tuple(spec for spec, _ in outs),
        out_shape=tuple(s for _, s in outs),
        scratch_shapes=scratch + [
            pltpu.VMEM((clips, width, count), low), pltpu.VMEM((width, 2 * width), low),
            pltpu.VMEM((2, count, width), full), pltpu.SemaphoreType.DMA((1,)), pltpu.SemaphoreType.DMA((2,)),
        ],
        compiler_params=pltpu.CompilerParams(collective_id=1, has_side_effects=True, vmem_limit_bytes=63 * 2**20),
        name="fused_finish",
    )(normed_one, qkv, attended, self_low, normed_two, cq, mixed, cross_low, frames, dkv, ckv_full,
      scatter_view(small))


def from_behind(value, axis, steps):
    count = lax.axis_size(axis)
    leading, last = (max(0, -steps), min(count, count - steps))
    return lax.ppermute(value, axis, [(source, source + steps) for source in range(leading, last)])


def layer_norm(values, gain, shift):
    average = jnp.mean(values, -1, keepdims=True)
    centred = values - average
    spread = jnp.mean(centred * centred, -1, keepdims=True)
    return centred * lax.rsqrt(spread + 1e-05) * gain + shift


def matmul(left, right):
    return jnp.dot(left, right, preferred_element_type=jnp.float32)


def swap_halves(value):
    return lax.ppermute(value, "seq", [(0, 1), (1, 0)])


def seq_halves(value, axis):
    span = value.shape[axis] // 2
    half = lax.axis_index("seq")
    mine = lax.dynamic_slice_in_dim(value, half * span, span, axis)
    other = lax.dynamic_slice_in_dim(value, (1 - half) * span, span, axis)
    return mine, other


def seq_scatter(value):
    mine, other = seq_halves(value, 0)
    return mine + swap_halves(other.astype(jnp.bfloat16)).astype(value.dtype)


def per_head(values):
    rows = values.reshape(-1, values.shape[2]).T
    return jnp.repeat(rows, HEAD_DIM, axis=1)


def head_sums(values):
    sums = jnp.sum(values.reshape(values.shape[0], -1, HEAD_DIM), -1)
    return sums.T.reshape(-1, 2, values.shape[0])


def plain_forward(
    which, layer_input, frames, mask_bias, row_segment, weights
):
    self_full, cross_full, up_full, down_full, bias_full, out_bias_full, vectors = (
        lax.all_gather(part, ("dp", "seq"), axis=0, tiled=True) for part in weights
    )
    vec = jnp.pad(
        jnp.concatenate([vectors.T, out_bias_full[None]]).astype(jnp.float32), ((0, 3), (0, 0))
    )
    model_width = layer_input.shape[1]
    cross_in = [cross_full[:, k * model_width : (k + 1) * model_width] for k in range(4)]
    ckv_full = cross_full[:, model_width : 3 * model_width]
    cqo_full = jnp.concatenate([cross_in[0], cross_in[3]], 1)
    source = layer_input.astype(jnp.float32)
    normed_one = layer_norm(source, vec[0], vec[1]).astype(jnp.bfloat16)
    proj_bias = jnp.concatenate([vec[6], jnp.zeros_like(vec[6]), vec[7]])
    qkv_low = (matmul(normed_one, self_full[:, : 3 * model_width]) + proj_bias).astype(jnp.bfloat16)
    query = qkv_low[:, :model_width] * jnp.bfloat16(0.125)
    kv_own = qkv_low[:, model_width:]
    kv_row = jnp.concatenate([from_behind(kv_own, "seq", 1), kv_own])
    attended, self_lse = self_forward(query, kv_row, mask_bias)
    attended_low = attended.astype(jnp.bfloat16)
    after_self = source + matmul(attended_low, self_full[:, 3 * model_width :]) + vec[8]
    normed_two = layer_norm(after_self, vec[2], vec[3]).astype(jnp.bfloat16)
    cross_query = (matmul(normed_two, cross_in[0]) + vec[9]).astype(jnp.bfloat16)
    cross_key = jnp.einsum(
        "cfd,de->cfe", frames, cross_in[1], preferred_element_type=jnp.float32
    ).astype(jnp.bfloat16)
    cross_value = (
        jnp.einsum("cfd,de->cfe", frames, cross_in[2], preferred_element_type=jnp.float32)
        + vec[10]
    ).astype(jnp.bfloat16)
    row_query = lax.all_gather(cross_query * jnp.bfloat16(0.125), "seq", axis=0, tiled=True)
    cross_kv = jnp.concatenate([cross_key, cross_value], 2)
    part_mixed, part_stats = cross_forward(which, row_query, cross_kv, row_segment)
    mixed_mine, mixed_other = seq_halves(part_mixed, 0)
    stats_mine, stats_other = seq_halves(part_stats, 2)
    mixed_came = swap_halves(mixed_other.astype(jnp.bfloat16))
    stats_came = swap_halves(stats_other)
    peak = jnp.maximum(stats_mine[:, :2], stats_came[:, :2])
    share_mine = stats_mine[:, 2:] * jnp.exp(stats_mine[:, :2] - peak)
    share_came = stats_came[:, 2:] * jnp.exp(stats_came[:, :2] - peak)
    total = share_mine + share_came
    cross_lse = peak + jnp.log(total)
    mixed_full = mixed_mine * per_head(share_mine / total) + mixed_came.astype(
        jnp.float32
    ) * per_head(share_came / total)
    mixed = mixed_full.astype(jnp.bfloat16)
    after_cross = after_self + matmul(mixed, cross_in[3]) + vec[11]
    normed_three = layer_norm(after_cross, vec[4], vec[5]).astype(jnp.bfloat16)
    return (
        bias_full, ckv_full, self_full, cqo_full, up_full, down_full, cross_kv, vec, normed_one, query, kv_row, attended,
        self_lse, after_self, normed_two, row_query, cross_lse, mixed_full, after_cross, normed_three,
    )


def forward(which, layer_input, frames, mask_bias, row_segment, weights):
    if lax.axis_size("dp") != 16:
        return plain_forward(which, layer_input, frames, mask_bias, row_segment, weights)
    self_weights, cross_weights, up_weights, down_weights, up_bias, down_bias, vectors = weights

    def as_row(values):
        return jnp.pad(values, ((0, 0), (0, 128 - values.shape[1])))

    small = jnp.concatenate(
        [as_row(vectors.T), as_row(down_bias[None]), as_row(up_bias[None]), jnp.zeros((2, 128), vectors.dtype)]
    )
    group = jnp.broadcast_to(which[:, None], (2, 128))
    whole = fused_forward(
        group, layer_input, frames, mask_bias, row_segment, small, self_weights, cross_weights, up_weights,
        down_weights,
    )
    return (whole[0][:, 13, : up_bias.shape[0]].reshape(-1),) + tuple(whole[1:])


def plain_backward(
    which, layer_input, mask_bias, row_segment, vec, grad_after_cross, mixed_full, cross_lse, row_query, after_self,
    attended, self_lse, query, kv_row, cqo_full, self_full, cross_kv
):
    tok_span, model_width = layer_input.shape
    source = layer_input.astype(jnp.float32)
    grad_cross_low = grad_after_cross.astype(jnp.bfloat16)
    grad_mixed = matmul(grad_cross_low, cqo_full[:, model_width:].T).astype(jnp.bfloat16)
    row_grad = lax.all_gather(grad_mixed, "seq", axis=0, tiled=True)
    cross_inner = head_sums(grad_mixed.astype(jnp.float32) * mixed_full)
    row_stats = lax.all_gather(jnp.stack([cross_lse, cross_inner]), "seq", axis=3, tiled=True)
    part_query, grad_key, grad_value = cross_backward(
        which, row_query, cross_kv, row_segment, row_stats[0], row_stats[1], row_grad
    )
    grad_query_sum = seq_scatter(part_query).astype(jnp.bfloat16)
    grad_cq_bias = jnp.sum(grad_query_sum, 0, dtype=jnp.float32)
    grad_normed_two = matmul(grad_query_sum, cqo_full[:, :model_width].T)
    grad_cv_bias = jnp.sum(grad_value, (0, 1), dtype=jnp.float32)
    _, norm_pull_two = jax.vjp(layer_norm, after_self, vec[2], vec[3])
    grad_part, grad_gain_two, grad_shift_two = norm_pull_two(grad_normed_two)
    grad_after_self = grad_after_cross + grad_part
    grad_self_low = grad_after_self.astype(jnp.bfloat16)
    grad_self_bias = jnp.sum(grad_self_low, 0, dtype=jnp.float32)
    grad_attended = matmul(grad_self_low, self_full[:, 3 * model_width :].T).astype(jnp.bfloat16)
    self_inner = head_sums(grad_attended.astype(jnp.float32) * attended)
    grad_query, grad_key_row, grad_value_row = self_backward(
        query, kv_row, mask_bias, self_lse, self_inner, grad_attended
    )
    grad_kv = jnp.concatenate([grad_key_row, grad_value_row], 1)
    back_kv = from_behind(grad_kv[:tok_span].astype(jnp.bfloat16), "seq", -1)
    grad_qkv_low = jnp.concatenate(
        [grad_query, grad_kv[tok_span:] + back_kv.astype(jnp.float32)], 1
    ).astype(jnp.bfloat16)
    grad_qkv_bias = jnp.sum(grad_qkv_low, 0, dtype=jnp.float32)
    grad_normed_one = matmul(grad_qkv_low, self_full[:, : 3 * model_width].T)
    _, norm_pull_one = jax.vjp(layer_norm, source, vec[0], vec[1])
    grad_part, grad_gain_one, grad_shift_one = norm_pull_one(grad_normed_one)
    input_grad = grad_after_self + grad_part
    nothing = jnp.zeros_like(grad_cq_bias)
    vec_grads = jnp.stack(
        [
            grad_gain_one,
            grad_shift_one,
            grad_gain_two,
            grad_shift_two,
            nothing,
            nothing,
            grad_qkv_bias[:model_width],
            grad_qkv_bias[2 * model_width :],
            grad_self_bias,
            grad_cq_bias,
            grad_cv_bias,
        ]
        + [nothing] * 5
    )
    return (
        input_grad, grad_query_sum, grad_self_low, grad_qkv_low, vec_grads,
        jnp.concatenate([grad_key, grad_value], 2),
    )


def plain_finish(
    normed_one, grad_qkv_low, attended_low, grad_self_low, normed_two, grad_query_sum, mixed, grad_cross_low, frames,
    cross_kv_grad, ckv_full
):
    width = normed_one.shape[1]
    grads_self = jnp.concatenate([matmul(normed_one.T, grad_qkv_low), matmul(attended_low.T, grad_self_low)], 1)
    grad_ckv = jnp.einsum("cfd,cfe->de", frames, cross_kv_grad, preferred_element_type=jnp.float32)
    grads_cross = jnp.concatenate(
        [matmul(normed_two.T, grad_query_sum), grad_ckv, matmul(mixed.T, grad_cross_low)], 1
    )
    encoder_grad = jnp.einsum(
        "cfe,de->cfd", cross_kv_grad, ckv_full, preferred_element_type=jnp.float32
    )
    return encoder_grad, (grads_self, grads_cross)


def per_device(
    layer_input,
    encoder_states,
    clip_lengths,
    out_grad,
    self_weights,
    cross_weights,
    up_weights,
    down_weights,
    up_bias,
    down_bias,
    vectors,
):
    model_width = layer_input.shape[2]
    tok_span = layer_input.shape[1]
    seq_half = lax.axis_index("seq")
    source = layer_input[0].astype(jnp.float32)
    position = seq_half * tok_span + jnp.arange(tok_span, dtype=jnp.int32)
    clip_ends = jnp.cumsum(clip_lengths[0])
    segment = jnp.sum((position[:, None] >= clip_ends[None, :]).astype(jnp.int32), 1)
    key_position = jnp.concatenate([position - tok_span, position])
    key_segment = jnp.sum((key_position[:, None] >= clip_ends[None, :]).astype(jnp.int32), 1)
    allowed = (
        (key_segment[:, None] == segment[None, :])
        & (key_position[:, None] <= position[None, :])
        & (key_position[:, None] >= 0)
    )
    mask_bias = jnp.where(allowed, 0.0, -1e30).astype(jnp.float32)
    row_position = jnp.arange(2 * tok_span, dtype=jnp.int32)
    row_segment = jnp.sum((row_position[:, None] >= clip_ends[None, :]).astype(jnp.int32), 1)[None]
    big = jnp.argmax(clip_lengths[0]).astype(jnp.int32)
    small_one = jnp.where(big == 0, 1, 0)
    small_two = jnp.where(big == 2, 1, 2)
    last_group = 2 * tok_span // 128 - 1
    order = jnp.stack([big, small_one, small_two]).astype(jnp.int32)
    row_segment = jnp.where(
        row_segment == order[0], 0, jnp.where(row_segment == order[1], 1, jnp.where(row_segment == order[2], 2, 3))
    )
    which = jnp.where(order[1:] < big, 0, last_group).astype(jnp.int32)

    frames = jnp.take(encoder_states[0], order, axis=0, mode="clip")
    (
        bias_full, ckv_full, self_full, cqo_full, up_full, down_full, cross_kv, vec, normed_one, query, kv_row, attended,
        self_lse, after_self, normed_two, row_query, cross_lse, mixed_full, after_cross, normed_three,
    ) = forward(
        which, layer_input[0], frames, mask_bias, row_segment,
        (self_weights, cross_weights, up_weights, down_weights, up_bias, down_bias, vectors),
    )
    bias_full = bias_full.astype(jnp.float32)
    attended_low = attended.astype(jnp.bfloat16)
    mixed = mixed_full.astype(jnp.bfloat16)
    layer_output, grad_after_cross, grad_up, grad_down, grad_up_bias, ffn_rows = ffn(
        normed_three, out_grad[0], after_cross, vec, up_full, bias_full[None], down_full
    )
    grad_cross_low = grad_after_cross.astype(jnp.bfloat16)
    grad_out_bias = ffn_rows[12]
    operands = (
        layer_input[0], mask_bias, row_segment, vec, grad_after_cross, mixed_full, cross_lse, row_query, after_self,
        attended, self_lse, query, kv_row, cqo_full, self_full, cross_kv,
    )
    fused = lax.axis_size("dp") == 16
    if fused:
        group = jnp.broadcast_to(which[:, None], (2, 128))
        large = [g.reshape(32, -1, g.shape[1]) for g in (grad_up, grad_down)]
        *results, up_share, down_share = fused_backward(group, *operands, *large)
    else:
        results = plain_backward(which, *operands)
    input_grad, grad_query_sum, grad_self_low, grad_qkv_low, vec_grads, cross_kv_grad = results
    vector_grads = (vec_grads + ffn_rows)[:12]
    last_operands = (
        normed_one, grad_qkv_low, attended_low, grad_self_low, normed_two, grad_query_sum, mixed, grad_cross_low, frames,
        cross_kv_grad, ckv_full,
    )
    if fused:
        blocks = jnp.pad(vector_grads.reshape(12, 32, -1).transpose(1, 0, 2), ((0, 0), (0, 0), (0, 104)))
        ups = jnp.pad(grad_up_bias.reshape(32, 1, -1), ((0, 0), (0, 0), (0, 32)))
        downs = jnp.pad(grad_out_bias.reshape(32, 1, -1), ((0, 0), (0, 0), (0, 104)))
        small = jnp.concatenate([blocks, ups, downs, jnp.zeros((32, 2, 128), jnp.float32)], 1)
        encoder_grad, self_share, cross_share, row = fused_finish(*last_operands, small)
        shares = (
            self_share, cross_share, up_share, down_share, row[12, : up_bias.shape[0]], row[13, : down_bias.shape[0]],
            row[:12, : vectors.shape[0]].T,
        )
    else:
        encoder_grad, large = plain_finish(*last_operands)
        shares = tuple(
            lax.psum_scatter(part, ("dp", "seq"), scatter_dimension=0, tiled=True)
            for part in large
            + (grad_up.astype(jnp.float32), grad_down.astype(jnp.float32), grad_up_bias[0], grad_out_bias, vector_grads.T)
        )
    return (layer_output[None], input_grad[None], place_clips(order, encoder_grad)) + shares


def solution(mesh):
    return jax.shard_map(
        per_device,
        mesh=mesh,
        in_specs=(
            P("dp", "seq", None),
            P("dp", None, "seq", None),
            P("dp", None),
            P("dp", "seq", None),
            P(("dp", "seq"), None),
            P(("dp", "seq"), None),
            P(("dp", "seq"), None),
            P(("dp", "seq"), None),
            P(("dp", "seq")),
            P(("dp", "seq")),
            P(("dp", "seq"), None),
        ),
        out_specs=(
            P("dp", "seq", None),
            P("dp", "seq", None),
            P("dp", None, "seq", None),
            P(("dp", "seq"), None),
            P(("dp", "seq"), None),
            P(("dp", "seq"), None),
            P(("dp", "seq"), None),
            P(("dp", "seq")),
            P(("dp", "seq")),
            P(("dp", "seq"), None),
        ),
        check_vma=False,
    )
```

profile of v0, /device:TPU:0, one launch (start us, length us, event | category | flops | bytes accessed | tf_op | source)
XLA Modules:
  0.0 330.1 jit_solution(1804990090791529243)
XLA Ops:
  0.7 0.8 reduce-window.8
  1.7 1.1 and_select_fusion.refs_3_.refs_2_
  2.7 1.3 bitcast_reduce_fusion
  5.4 1.2 select_select_fusion
  6.6 0.7 pad_add_fusion.1.order
  7.3 4.7 %gather_fusion = bf16[3,750,768]{2,1,0:T(8,128)(2,1)} fusion(bf16[3,750,768]{2,1,0:T(8,128)(2,1)} %bitcast.31, s32[1024]{0:T(1024)S(1)} %pad_clamp_fusion), kind=kCustom, calls=%fused_computation | custom fusion | bytes 6912012 | tf_op jit(solution)/shard_map/jit(_take)/gather | solution.py:1416
  12.1 0.8 compare_select_fusion
  12.8 0.6 broadcast_in_dim.76.refs_0_
  13.6 0.7 fusion.9.refs_5_
  14.2 126.4 %fused_forward.1 = (bf16[32,16,128]{2,1,0:T(8,128)(2,1)}, bf16[768,1536]{1,0:T(8,128)(2,1)}, bf16[768,3072]{1,0:T(8,128)(2,1)}, bf16[768,1536]{1,0:T(8,128)(2,1)...) custom-call(s32[2,128]{1,0:T(2,128)} %broadcast_in_dim.76.refs_0_, ...), custom_call_target="tpu_custom_call" | custom-call | tf_op jit(solution)/shard_map/fused_forward/pallas_call | solution.py:607
  140.7 0.9 convert_reduce_fusion
  141.7 1.1 copy-done.2
  142.8 1.0 copy-done.4
  143.8 0.8 copy-done.5
  144.6 17.9 %ffn.1 = (bf16[256,768]{1,0:T(8,128)(2,1)}, f32[256,768]{1,0:T(8,128)S(1)}, bf16[768,3072]{1,0:T(8,128)(2,1)}, bf16[3072,768]{1,0:T(8,128)(2,1)}, f32[1,3072]{1,0:T(1,128)S(1)}, /*index=5*/f32[16,768]{1,0:T(8,128)S(1)}) custom-call(bf16[256,768]{1,0:T(8,128)(2,1)S(1)} %copy-done.4, bf16[256,768]{1,0:T(8,128)(2,1)S(1)} %bitcast.27, f32[256,768]{1,0:T(8,128)S(1)} %copy-done.2, ...), custom_call_target="tpu_custom_call" | custom-call | tf_op jit(solution)/shard_map/ffn/pallas_call | solution.py:1040
  162.5 0.9 copy-done
  163.4 76.4 %fused_backward.1 = (f32[256,768]{1,0:T(8,128)}, bf16[256,768]{1,0:T(8,128)(2,1)}, bf16[256,768]{1,0:T(8,128)(2,1)}, bf16[256,2304]{1,0:T(8,128)(2,1)}, f32[16,7...) custom-call(s32[2,128]{1,0:T(2,128)} %broadcast_in_dim.76.refs_0_, ...), custom_call_target="tpu_custom_call" | custom-call | tf_op jit(solution)/shard_map/fused_backward/pallas_call | solution.py:975
  239.9 0.9 slice_add_fusion
  240.9 0.5 broadcast.149
  241.4 0.7 reduce.28
  242.4 0.9 copy.27
  243.3 0.8 convert_element_type.50.refs_7_
  244.1 1.9 convert_element_type.48.refs_2_
  246.0 0.8 convert_element_type.49.refs_6_
  246.8 68.6 %fused_finish.1 = (f32[3,750,768]{2,1,0:T(8,128)}, f32[24,3072]{1,0:T(8,128)}, f32[24,3072]{1,0:T(8,128)}, f32[16,128]{1,0:T(8,128)}) custom-call(bf16[256,768]{1,0:T(8,128)(2,1)} %get-tuple-element.72.refs_0_, bf16[256,2304]{1,0:T(8,128)(2,1)} %get-tuple-element.73.refs_1_, bf16[256,768]{1,0:T(8,128)(2,1)} %convert_element_type.48.refs_2_, ...), custom_call_target="tpu_custom_call" | custom-call | tf_op jit(solution)/shard_map/fused_finish/pallas_call | solution.py:1165
  315.4 9.2 %place_clips.1 = f32[13500,1,128]{2,1,0:T(1,128)} custom-call(s32[3]{0:T(128)S(1)} %pad_add_fusion.1.order, f32[3,750,768]{2,1,0:T(8,128)} %get-tuple-element.82.in_ref), custom_call_target="tpu_custom_call" | custom-call | tf_op jit(solution)/shard_map/place_clips/pallas_call | solution.py:1065
  324.7 0.6 slice_bitcast_fusion
  326.3 0.9 copy.34
  327.2 0.7 copy.35
  327.9 0.7 copy.36
  328.6 0.7 copy.37
  329.3 0.7 copy.38
  (46 shorter events, 1.9 us)
Async XLA Ops:
  7.3 6.2 %copy-start.13 = (bf16[24,12]{0,1:T(8,128)(2,1)S(1)}, bf16[24,12]{0,1:T(8,128)(2,1)}, u32[]{:S(2)}) copy-start(bf16[24,12]{0,1:T(8,128)(2,1)} %param.21) | copy-start | bytes 1732
  7.3 6.2 %copy-start.14 = (bf16[96]{0:T(256)(128)(2,1)S(1)}, bf16[96]{0:T(256)(128)(2,1)}, u32[]{:S(2)}) copy-start(bf16[96]{0:T(256)(128)(2,1)} %param.19) | copy-start | bytes 580
  7.3 6.2 %copy-start.15 = (bf16[24]{0:T(256)(128)(2,1)S(1)}, bf16[24]{0:T(256)(128)(2,1)}, u32[]{:S(2)}) copy-start(bf16[24]{0:T(256)(128)(2,1)} %param.20) | copy-start | bytes 148
  12.1 129.6 %copy-start.3 = (bf16[1,256,768]{2,1,0:T(8,128)(2,1)S(1)}, bf16[1,256,768]{2,1,0:T(8,128)(2,1)}, u32[]{:S(2)}) copy-start(bf16[1,256,768]{2,1,0:T(8,128)(2,1)} %param.14) | copy-start | bytes 1179652
  141.7 1.1 copy-start.2
  142.8 1.0 copy-start.4
  143.8 0.8 copy-start.5
  162.5 0.9 copy-start
  163.4 79.9 %copy-start.1 = (f32[256,768]{1,0:T(8,128)S(1)}, f32[256,768]{1,0:T(8,128)}, u32[]{:S(2)}) copy-start(f32[256,768]{1,0:T(8,128)} %copy-done) | copy-start | bytes 2359300
  239.8 6.2 %copy-start.6 = (f32[256,768]{1,0:T(8,128)S(1)}, f32[256,768]{1,0:T(8,128)}, u32[]{:S(2)}) copy-start(f32[256,768]{1,0:T(8,128)} %get-tuple-element.58.refs_6_) | copy-start | bytes 2359300
  315.4 9.3 %copy-start.12 = (f32[16,128]{1,0:T(8,128)S(1)}, f32[16,128]{1,0:T(8,128)}, u32[]{:S(2)}) copy-start(f32[16,128]{1,0:T(8,128)} %get-tuple-element.87) | copy-start | bytes 24580
  315.4 10.9 %copy-start.7 = (f32[256,768]{1,0:T(8,128)S(1)}, f32[256,768]{1,0:T(8,128)}, u32[]{:S(2)}) copy-start(f32[256,768]{1,0:T(8,128)} %get-tuple-element.71) | copy-start | bytes 2359300
  315.4 11.8 %copy-start.11 = (f32[24,3072]{1,0:T(8,128)S(1)}, f32[24,3072]{1,0:T(8,128)}, u32[]{:S(2)}) copy-start(f32[24,3072]{1,0:T(8,128)} %get-tuple-element.135) | copy-start | bytes 884740
  315.4 12.5 %copy-start.10 = (f32[24,3072]{1,0:T(8,128)S(1)}, f32[24,3072]{1,0:T(8,128)}, u32[]{:S(2)}) copy-start(f32[24,3072]{1,0:T(8,128)} %get-tuple-element.136) | copy-start | bytes 884740
  315.4 13.2 %copy-start.9 = (f32[24,3072]{1,0:T(8,128)S(1)}, f32[24,3072]{1,0:T(8,128)}, u32[]{:S(2)}) copy-start(f32[24,3072]{1,0:T(8,128)} %get-tuple-element.137) | copy-start | bytes 884740
  324.7 4.7 %copy-start.8 = (f32[96,768]{1,0:T(8,128)S(1)}, f32[96,768]{1,0:T(8,128)}, u32[]{:S(2)}) copy-start(f32[96,768]{1,0:T(8,128)} %get-tuple-element.138) | copy-start | bytes 884740
where the time goes:
time: 331 us; the launch traced here: 330 us
  Pallas kernels  299 us (90%)
  local copies, waits for them, and re-layouts  16.5 us (5%)
  other arithmetic  12.8 us (4%)
    pallas_call x1, Pallas kernels, fused_forward(): pl.pallas_call(forward_kernel, in_specs=[vmem] * 5 + [hbm] + [vmem] * 3 +...  126 us
    pallas_call x1, Pallas kernels, fused_backward(): pl.pallas_call(backward_kernel, in_specs=[vmem] * 14 + [hbm] * 5, out_spe...  76.4 us
    pallas_call x1, Pallas kernels, fused_finish(): pl.pallas_call(finish_kernel, in_specs=[vmem] * 10 + [hbm] * 2, out_specs...  68.6 us
    pallas_call x1, Pallas kernels, ffn(): pl.pallas_call(ffn_kernel, grid=(hidden // size,), in_specs=[rows, rows,...  17.9 us
    pallas_call x1, Pallas kernels, place_clips(): pl.pallas_call(place_clips_kernel, grid_spec=pltpu.PrefetchScalarGridSpec...  9.23 us
    unnamed x37, local copies, waits for them, and re-layouts  7.58 us

commit v1 on v0

--- a/solution.py
+++ b/solution.py
@@ -225,41 +225,20 @@
         base = self.z * 4
         self.first = (base + self.p_first, self.core)
         self.second = (base + self.p_second, self.core)
-        self.up = (lax.rem(self.dp + 4, 16), self.core)
-        self.down = (lax.rem(self.dp + 12, 16), self.core)
         self.mate = (self.dp, 1 - self.core)
-        self.has_up = self.z < Z - 1
-        self.has_down = self.z > 0
+        half = self.z // 2
+        near = self.z + half * (3 - 2 * self.z)
+        self.line = [base + half * (3 - 2 * base) for base in (3, 2, 1 - near)]
+        self.peers = [self.mate, self.first, self.second] + [self.on_line(z) for z in self.line]
+
+    def on_line(self, z):
+        return (z * 4 + self.p, self.core)
 
     def greet(self):
         barrier = pltpu.get_barrier_semaphore()
-        for target in (self.mate, self.first, self.second):
+        for target in self.peers:
             pl.semaphore_signal(barrier, inc=1, device_id=target, device_id_type=MESH)
-
-        @pl.when(self.has_up)
-        def _():
-            pl.semaphore_signal(barrier, inc=1, device_id=self.up, device_id_type=MESH)
-
-        @pl.when(self.has_down)
-        def _():
-            pl.semaphore_signal(barrier, inc=1, device_id=self.down, device_id_type=MESH)
-
-        pl.semaphore_wait(barrier, 3 + (self.z + 3) // 4 + (6 - self.z) // 4)
-
-
-def when(cond, fn):
-    if cond is None:
-        fn()
-    else:
-        pl.when(cond)(fn)
-
-
-def both(a, b):
-    if a is None:
-        return b
-    if b is None:
-        return a
-    return jnp.logical_and(a, b)
+        pl.semaphore_wait(barrier, len(self.peers))
 
 
 HALF_COLS = {1: 768, 2: 1536, 3: 768, 4: 1536}
@@ -284,46 +263,43 @@
         rows = pl.ds(pl.multiple_of(chip * 48, 48), 48)
         return self.outs[m].at[rows, columns(core, HALF_COLS[m])]
 
-    def sender(self, m, src, chip, target, cond):
+    def sender(self, m, src, chip, target):
         copy = pltpu.make_async_remote_copy(
             src_ref=src, dst_ref=self.piece(m, chip, self.me.core), send_sem=self.send_sem.at[len(self.sends)],
             recv_sem=self.recv_sem.at[m, chip * 2 + self.me.core], device_id=target, device_id_type=MESH)
-        self.sends.append((cond, copy))
-        return lambda: when(cond, copy.start)
-
-    def arrival(self, m, chip, core, cond=None):
+        self.sends.append(copy)
+        return copy.start
+
+    def arrival(self, m, chip, core):
         piece = self.piece(m, chip, core)
-        copy = pltpu.make_async_remote_copy(
+        return pltpu.make_async_remote_copy(
             src_ref=piece, dst_ref=piece, send_sem=self.send_sem.at[0],
-            recv_sem=self.recv_sem.at[m, chip * 2 + core], device_id=self.me.mate, device_id_type=MESH)
-        return lambda: when(cond, copy.wait_recv)
-
-    def forward(self, m, z, p, targets, cond=None):
+            recv_sem=self.recv_sem.at[m, chip * 2 + core], device_id=self.me.mate, device_id_type=MESH).wait_recv
+
+    def forward(self, m, z, p, targets):
         chip = z * 4 + p
-        return [self.arrival(m, chip, self.me.core, cond)] + [
-            self.sender(m, self.piece(m, chip, self.me.core), chip, target, both(cond, extra))
-            for target, extra in targets
+        return [self.arrival(m, chip, self.me.core)] + [
+            self.sender(m, self.piece(m, chip, self.me.core), chip, target) for target in targets
         ]
 
     def steps(self, m):
         me = self.me
-        up, down, mate = (me.up, me.has_up), (me.down, me.has_down), (me.mate, None)
-        first, second = (me.first, None), (me.second, None)
-
-        def at(d, p, below_to, above_to):
-            if d == 0:
-                return self.forward(m, me.z, p, below_to)
-            return self.forward(m, me.z - d, p, below_to, me.z - d >= 0) + self.forward(
-                m, me.z + d, p, above_to, me.z + d < Z)
-
-        begin = [self.sender(m, self.srcs[m], me.dp, *target) for target in (up, down, first, second, mate)]
+        begin = [
+            self.sender(m, self.srcs[m], me.dp, target)
+            for target in [me.on_line(z) for z in me.line] + [me.first, me.second, me.mate]
+        ]
         begin.append(pltpu.make_async_copy(self.srcs[m], self.piece(m, me.dp, me.core), self.own_sem.at[m]).start)
-        steps = [begin]
-        for d in range(1, Z + 1):
-            line = at(d, me.p, [up, first, second, mate], [down, first, second, mate]) if d < Z else []
-            steps.append(line + at(d - 1, me.p_first, [second, mate], [second, mate]))
-        steps.append([act for p in (me.p_second, me.p_diag) for d in range(Z) for act in at(d, p, [mate], [mate])])
-        return steps
+        line = []
+        for z in me.line[::-1]:
+            line += self.forward(m, z, me.p, [me.first, me.second, me.mate])
+        beside = []
+        for z in [me.z] + me.line[::-1]:
+            beside += self.forward(m, z, me.p_first, [me.second, me.mate])
+        rest = []
+        for p in (me.p_second, me.p_diag):
+            for z in [me.z] + me.line[::-1]:
+                rest += self.forward(m, z, p, [me.mate])
+        return [begin, line, beside, rest]
 
     def run(self, entry):
         for act in entry[2]:
@@ -348,33 +324,38 @@
             self.arrival(m, chip, 1 - self.me.core)()
 
     def finish(self):
-        for cond, copy in self.sends:
-            when(cond, copy.wait_send)
+        for copy in self.sends:
+            copy.wait_send()
 
 
 GATHER_TIMES = (
-    (1, 4.5, 8.5, 12.5, 16.5, 18.5),
-    (0, 4, 8, 12, 16, 18),
-    (2, 9, 14, 19, 24, 27),
-    (10, 20, 25, 29, 33, 36),
-    (20, 31, 38, 45, 51, 55),
-    (32, 50, 58, 66, 73, 78),
+    (1, 6, 10, 15),
+    (0, 5, 9, 14),
+    (2, 11, 19, 27),
+    (10, 20, 26, 34),
+    (18, 31, 42, 54),
+    (30, 48, 60, 74),
 )
 
 
-def loop_with(gather, count, begin, length, body):
-    due = [gather.take_until(begin + length * i) for i in range(count)]
+def loop_with(steps, count, begin, length, body, slots=(0,)):
+    due = {}
+    for i in range(count):
+        for part, k in sorted((part, k) for k, part in enumerate(slots)):
+            due[i, k] = steps.take_until(begin + length * (i + part))
 
     def turn(i, carry):
-        for k, tasks in enumerate(due):
-            if tasks:
-
-                def run(tasks=tasks):
-                    for task in tasks:
-                        gather.run(task)
-
-                pl.when(i == k)(run)
-        body(i)
+        def tick(k):
+            for at in range(count):
+                if due[at, k]:
+
+                    def run(entries=due[at, k]):
+                        for entry in entries:
+                            steps.run(entry)
+
+                    pl.when(i == at)(run)
+
+        body(i, tick)
         return carry
 
     lax.fori_loop(0, count, turn, 0)
@@ -385,6 +366,10 @@
     centred = values - average
     spread = jnp.mean(centred * centred, -1, keepdims=True)
     return centred * lax.rsqrt(spread + 1e-05) * gain + shift
+
+
+def two_heads(values):
+    return jnp.concatenate([one_head(values, 0), one_head(values, 1)], 0)
 
 
 def columns(j, size=128):
@@ -433,14 +418,14 @@
         came = came_ref[...].astype(jnp.float32)
         both_ref[...] = jnp.concatenate(
             [jnp.where(core == 0, own, came), jnp.where(core == 0, came, own)], 0).astype(jnp.bfloat16)
-        gather.run_until((0, 1, 2, 2, 4.5)[m])
+        gather.run_until((0, 1, 2, 2, 2)[m])
 
     def fetch(src, dst, k):
         copy = pltpu.make_async_copy(src, dst, load_sem.at[k])
         copy.start()
         copy.wait()
 
-    gather.run_until(18.5)
+    gather.run_until(15)
     gather.need(0)
     fetch(small_out, small_vm, 0)
     row = lax.broadcasted_iota(jnp.int32, (128, width), 0)
@@ -462,12 +447,13 @@
     clips = frames_ref.shape[0]
     tiles = 2 * width // 256
 
-    def project(t):
+    def project(t, tick):
+        tick(0)
         clip, tile = t // tiles, t % tiles
         result = dot(frames_ref[clip], ckv_vm[:, columns(tile, 256)], NN)
         is_value = (tile >= 3).astype(jnp.float32)
         shift = vec_ref[10:11, columns(tile % 3, 256)] * is_value
-        kv_vm[clip, :, columns(tile, 256)] = (result + shift).astype(jnp.bfloat16)
+        kv_vm[clip, :frames_ref.shape[1], columns(tile, 256)] = (result + shift).astype(jnp.bfloat16)
 
     loop_with(gather, clips * tiles, 20, 0.65, project)
     kv_store = pltpu.make_async_copy(kv_vm, kv_out, load_sem.at[1])
@@ -487,7 +473,8 @@
     gather.run_until(35)
     kv_copy.wait()
 
-    def self_pair(j):
+    def self_pair(j, tick):
+        tick(0)
         cols = columns(j)
         keys = kv_row_ref[:, cols]
         values_t = kv_row_ref[:, columns(j + 6)].T
@@ -517,42 +504,47 @@
     gather.run_until(48)
     query_copy.wait()
 
-    def attend(clip, values_t, query, j, h):
-        scores = dot(kv_vm[clip, :, columns(j)], query, NT)
+    frame_count = frames_ref.shape[1]
+
+    def attend(clip, values_t, query, j):
+        scores = dot(kv_vm[clip, :frame_count, columns(j)], query, NT)
         peak = jnp.max(scores, 0, keepdims=True)
         terms = jnp.exp(scores - peak)
         total = jnp.sum(terms, 0, keepdims=True)
-        result = dot(values_t[h * 64:(h + 1) * 64], terms.astype(jnp.bfloat16), NN)
-        return result / total, peak, total
-
-    def cross_pair(j):
-        values_t = kv_vm[0, :, columns(j + 6)].T
+        return dot(values_t, terms.astype(jnp.bfloat16), NN), peak, total
+
+    def cross_pair(j, tick):
+        values_t = kv_vm[0, :frame_count, columns(j + 6)].T
         mine = seg_ref[...] == 0
         for h in range(2):
-            result, peak, total = attend(0, values_t, one_head(row_query_ref[:, columns(j)], h), j, h)
-            acc_ref[h * 64:(h + 1) * 64] = jnp.where(mine, result, 0.0)
+            tick(h)
+            rows = slice(h * 64, (h + 1) * 64)
+            result, peak, total = attend(0, values_t[rows], one_head(row_query_ref[:, columns(j)], h), j)
+            acc_ref[rows] = jnp.where(mine, result / total, 0.0)
             stat_ref[h:h + 1] = jnp.where(mine, peak, 0.0)
             stat_ref[2 + h:3 + h] = jnp.where(mine, total, 1.0)
         for clip in (1, 2):
-            values_t = kv_vm[clip, :, columns(j + 6)].T
+            tick(clip + 1)
+            values_t = kv_vm[clip, :frame_count, columns(j + 6)].T
             query_rows = jnp.where(
                 group_ref[clip - 1:clip] == 0, row_query_ref[:128, columns(j)], row_query_ref[384:, columns(j)])
+            result, peak, total = attend(clip, values_t, two_heads(query_rows), j)
             for h in range(2):
-                result, peak, total = attend(clip, values_t, one_head(query_rows, h), j, h)
+                rows, part = slice(h * 64, (h + 1) * 64), slice(h * 128, (h + 1) * 128)
+                of_head = result[rows, part] / total[:, part]
                 for spot in (0, 3):
                     cols = slice(spot * 128, (spot + 1) * 128)
                     mine = seg_ref[:, cols] == clip
-                    rows = slice(h * 64, (h + 1) * 64)
-                    acc_ref[rows, cols] = jnp.where(mine, result, acc_ref[rows, cols])
-                    stat_ref[h:h + 1, cols] = jnp.where(mine, peak, stat_ref[h:h + 1, cols])
-                    stat_ref[2 + h:3 + h, cols] = jnp.where(mine, total, stat_ref[2 + h:3 + h, cols])
+                    acc_ref[rows, cols] = jnp.where(mine, of_head, acc_ref[rows, cols])
+                    stat_ref[h:h + 1, cols] = jnp.where(mine, peak[:, part], stat_ref[h:h + 1, cols])
+                    stat_ref[2 + h:3 + h, cols] = jnp.where(mine, total[:, part], stat_ref[2 + h:3 + h, cols])
         my_cols, mate_cols = columns(core, toks), columns(1 - core, toks)
         part_ref[j] = acc_ref[:, my_cols]
         part_stat_ref[j] = stat_ref[:, my_cols]
         give_ref[j] = acc_ref[:, mate_cols].astype(jnp.bfloat16)
         give_stat_ref[j] = stat_ref[:, mate_cols]
 
-    loop_with(gather, 6, 48, 3.8, cross_pair)
+    loop_with(gather, 6, 48, 3, cross_pair, (0, 0.33, 0.66, 0.83))
     give_copy = to_mate(give_ref, take_ref, 2)
     give_copy.start()
     give_stat_copy = to_mate(give_stat_ref, take_stat_ref, 3)
@@ -580,6 +572,7 @@
     after_cross = after_self_ref[...] + dot(mixed_ref[...].astype(jnp.bfloat16), cqo_vm[:, width:], NN) + vec(11)
     after_cross_ref[...] = after_cross
     normed_three_ref[...] = norm_rows(after_cross, vec(4), vec(5)).astype(jnp.bfloat16)
+    gather.run_until(1000)
     gather.need(4)
     gather.need(5)
     kv_store.wait()
@@ -597,7 +590,7 @@
         (hbm, shape((32, 16, 128), low)), (hbm, shape((width, 2 * width), low)), (hbm, shape((width, 4 * width), low)),
         (hbm, shape((width, 2 * width), low)), (hbm, shape((width, 4 * width), low)),
         (hbm, shape((4 * width, width), low)),
-        (hbm, shape((clips, count, 2 * width), low)),
+        (hbm, shape((clips, width, 2 * width), low)),
         (vmem, shape((16, width), full)), (vmem, shape((toks, width), low)), (vmem, shape((toks, width), low)),
         (vmem, shape((2 * toks, 2 * width), low)), (vmem, shape((toks, width), full)),
         (vmem, shape((pairs, 2, toks), full)), (vmem, shape((toks, width), full)), (vmem, shape((toks, width), low)),
@@ -613,7 +606,7 @@
             pltpu.VMEM((2, 24, 2 * width), low), pltpu.VMEM((2, 24, width), low), pltpu.VMEM((2, 48, 2 * width), low),
             pltpu.VMEM((2, 48, width), low), pltpu.VMEM((32, 16, 128), low),
             pltpu.VMEM((width, 2 * width), low), pltpu.VMEM((width, 4 * width), low), pltpu.VMEM((width, 2 * width), low),
-            pltpu.VMEM((clips, count, 2 * width), low), pltpu.VMEM((128, 2 * toks), full), pltpu.VMEM((4, 2 * toks), full),
+            pltpu.VMEM((clips, width, 2 * width), low), pltpu.VMEM((128, 2 * toks), full), pltpu.VMEM((4, 2 * toks), full),
             pltpu.VMEM((pairs, 128, toks), full), pltpu.VMEM((pairs, 4, toks), full),
             pltpu.VMEM((pairs, 128, toks), low), pltpu.VMEM((pairs, 4, toks), full),
             pltpu.VMEM((pairs, 128, toks), low), pltpu.VMEM((pairs, 4, toks), full),
@@ -626,25 +619,39 @@
 
 
 class Scatter:
-    def __init__(self, me, grads, outs, buffers, sems, times):
-        self.me, self.grads, self.outs = me, grads, outs
-        self.buffers = buffers
-        self.send_sem, self.own_sem, self.pair_sem, self.plane_sem, self.line_sem = sems
-        self.sends = []
-        half = me.z // 2
-        near = me.z + half * (3 - 2 * me.z)
-        self.order = [base + half * (3 - 2 * base) for base in (3, 2, 1 - near, near)]
+    def __init__(self, me, grads, outs, buffers, sems, times, after):
+        self.me, self.grads, self.outs, self.buffers = me, grads, outs, buffers
+        self.send_sem, self.own_sem, self.pair_sem, self.plane_sem, self.line_sem, self.free_sem = sems
+        self.sends = {m: [] for m in range(len(grads))}
+        self.count = 0
+        self.order = me.line + [me.z]
         self.tasks = []
-        for m, (begin, ats) in enumerate(times):
-            for at, acts in zip(ats, self.steps(m)):
-                self.tasks.append((begin + at, m, acts))
+        for m, times_of in enumerate(times):
+            for time, acts in zip(times_of, self.steps(m)):
+                self.tasks.append((time, m, acts))
+        for late, early in after.items():
+            self.tasks = [
+                (time, m, ([self.wait_free] if m == late and time == times[late][0] else []) + acts
+                 + ([functools.partial(self.give_free, early)] if m == early and time == times[early][-1] else []))
+                for time, m, acts in self.tasks
+            ]
         self.tasks.sort(key=lambda entry: entry[:2])
 
-    def sender(self, src, dst, sem, target):
+    def give_free(self, m):
+        for copy in self.sends.pop(m):
+            copy.wait_send()
+        for target in self.me.peers:
+            pl.semaphore_signal(self.free_sem, inc=1, device_id=target, device_id_type=MESH)
+
+    def wait_free(self):
+        pl.semaphore_wait(self.free_sem, len(self.me.peers))
+
+    def sender(self, m, src, dst, sem, target):
         copy = pltpu.make_async_remote_copy(
-            src_ref=src, dst_ref=dst, send_sem=self.send_sem.at[len(self.sends)], recv_sem=sem, device_id=target,
+            src_ref=src, dst_ref=dst, send_sem=self.send_sem.at[self.count], recv_sem=sem, device_id=target,
             device_id_type=MESH)
-        self.sends.append(copy)
+        self.count += 1
+        self.sends[m].append(copy)
         return copy.start
 
     def arrival(self, dst, sem):
@@ -656,10 +663,6 @@
         me, order = self.me, self.order
         grad, out = self.grads[m], self.outs[m]
         own, pair, plane_a, plane_b, plane_c, line = self.buffers[m]
-
-        def own_at(z, p):
-            return grad.at[z, p, me.core] if own is None else own.at[z, p]
-
         own_sem, pair_sem, plane_sem, line_sem = self.own_sem, self.pair_sem, self.plane_sem, self.line_sem
 
         def adder(dst, *others):
@@ -670,68 +673,48 @@
                 dst[...] = total.astype(dst.dtype)
             return act
 
-        loads = {}
-        begin = []
-        for k, p in enumerate((me.p_diag, me.p_second, me.p_first, me.p)):
-            if own is not None:
-                loads[k] = pltpu.make_async_copy(grad.at[:, p, me.core], own.at[:, p], own_sem.at[m, p])
-                begin.append(loads[k].start)
+        loads = [
+            pltpu.make_async_copy(grad.at[:, p, me.core], own, own_sem.at[m, k])
+            for k, p in enumerate((me.p_diag, me.p_second, me.p_first, me.p))
+        ]
+        begin = [loads[0].start]
         for p in (me.p_diag, me.p_first, me.p_second, me.p):
-            begin.append(self.sender(grad.at[:, p, 1 - me.core], pair.at[:, p], pair_sem.at[m, p], me.mate))
-
-        def paired(k, p):
-            return ([loads[k].wait] if loads else []) + [self.arrival(pair.at[:, p], pair_sem.at[m, p])]
-
-        diag = paired(0, me.p_diag)
-        second = paired(1, me.p_second)
-        first = paired(2, me.p_first)
+            begin.append(self.sender(m, grad.at[:, p, 1 - me.core], pair.at[:, p], pair_sem.at[m, p], me.mate))
+        diag, second, first, last = (
+            [loads[k].wait, self.arrival(pair.at[:, p], pair_sem.at[m, p])]
+            for k, p in enumerate((me.p_diag, me.p_second, me.p_first, me.p))
+        )
         for z in order:
-            diag += [adder(own_at(z, me.p_diag), pair.at[z, me.p_diag]),
-                     self.sender(own_at(z, me.p_diag), plane_a.at[z], plane_sem.at[m, 0, z], me.second)]
-            second += [adder(own_at(z, me.p_second), pair.at[z, me.p_second]),
-                       self.sender(own_at(z, me.p_second), plane_c.at[z], plane_sem.at[m, 2, z], me.second)]
+            diag += [adder(pair.at[z, me.p_diag], own.at[z]),
+                     self.sender(m, pair.at[z, me.p_diag], plane_a.at[z], plane_sem.at[m, 0, z], me.second)]
+            second += [adder(pair.at[z, me.p_second], own.at[z]),
+                       self.sender(m, pair.at[z, me.p_second], plane_c.at[z], plane_sem.at[m, 2, z], me.second)]
             first += [self.arrival(plane_a.at[z], plane_sem.at[m, 0, z]),
-                      adder(own_at(z, me.p_first), pair.at[z, me.p_first], plane_a.at[z]),
-                      self.sender(own_at(z, me.p_first), plane_b.at[z], plane_sem.at[m, 1, z], me.first)]
-        steps = [begin, diag, second, first]
-        for k, z in enumerate(order):
-            acts = paired(3, me.p) if k == 0 else []
-            acts += [self.arrival(plane_b.at[z], plane_sem.at[m, 1, z]),
-                     self.arrival(plane_c.at[z], plane_sem.at[m, 2, z])]
-            if k < 3:
-                acts.append(adder(own_at(z, me.p), pair.at[z, me.p], plane_b.at[z], plane_c.at[z]))
-                upward = (z - me.z + 3) // 4
-                source = me.z + 1 - 2 * upward
-                came = jnp.logical_and(source >= 0, source < Z)
-                slot = line.at[upward, z]
-                arrival, add = self.arrival(slot, line_sem.at[m, upward, z]), adder(own_at(z, me.p), slot)
-
-                def join(came=came, arrival=arrival, add=add):
-                    def go():
-                        arrival()
-                        add()
-                    pl.when(came)(go)
-
-                target = (lax.rem(me.dp + 12 + 8 * upward, 16), me.core)
-                acts += [join, self.sender(own_at(z, me.p), slot, line_sem.at[m, upward, z], target)]
-            else:
-                def total():
-                    part = own_at(me.z, me.p)[...].astype(jnp.float32) + pair[me.z, me.p].astype(jnp.float32)
-                    out[...] = part + plane_b[me.z].astype(jnp.float32) + plane_c[me.z].astype(jnp.float32)
-
-                acts.append(total)
-                for upward, cond in ((0, me.has_up), (1, me.has_down)):
-                    arrival = self.arrival(line.at[upward, me.z], line_sem.at[m, upward, me.z])
-
-                    def last(upward=upward, cond=cond, arrival=arrival):
-                        def go():
-                            arrival()
-                            out[...] += line[upward, me.z].astype(jnp.float32)
-                        pl.when(cond)(go)
-
-                    acts.append(last)
-            steps.append(acts)
-        return steps
+                      adder(pair.at[z, me.p_first], own.at[z], plane_a.at[z]),
+                      self.sender(m, pair.at[z, me.p_first], plane_b.at[z], plane_sem.at[m, 1, z], me.first)]
+        diag.append(loads[1].start)
+        second.append(loads[2].start)
+        first.append(loads[3].start)
+        for z in me.line:
+            last += [self.arrival(plane_b.at[z], plane_sem.at[m, 1, z]),
+                     self.arrival(plane_c.at[z], plane_sem.at[m, 2, z]),
+                     adder(pair.at[z, me.p], own.at[z], plane_b.at[z], plane_c.at[z]),
+                     self.sender(m, pair.at[z, me.p], line.at[me.z], line_sem.at[m, me.z], me.on_line(z))]
+
+        def total():
+            part = own[me.z].astype(jnp.float32) + pair[me.z, me.p].astype(jnp.float32)
+            out[...] = part + plane_b[me.z].astype(jnp.float32) + plane_c[me.z].astype(jnp.float32)
+
+        def from_line(source):
+            def act():
+                out[...] += line[source].astype(jnp.float32)
+            return act
+
+        final = [self.arrival(plane_b.at[me.z], plane_sem.at[m, 1, me.z]),
+                 self.arrival(plane_c.at[me.z], plane_sem.at[m, 2, me.z]), total]
+        for source in me.line[::-1]:
+            final += [self.arrival(line.at[source], line_sem.at[m, source]), from_line(source)]
+        return [begin, diag, second, first, last, final]
 
     def run(self, entry):
         for act in entry[2]:
@@ -749,30 +732,33 @@
 
     def finish(self):
         self.run_until(10**6)
-        for copy in self.sends:
-            copy.wait_send()
-
-
-def scatter_scratch(grads):
-    shapes = []
-    for g in grads:
-        for lead in ((4, 4), (4, 4), (4,), (4,), (4,), (2, 4)):
-            shapes.append(pltpu.VMEM(lead + g.shape[1:], g.dtype))
-    count = len(grads)
-    return shapes + [
-        pltpu.SemaphoreType.DMA((20 * count,)),
-        pltpu.SemaphoreType.DMA((count, 4)),
-        pltpu.SemaphoreType.DMA((count, 4)),
-        pltpu.SemaphoreType.DMA((count, 3, 4)),
-        pltpu.SemaphoreType.DMA((count, 2, 4)),
-    ]
+        for copies in self.sends.values():
+            for copy in copies:
+                copy.wait_send()
+
+
+def scatter_buffers(grad):
+    leads = ((4,), (4, 4), (4,), (4,), (4,), (4,))
+    return [pltpu.VMEM(lead + grad.shape[1:], grad.dtype) for lead in leads]
+
+
+def scatter_sems(count):
+    dma = pltpu.SemaphoreType.DMA
+    return [dma((20 * count,)), dma((count, 4)), dma((count, 4)), dma((count, 3, 4)), dma((count, 4)),
+            pltpu.SemaphoreType.REGULAR]
 
 
 def scatter_view(grad):
     return grad.reshape((4, 4, 2) + grad.shape[1:])
 
 
-BACK_TIMES = ((0, (0, 4, 6, 12, 22, 27, 32, 38)), (1, (0, 14, 16, 22, 34, 39, 44, 50)))
+BACK_TIMES = (
+    (0, 8, 9, 20, 32, 44),
+    (1, 20, 21, 34, 46, 58),
+    (44, 54, 55, 68, 78, 88),
+    (80, 85, 86, 94, 102, 110),
+    (80.5, 86.0, 87.0, 95.0, 103.0, 111.5),
+)
 
 
 def norm_rows_back(values, gain, grad):
@@ -789,26 +775,31 @@
 
 def backward_kernel(*refs):
     (group_ref, x_ref, bias_ref, seg_ref, vec_ref, gac_ref, mixed_ref, cross_lse_ref, row_query_ref, after_self_ref,
-     attended_ref, self_lse_ref, query_ref, kv_row_ref, cqo_hbm, self_hbm, kv_hbm, up_hbm, down_hbm) = refs[:19]
-    (input_grad_ref, cq_ref, self_low_ref, qkv_ref, vec_grad_ref, dkv_hbm, up_out, down_out) = refs[19:27]
-    scratch = refs[27:]
-    scatter_refs, scratch = scratch[:17], scratch[17:]
-    (cross_vm, self_vm, kv_vm, row_grad_ref, row_stat_ref, acc_ref, own_ref, give_ref, take_ref,
-     take_query_ref, load_sem, mate_sems) = scratch
+     attended_ref, self_lse_ref, query_ref, kv_row_ref, normed_one_ref, normed_two_ref, rows_ref, up_bias_ref, cqo_hbm,
+     ckv_hbm, self_hbm, kv_hbm, frames_hbm, up_hbm, down_hbm) = refs[:25]
+    (input_grad_ref, encoder_hbm, up_out, down_out, cross_out, self_out, small_out, dkv_hbm, cross_hbm,
+     self_grad_hbm) = refs[25:35]
+    scratch = refs[35:]
+    up_buffers, down_buffers, cross_buffers, small_buffers = (scratch[k * 6:(k + 1) * 6] for k in range(4))
+    sems, scratch = scratch[24:30], scratch[30:]
+    (cross_vm, kv_vm, frame_ref, turned_ref, tile_ref, stage_ref, small_ref, row_grad_ref, row_stat_ref, acc_ref,
+     own_ref, give_ref, take_ref, take_query_ref, cq_ref, qkv_ref, vec_grad_ref, load_sem, mate_sems, tile_sem,
+     stage_sem) = scratch
     me = Place()
     core = me.core
     toks, width = x_ref.shape
-    loads = [
-        pltpu.make_async_copy(cqo_hbm.at[:, pl.ds(0, width)], cross_vm.at[0], load_sem.at[0]),
-        pltpu.make_async_copy(cqo_hbm.at[:, pl.ds(width, width)], cross_vm.at[1], load_sem.at[1]),
-        pltpu.make_async_copy(kv_hbm, kv_vm, load_sem.at[2]),
-        pltpu.make_async_copy(self_hbm, self_vm, load_sem.at[3]),
-    ]
-    for copy in (loads[1], loads[0], loads[2], loads[3]):
+    frames = frames_hbm.shape[1]
+    clips = kv_hbm.shape[0]
+    low, full = jnp.bfloat16, jnp.float32
+    halves = [pltpu.make_async_copy(cqo_hbm.at[:, pl.ds(k * width, width)], cross_vm.at[k], load_sem.at[k])
+              for k in range(2)]
+    kv_load = pltpu.make_async_copy(kv_hbm, kv_vm, load_sem.at[2])
+    for copy in (halves[1], kv_load, halves[0]):
         copy.start()
     me.greet()
-    scatter = Scatter(me, (up_hbm, down_hbm), (up_out, down_out), (scatter_refs[:6], scatter_refs[6:12]),
-                      scatter_refs[12:], BACK_TIMES)
+    scatter = Scatter(
+        me, (up_hbm, down_hbm, cross_hbm, self_grad_hbm, small_ref), (up_out, down_out, cross_out, self_out, small_out),
+        (up_buffers, down_buffers, cross_buffers, up_buffers, small_buffers), sems, BACK_TIMES, {3: 0})
     scatter.run_until(1)
 
     def to_mate(src, dst, k):
@@ -824,14 +815,39 @@
         for h in range(2):
             store(h, jnp.sum(turned[h * 64:(h + 1) * 64], 0, keepdims=True))
 
-    loads[1].wait()
-    grad_mixed = dot(gac_ref[...].astype(jnp.bfloat16), cross_vm[1], NT).astype(jnp.bfloat16)
+    def tile_store(grad_hbm, slot, t):
+        return pltpu.make_async_copy(tile_ref.at[slot], grad_hbm.at[:, :, :, :, columns(t, 256)], tile_sem.at[slot])
+
+    def weight_tiles(grad_hbm, first_tile, count, tile, before=None):
+        def turn(t, carry):
+            slot = t % 2
+
+            @pl.when(t >= 2)
+            def _():
+                tile_store(grad_hbm, slot, first_tile + t - 2).wait()
+
+            value = tile(columns(t, 256))
+            tile_ref[slot] = value.reshape(4, 4, 2, width // 32, 256).astype(low)
+            tile_store(grad_hbm, slot, first_tile + t).start()
+            return carry
+
+        lax.fori_loop(0, count, turn, 0)
+        for t in range(max(0, count - 2), count):
+            tile_store(grad_hbm, t % 2, first_tile + t).wait()
+
+    def product_tiles(grad_hbm, first_tile, left, right_ref):
+        turned = left.T
+        weight_tiles(grad_hbm, first_tile, right_ref.shape[1] // 256, lambda cols: dot(turned, right_ref[:, cols], NN))
+
+    halves[1].wait()
+    grad_cross = gac_ref[...].astype(low)
+    grad_mixed = dot(grad_cross, cross_vm[1], NT).astype(low)
     row_grad_ref[my_rows] = grad_mixed
     grad_copy = to_mate(row_grad_ref.at[my_rows], row_grad_ref.at[my_rows], 0)
     grad_copy.start()
     for j in range(6):
         cols = slice(j * 128, (j + 1) * 128)
-        product = grad_mixed[:, cols].astype(jnp.float32) * mixed_ref[:, cols]
+        product = grad_mixed[:, cols].astype(full) * mixed_ref[:, cols]
         row_stat_ref[j, 0:2, my_cols] = cross_lse_ref[j]
 
         def keep(h, row, j=j):
@@ -840,77 +856,105 @@
         head_rows(product, keep)
     stat_copy = to_mate(row_stat_ref.at[:, :, my_cols], row_stat_ref.at[:, :, my_cols], 1)
     stat_copy.start()
-    loads[2].wait()
+    cq_ref[...] = grad_cross
+    product_tiles(cross_hbm, 9, mixed_ref[...].astype(low), cq_ref)
+    kv_load.wait()
     scatter.run_until(5)
     grad_copy.wait()
     stat_copy.wait()
 
-    def cross_pair(j):
-        def back(clip, keys_t, query, grad, lse, inner, h):
-            weights = jnp.exp(dot(kv_vm[clip, :, columns(j)], query, NT) - lse)
-            grad_v = dot(weights.astype(jnp.bfloat16), grad, NN)
-            grad_s = (weights * (dot(kv_vm[clip, :, columns(j + 6)], grad, NT) - inner)).astype(jnp.bfloat16)
-            return dot(keys_t[h * 64:(h + 1) * 64], grad_s, NN), dot(grad_s, query, NN), grad_v
-
-        for clip in range(3):
-            keys_t = kv_vm[clip, :, columns(j)].T
-            grads = []
+    def cross_pair(j, tick):
+        def back(clip, keys_t, query, grad, lse, inner):
+            weights = jnp.exp(dot(kv_vm[clip, :frames, columns(j)], query, NT) - lse)
+            grad_v = dot(weights.astype(low), grad, NN)
+            grad_s = (weights * (dot(kv_vm[clip, :frames, columns(j + 6)], grad, NT) - inner)).astype(low)
+            return dot(keys_t, grad_s, NN), dot(grad_s, query, NN), grad_v
+
+        keys_t = kv_vm[0, :frames, columns(j)].T
+        mine = seg_ref[...] == 0
+        grad_k = grad_v = None
+        for h in range(2):
+            tick(h)
+            query, grad = one_head(row_query_ref[:, columns(j)], h), one_head(row_grad_ref[:, columns(j)], h)
+            rows = slice(h * 64, (h + 1) * 64)
+            acc_ref[rows], part_k, part_v = back(
+                0, keys_t[rows], query, grad, jnp.where(mine, row_stat_ref[j, h:h + 1], 1e30),
+                row_stat_ref[j, 2 + h:3 + h])
+            grad_k = part_k if grad_k is None else grad_k + part_k
+            grad_v = part_v if grad_v is None else grad_v + part_v
+        kv_vm[0, :frames, columns(j)] = grad_k.astype(low)
+        kv_vm[0, :frames, columns(j + 6)] = grad_v.astype(low)
+        for clip in (1, 2):
+            tick(clip + 1)
+            in_first = group_ref[clip - 1:clip] == 0
+
+            def chosen(ref):
+                return two_heads(jnp.where(in_first, ref[:128, columns(j)], ref[384:, columns(j)]))
+
+            def chosen_row(row):
+                return jnp.where(in_first, row_stat_ref[j, row:row + 1, :128], row_stat_ref[j, row:row + 1, 384:])
+
+            mine = jnp.where(in_first, seg_ref[:, :128], seg_ref[:, 384:]) == clip
+            lse = jnp.concatenate([jnp.where(mine, chosen_row(h), 1e30) for h in range(2)], 1)
+            inner = jnp.concatenate([chosen_row(2 + h) for h in range(2)], 1)
+            grad_q, grad_k, grad_v = back(
+                clip, kv_vm[clip, :frames, columns(j)].T, chosen(row_query_ref), chosen(row_grad_ref), lse, inner)
             for h in range(2):
-                if clip == 0:
-                    query, grad = row_query_ref[:, columns(j)], row_grad_ref[:, columns(j)]
-                    mine = seg_ref[...] == 0
-                    lse, inner = row_stat_ref[j, h:h + 1], row_stat_ref[j, 2 + h:3 + h]
-                else:
-                    low = group_ref[clip - 1:clip] == 0
-
-                    def chosen(ref):
-                        return jnp.where(low, ref[:128, columns(j)], ref[384:, columns(j)])
-
-                    def chosen_row(row):
-                        return jnp.where(low, row_stat_ref[j, row:row + 1, :128], row_stat_ref[j, row:row + 1, 384:])
-
-                    query, grad = chosen(row_query_ref), chosen(row_grad_ref)
-                    mine = jnp.where(low, seg_ref[:, :128], seg_ref[:, 384:]) == clip
-                    lse, inner = chosen_row(h), chosen_row(2 + h)
-                grads.append(back(clip, keys_t, one_head(query, h), one_head(grad, h), jnp.where(mine, lse, 1e30),
-                                  inner, h))
-            grad_q, grad_k, grad_v = zip(*grads)
-            grad_q = jnp.concatenate(grad_q, 0)
-            if clip == 0:
-                acc_ref[...] = grad_q
-            else:
+                rows, part = slice(h * 64, (h + 1) * 64), slice(h * 128, (h + 1) * 128)
                 for spot in (0, 3):
                     cols = slice(spot * 128, (spot + 1) * 128)
-                    acc_ref[:, cols] += jnp.where(low == (spot == 0), grad_q, 0.0)
-            kv_vm[clip, :, columns(j)] = (grad_k[0] + grad_k[1]).astype(jnp.bfloat16)
-            kv_vm[clip, :, columns(j + 6)] = (grad_v[0] + grad_v[1]).astype(jnp.bfloat16)
+                    acc_ref[rows, cols] += jnp.where(in_first == (spot == 0), grad_q[rows, part], 0.0)
+            kv_vm[clip, :frames, columns(j)] = grad_k.astype(low)
+            kv_vm[clip, :frames, columns(j + 6)] = grad_v.astype(low)
         own_ref[:, columns(j)] = (acc_ref[:, my_cols] * 0.125).T
-        give_ref[:, columns(j)] = (acc_ref[:, columns(1 - core, toks)] * 0.125).T.astype(jnp.bfloat16)
-
-    loop_with(scatter, 6, 6, 4.7, cross_pair)
+        give_ref[:, columns(j)] = (acc_ref[:, columns(1 - core, toks)] * 0.125).T.astype(low)
+
+    loop_with(scatter, 6, 6, 4, cross_pair, (0, 0.33, 0.66, 0.83))
     query_copy = to_mate(give_ref.at[:, pl.ds(0, width)], take_query_ref, 2)
     query_copy.start()
     dkv_store = pltpu.make_async_copy(kv_vm, dkv_hbm, load_sem.at[2])
     dkv_store.start()
-    vec_grad_ref[...] = jnp.zeros_like(vec_grad_ref)
-    cv_bias = sum(jnp.sum(kv_vm[clip, :, width:].astype(jnp.float32), 0, keepdims=True) for clip in range(3))
-    vec_grad_ref[10:11] = cv_bias
-    loads[0].wait()
-    loads[3].wait()
-    scatter.run_until(35)
+    vec_grad_ref[...] = rows_ref[...]
+    vec_grad_ref[10:11] = sum(
+        jnp.sum(kv_vm[clip, :frames, width:].astype(full), 0, keepdims=True) for clip in range(clips))
+    for clip in range(clips):
+        copy = pltpu.make_async_copy(frames_hbm.at[clip], frame_ref, load_sem.at[3])
+        copy.start()
+        copy.wait()
+        turned_ref[clip] = frame_ref[...].T
+    scatter.run_until(37)
+
+    def frames_tile(cols):
+        total = dot(turned_ref[0], kv_vm[0, :frames, cols], NN)
+        for clip in range(1, clips):
+            total = total + dot(turned_ref[clip], kv_vm[clip, :frames, cols], NN)
+        return total
+
+    weight_tiles(cross_hbm, 3, 6, frames_tile)
+    halves[0].wait()
     query_copy.wait()
-    grad_query = (own_ref[:, :width] + take_query_ref[...].astype(jnp.float32)).astype(jnp.bfloat16)
+    grad_query = (own_ref[:, :width] + take_query_ref[...].astype(full)).astype(low)
     cq_ref[...] = grad_query
-    vec_grad_ref[9:10] = jnp.sum(grad_query.astype(jnp.float32), 0, keepdims=True)
+    product_tiles(cross_hbm, 0, normed_two_ref[...], cq_ref)
+    dkv_store.wait()
+    self_loads = [
+        pltpu.make_async_copy(
+            self_hbm.at[:, pl.ds(k * 2 * width, 2 * width)], kv_vm.at[k], load_sem.at[2 + k]) for k in range(2)
+    ]
+    for copy in self_loads:
+        copy.start()
+    scatter.run_until(46)
+    vec_grad_ref[9:10] = jnp.sum(grad_query.astype(full), 0, keepdims=True)
     grad_part, gain, shift = norm_rows_back(after_self_ref[...], vec_ref[2:3], dot(grad_query, cross_vm[0], NT))
     vec_grad_ref[2:3] = gain
     vec_grad_ref[3:4] = shift
     grad_after_self = gac_ref[...] + grad_part
     input_grad_ref[...] = grad_after_self
-    grad_low = grad_after_self.astype(jnp.bfloat16)
-    self_low_ref[...] = grad_low
-    vec_grad_ref[8:9] = jnp.sum(grad_low.astype(jnp.float32), 0, keepdims=True)
-    grad_attended = dot(grad_low, self_vm[:, 3 * width:], NT).astype(jnp.bfloat16)
+    grad_low = grad_after_self.astype(low)
+    vec_grad_ref[8:9] = jnp.sum(grad_low.astype(full), 0, keepdims=True)
+    for copy in self_loads:
+        copy.wait()
+    grad_attended = dot(grad_low, kv_vm[1, :width, width:], NT).astype(low)
     row_grad_ref[:toks] = grad_attended
     for j in range(6):
         cols = slice(j * 128, (j + 1) * 128)
@@ -918,9 +962,10 @@
         def keep_self(h, row, j=j):
             row_stat_ref[j, h:h + 1, :toks] = row
 
-        head_rows(grad_attended[:, cols].astype(jnp.float32) * attended_ref[:, cols], keep_self)
-
-    def self_pair(j):
+        head_rows(grad_attended[:, cols].astype(full) * attended_ref[:, cols], keep_self)
+
+    def self_pair(j, tick):
+        tick(0)
         cols, value_cols = columns(j), columns(j + 6)
         keys, values = kv_row_ref[:, cols], kv_row_ref[:, value_cols]
         keys_t = keys.T
@@ -929,64 +974,116 @@
         for h in range(2):
             query, grad = one_head(query_ref[:, cols], h), one_head(row_grad_ref[:toks, cols], h)
             weights = jnp.exp(dot(keys, query, NT) + bias_ref[...] - self_lse_ref[j, h:h + 1])
-            part = dot(weights.astype(jnp.bfloat16), grad, NN)
+            part = dot(weights.astype(low), grad, NN)
             grad_v = part if grad_v is None else grad_v + part
             inner = row_stat_ref[j, h:h + 1, :toks]
-            grad_s = (weights * (dot(values, grad, NT) - inner)).astype(jnp.bfloat16)
+            grad_s = (weights * (dot(values, grad, NT) - inner)).astype(low)
             part = dot(grad_s, query, NN)
             grad_k = part if grad_k is None else grad_k + part
             parts.append(dot(keys_t[h * 64:(h + 1) * 64], grad_s, NN))
-        qkv_ref[:, cols] = (jnp.concatenate(parts, 0) * 0.125).T.astype(jnp.bfloat16)
+        qkv_ref[:, cols] = (jnp.concatenate(parts, 0) * 0.125).T.astype(low)
         own_ref[:, cols] = grad_k[toks:]
         own_ref[:, value_cols] = grad_v[toks:]
-        give_ref[:, cols] = grad_k[:toks].astype(jnp.bfloat16)
-        give_ref[:, value_cols] = grad_v[:toks].astype(jnp.bfloat16)
-
-    loop_with(scatter, 6, 42, 1.3, self_pair)
+        give_ref[:, cols] = grad_k[:toks].astype(low)
+        give_ref[:, value_cols] = grad_v[:toks].astype(low)
+
+    loop_with(scatter, 6, 52, 1.4, self_pair)
     row_copy = to_mate(give_ref, take_ref, 3)
     row_copy.start()
-    scatter.run_until(51)
+    cq_ref[...] = grad_low
+    product_tiles(self_grad_hbm, 9, attended_ref[...].astype(low), cq_ref)
+    scatter.run_until(62)
     row_copy.wait()
-    qkv_ref[:, width:] = (own_ref[...] + take_ref[...].astype(jnp.float32)).astype(jnp.bfloat16)
-    sums = jnp.sum(qkv_ref[...].astype(jnp.float32), 0, keepdims=True)
+    qkv_ref[:, width:] = (own_ref[...] + take_ref[...].astype(full)).astype(low)
+    product_tiles(self_grad_hbm, 0, normed_one_ref[...], qkv_ref)
+    sums = jnp.sum(qkv_ref[...].astype(full), 0, keepdims=True)
     vec_grad_ref[6:7] = sums[:, :width]
     vec_grad_ref[7:8] = sums[:, 2 * width:]
-    grad_normed = dot(qkv_ref[...], self_vm[:, :3 * width], NT)
-    grad_part, gain, shift = norm_rows_back(x_ref[...].astype(jnp.float32), vec_ref[0:1], grad_normed)
+    grad_normed = dot(qkv_ref[:, :2 * width], kv_vm[0, :width], NT) + dot(
+        qkv_ref[:, 2 * width:], kv_vm[1, :width, :width], NT)
+    grad_part, gain, shift = norm_rows_back(x_ref[...].astype(full), vec_ref[0:1], grad_normed)
     vec_grad_ref[0:1] = gain
     vec_grad_ref[1:2] = shift
     input_grad_ref[...] += grad_part
+    kv_load = pltpu.make_async_copy(dkv_hbm, kv_vm, load_sem.at[2])
+    kv_load.start()
+    for k in range(2):
+        pltpu.make_async_copy(ckv_hbm.at[:, pl.ds(k * width, width)], cross_vm.at[k], load_sem.at[k]).start()
+    small_ref[...] = jnp.zeros_like(small_ref)
+    rows = vec_grad_ref[...]
+    for d in range(32):
+        place = (d // 8, d // 2 % 4, d % 2)
+        turned_rows = rows if d == 0 else pltpu.roll(rows, width - d * 24, 1)
+        small_ref[place] = turned_rows[:, :128]
+        small_ref[place + (slice(13, 14),)] = up_bias_ref[d:d + 1]
+    scatter.run_until(70)
+    for k in range(2):
+        pltpu.make_async_copy(ckv_hbm.at[:, pl.ds(k * width, width)], cross_vm.at[k], load_sem.at[k]).wait()
+    kv_load.wait()
+    tiles = width // 256
+
+    def encoder_store(slot, t):
+        return pltpu.make_async_copy(
+            stage_ref.at[slot], encoder_hbm.at[t // tiles, :, columns(t % tiles, 256)], stage_sem.at[slot])
+
+    def encoder_tile(t, tick):
+        tick(0)
+        clip, tile, slot = t // tiles, t % tiles, t % 2
+
+        @pl.when(t >= 2)
+        def _():
+            encoder_store(slot, t - 2).wait()
+
+        cols = columns(tile, 256)
+        stage_ref[slot] = dot(kv_vm[clip, :frames, :width], cross_vm[0, cols], NT) + dot(
+            kv_vm[clip, :frames, width:], cross_vm[1, cols], NT)
+        encoder_store(slot, t).start()
+
+    loop_with(scatter, clips * tiles, 71, 0.8, encoder_tile)
+    for t in range(clips * tiles - 2, clips * tiles):
+        encoder_store(t % 2, t).wait()
     scatter.finish()
-    dkv_store.wait()
 
 
 def fused_backward(group, x, bias, seg, vec, gac, mixed, cross_lse, row_query, after_self, attended, self_lse, query,
-                   kv_row, cqo_full, self_full, kv, grad_up, grad_down):
+                   kv_row, normed_one, normed_two, rows, up_bias, cqo_full, ckv_full, self_full, kv, frames, grad_up,
+                   grad_down):
     toks, width = x.shape
+    clips, count = frames.shape[:2]
     low, full = jnp.bfloat16, jnp.float32
     pairs = width // 128
     vmem, hbm = pl.BlockSpec(memory_space=pltpu.VMEM), pl.BlockSpec(memory_space=pl.ANY)
     shape = jax.ShapeDtypeStruct
+    small = shape((32, 16, 128), full)
+    wide = (4, 4, 2, width // 32, 4 * width)
     outs = [
-        (vmem, shape((toks, width), full)), (vmem, shape((toks, width), low)), (vmem, shape((toks, width), low)),
-        (vmem, shape((toks, 3 * width), low)), (vmem, shape((16, width), full)), (hbm, shape(kv.shape, low)),
-        (vmem, shape(grad_up.shape[1:], full)), (vmem, shape(grad_down.shape[1:], full)),
+        (vmem, shape((toks, width), full)), (hbm, shape(frames.shape, full)), (vmem, shape(grad_up.shape[1:], full)),
+        (vmem, shape(grad_down.shape[1:], full)), (vmem, shape(grad_up.shape[1:], full)),
+        (vmem, shape(grad_up.shape[1:], full)), (vmem, shape(small.shape[1:], full)), (hbm, shape(kv.shape, low)),
+        (hbm, shape(wide, low)), (hbm, shape(wide, low)),
     ]
     return pl.pallas_call(
         backward_kernel,
-        in_specs=[vmem] * 14 + [hbm] * 5,
+        in_specs=[vmem] * 18 + [hbm] * 7,
         out_specs=tuple(spec for spec, _ in outs),
         out_shape=tuple(s for _, s in outs),
-        scratch_shapes=scatter_scratch((grad_up, grad_down)) + [
-            pltpu.VMEM((2, width, width), low), pltpu.VMEM((width, 4 * width), low), pltpu.VMEM(kv.shape, low),
-            pltpu.VMEM((2 * toks, width), low), pltpu.VMEM((pairs, 4, 2 * toks), full),
-            pltpu.VMEM((128, 2 * toks), full), pltpu.VMEM((toks, 2 * width), full), pltpu.VMEM((toks, 2 * width), low),
-            pltpu.VMEM((toks, 2 * width), low), pltpu.VMEM((toks, width), low), pltpu.SemaphoreType.DMA((4,)), pltpu.SemaphoreType.DMA((2, 4)),
+        scratch_shapes=scatter_buffers(grad_up) + scatter_buffers(grad_down) + scatter_buffers(grad_up)
+        + scatter_buffers(small) + scatter_sems(5) + [
+            pltpu.VMEM((2, width, width), low), pltpu.VMEM((clips, width, 2 * width), low),
+            pltpu.VMEM((count, width), low), pltpu.VMEM((clips, width, count), low),
+            pltpu.VMEM((2,) + wide[:4] + (256,), low), pltpu.VMEM((2, count, 256), full),
+            pltpu.VMEM((4, 4, 2, 16, 128), full), pltpu.VMEM((2 * toks, width), low),
+            pltpu.VMEM((pairs, 4, 2 * toks), full), pltpu.VMEM((128, 2 * toks), full),
+            pltpu.VMEM((toks, 2 * width), full), pltpu.VMEM((toks, 2 * width), low),
+            pltpu.VMEM((toks, 2 * width), low), pltpu.VMEM((toks, width), low), pltpu.VMEM((toks, width), low),
+            pltpu.VMEM((toks, 3 * width), low), pltpu.VMEM((16, width), full), pltpu.SemaphoreType.DMA((4,)),
+            pltpu.SemaphoreType.DMA((2, 4)), pltpu.SemaphoreType.DMA((2,)), pltpu.SemaphoreType.DMA((2,)),
         ],
         compiler_params=pltpu.CompilerParams(collective_id=2, has_side_effects=True, vmem_limit_bytes=63 * 2**20),
         name="fused_backward",
     )(group, x, bias, seg, vec, gac, mixed, cross_lse, row_query, after_self, attended, self_lse, query, kv_row,
-      cqo_full, self_full, kv, scatter_view(grad_up), scatter_view(grad_down))
+      normed_one, normed_two, rows, up_bias, cqo_full, ckv_full, self_full, kv, frames, scatter_view(grad_up),
+      scatter_view(grad_down))
 
 
 def ffn_kernel(normed_ref, grad_ref, after_ref, vec_ref, up_ref, bias_ref, down_ref, out_ref, back_ref, grad_up_ref,
@@ -1075,106 +1172,6 @@
         name="place_clips",
     )(order, values)
     return flat.reshape(1, clips, frames, width)
-
-
-FINISH_TIMES = ((3, (0, 4, 6, 12, 22, 27, 32, 38)), (12, (0, 6, 8, 14, 26, 31, 36, 42)), (13, (0, 6, 8, 14, 26, 31, 36, 42)))
-
-
-def finish_kernel(*refs):
-    (normed_one_ref, qkv_ref, attended_ref, self_low_ref, normed_two_ref, cq_ref, mixed_ref, cross_low_ref, frames_ref,
-     dkv_ref, ckv_hbm, small_hbm) = refs[:12]
-    encoder_hbm, self_out, cross_out, small_out = refs[12:16]
-    scratch = refs[16:]
-    scatter_refs, scratch = scratch[:18], scratch[18:]
-    sems, (turned_ref, weight_ref, stage_ref, load_sem, store_sem) = scratch[:5], scratch[5:]
-    self_grad, cross_grad = scatter_refs[0], scatter_refs[6]
-    width = normed_one_ref.shape[1]
-    load = pltpu.make_async_copy(ckv_hbm, weight_ref, load_sem.at[0])
-    load.start()
-    me = Place()
-    me.greet()
-    scatter = Scatter(
-        me, (self_grad, cross_grad, small_hbm), (self_out, cross_out, small_out),
-        ((None,) + tuple(scatter_refs[1:6]), (None,) + tuple(scatter_refs[7:12]), tuple(scatter_refs[12:18])), sems,
-        FINISH_TIMES)
-
-    def store(grad, cols, value):
-        grad[..., cols] = value.reshape(4, 4, 2, 24, value.shape[1]).astype(jnp.bfloat16)
-
-    def weight_grad(grad, left_ref, right_ref, first_tile):
-        left = left_ref[...].T
-
-        def tile(t, carry):
-            store(grad, columns(first_tile + t, 256), dot(left, right_ref[:, columns(t, 256)], NN))
-            return carry
-
-        lax.fori_loop(0, right_ref.shape[1] // 256, tile, 0)
-
-    weight_grad(self_grad, normed_one_ref, qkv_ref, 0)
-    weight_grad(self_grad, attended_ref, self_low_ref, 9)
-    scatter.run_until(3)
-    weight_grad(cross_grad, normed_two_ref, cq_ref, 0)
-    weight_grad(cross_grad, mixed_ref, cross_low_ref, 9)
-    clips = frames_ref.shape[0]
-    for clip in range(clips):
-        turned_ref[clip] = frames_ref[clip].T
-    scatter.run_until(5)
-
-    def frames_tile(t):
-        cols = columns(t, 256)
-        total = dot(turned_ref[0], dkv_ref[0, :, cols], NN)
-        for clip in range(1, clips):
-            total = total + dot(turned_ref[clip], dkv_ref[clip, :, cols], NN)
-        store(cross_grad, columns(t + 3, 256), total)
-
-    loop_with(scatter, 6, 6, 1, frames_tile)
-    scatter.run_until(13)
-    load.wait()
-    stores = []
-    for clip in range(clips):
-        slot = clip % 2
-        if clip >= 2:
-            stores[clip - 2].wait()
-
-        def encoder_tile(t, clip=clip, slot=slot):
-            rows = columns(t, 256)
-            stage_ref[slot, :, rows] = dot(dkv_ref[clip], weight_ref[rows], NT)
-
-        loop_with(scatter, width // 256, 14 + 4 * clip, 1.3, encoder_tile)
-        stores.append(pltpu.make_async_copy(stage_ref.at[slot], encoder_hbm.at[clip], store_sem.at[slot]))
-        stores[clip].start()
-    scatter.finish()
-    for clip in range(max(0, clips - 2), clips):
-        stores[clip].wait()
-
-
-def fused_finish(normed_one, qkv, attended, self_low, normed_two, cq, mixed, cross_low, frames, dkv, ckv_full, small):
-    width = normed_one.shape[1]
-    clips, count = frames.shape[:2]
-    low, full = jnp.bfloat16, jnp.float32
-    vmem, hbm = pl.BlockSpec(memory_space=pltpu.VMEM), pl.BlockSpec(memory_space=pl.ANY)
-    shape = jax.ShapeDtypeStruct
-    large = shape((32, width // 32, 4 * width), low)
-    scratch = scatter_scratch((large, large, small))
-    for m in range(2):
-        scratch[6 * m] = pltpu.VMEM((4, 4, 2) + large.shape[1:], low)
-    outs = [
-        (hbm, shape(frames.shape, full)), (vmem, shape(large.shape[1:], full)), (vmem, shape(large.shape[1:], full)),
-        (vmem, shape(small.shape[1:], full)),
-    ]
-    return pl.pallas_call(
-        finish_kernel,
-        in_specs=[vmem] * 10 + [hbm] * 2,
-        out_specs=tuple(spec for spec, _ in outs),
-        out_shape=tuple(s for _, s in outs),
-        scratch_shapes=scratch + [
-            pltpu.VMEM((clips, width, count), low), pltpu.VMEM((width, 2 * width), low),
-            pltpu.VMEM((2, count, width), full), pltpu.SemaphoreType.DMA((1,)), pltpu.SemaphoreType.DMA((2,)),
-        ],
-        compiler_params=pltpu.CompilerParams(collective_id=1, has_side_effects=True, vmem_limit_bytes=63 * 2**20),
-        name="fused_finish",
-    )(normed_one, qkv, attended, self_low, normed_two, cq, mixed, cross_low, frames, dkv, ckv_full,
-      scatter_view(small))
 
 
 def from_behind(value, axis, steps):
@@ -1422,46 +1419,39 @@
         (self_weights, cross_weights, up_weights, down_weights, up_bias, down_bias, vectors),
     )
     bias_full = bias_full.astype(jnp.float32)
-    attended_low = attended.astype(jnp.bfloat16)
-    mixed = mixed_full.astype(jnp.bfloat16)
     layer_output, grad_after_cross, grad_up, grad_down, grad_up_bias, ffn_rows = ffn(
         normed_three, out_grad[0], after_cross, vec, up_full, bias_full[None], down_full
     )
-    grad_cross_low = grad_after_cross.astype(jnp.bfloat16)
-    grad_out_bias = ffn_rows[12]
     operands = (
         layer_input[0], mask_bias, row_segment, vec, grad_after_cross, mixed_full, cross_lse, row_query, after_self,
-        attended, self_lse, query, kv_row, cqo_full, self_full, cross_kv,
-    )
-    fused = lax.axis_size("dp") == 16
-    if fused:
+        attended, self_lse, query, kv_row,
+    )
+    if lax.axis_size("dp") == 16:
         group = jnp.broadcast_to(which[:, None], (2, 128))
         large = [g.reshape(32, -1, g.shape[1]) for g in (grad_up, grad_down)]
-        *results, up_share, down_share = fused_backward(group, *operands, *large)
-    else:
-        results = plain_backward(which, *operands)
-    input_grad, grad_query_sum, grad_self_low, grad_qkv_low, vec_grads, cross_kv_grad = results
-    vector_grads = (vec_grads + ffn_rows)[:12]
-    last_operands = (
-        normed_one, grad_qkv_low, attended_low, grad_self_low, normed_two, grad_query_sum, mixed, grad_cross_low, frames,
-        cross_kv_grad, ckv_full,
-    )
-    if fused:
-        blocks = jnp.pad(vector_grads.reshape(12, 32, -1).transpose(1, 0, 2), ((0, 0), (0, 0), (0, 104)))
-        ups = jnp.pad(grad_up_bias.reshape(32, 1, -1), ((0, 0), (0, 0), (0, 32)))
-        downs = jnp.pad(grad_out_bias.reshape(32, 1, -1), ((0, 0), (0, 0), (0, 104)))
-        small = jnp.concatenate([blocks, ups, downs, jnp.zeros((32, 2, 128), jnp.float32)], 1)
-        encoder_grad, self_share, cross_share, row = fused_finish(*last_operands, small)
+        bias_rows = jnp.pad(grad_up_bias.reshape(32, -1), ((0, 0), (0, 128 - up_bias.shape[0])))
+        input_grad, encoder_grad, up_share, down_share, cross_share, self_share, row, *_ = fused_backward(
+            group, *operands, normed_one, normed_two, ffn_rows, bias_rows, cqo_full, ckv_full, self_full, cross_kv, frames,
+            *large
+        )
         shares = (
-            self_share, cross_share, up_share, down_share, row[12, : up_bias.shape[0]], row[13, : down_bias.shape[0]],
+            self_share, cross_share, up_share, down_share, row[13, : up_bias.shape[0]], row[12, : down_bias.shape[0]],
             row[:12, : vectors.shape[0]].T,
         )
     else:
-        encoder_grad, large = plain_finish(*last_operands)
+        input_grad, grad_query_sum, grad_self_low, grad_qkv_low, vec_grads, cross_kv_grad = plain_backward(
+            which, *operands, cqo_full, self_full, cross_kv
+        )
+        encoder_grad, large = plain_finish(
+            normed_one, grad_qkv_low, attended.astype(jnp.bfloat16), grad_self_low, normed_two, grad_query_sum,
+            mixed_full.astype(jnp.bfloat16), grad_after_cross.astype(jnp.bfloat16), frames, cross_kv_grad, ckv_full,
+        )
+        vector_grads = vec_grads + ffn_rows
         shares = tuple(
             lax.psum_scatter(part, ("dp", "seq"), scatter_dimension=0, tiled=True)
             for part in large
-            + (grad_up.astype(jnp.float32), grad_down.astype(jnp.float32), grad_up_bias[0], grad_out_bias, vector_grads.T)
+            + (grad_up.astype(jnp.float32), grad_down.astype(jnp.float32), grad_up_bias[0], vector_grads[12],
+               vector_grads[:12].T)
         )
     return (layer_output[None], input_grad[None], place_clips(order, encoder_grad)) + shares
 

time: 331 us -> 302 us (0.912)
  Pallas kernels: 299 us -> 271 us
  other arithmetic: 12.8 us -> 9.05 us
    pallas_call x1, Pallas kernels: 126 us -> 112 us  [fused_forward(): pl.pallas_call(forward_kernel, in_specs=[vmem] * 5 + [hbm] + [vmem] * 3 +...]
    pallas_call x2 -> x1, Pallas kernels: 145 us -> 132 us  [fused_backward(): pl.pallas_call(backward_kernel, in_specs=[vmem] * 18 + [hbm] * 7, out_spe...]
    convert_element_type x3 -> x0, other arithmetic: 3.52 us -> none  [the longest x1 1.92 us: per_device(): attended_low = attended.astype(jnp.bfloat16)]
    unnamed x37 -> x27, local copies, waits for them, and re-layouts: 7.58 us -> 8.17 us
where the time goes in v1:
time: 302 us; the launch traced here: 301 us
  Pallas kernels  271 us (90%)
  local copies, waits for them, and re-layouts  18.5 us (6%)
  other arithmetic  9.05 us (3%)
    pallas_call x1, Pallas kernels, fused_backward(): pl.pallas_call(backward_kernel, in_specs=[vmem] * 18 + [hbm] * 7, out_spe...  132 us
    pallas_call x1, Pallas kernels, fused_forward(): pl.pallas_call(forward_kernel, in_specs=[vmem] * 5 + [hbm] + [vmem] * 3 +...  112 us
    pallas_call x1, Pallas kernels, ffn(): pl.pallas_call(ffn_kernel, grid=(hidden // size,), in_specs=[rows, rows,...  18 us
    pallas_call x1, Pallas kernels, place_clips(): pl.pallas_call(place_clips_kernel, grid_spec=pltpu.PrefetchScalarGridSpec...  9.26 us
    unnamed x27, local copies, waits for them, and re-layouts  8.17 us

profile of v1, /device:TPU:0, one launch (start us, length us, event | category | flops | bytes accessed | tf_op | source)
XLA Modules:
  0.0 301.0 jit_solution(6551863781238043276)
XLA Ops:
  0.6 0.8 reduce-window.8
  1.6 1.3 bitcast_reduce_fusion
  4.2 0.7 pad_add_fusion.1.order
  4.9 0.7 compare_select_fusion
  5.6 0.6 broadcast_in_dim.73.refs_0_
  6.3 0.1 convert_reduce_fusion.3
  6.4 1.4 fusion.6.refs_5_
  7.7 0.1 convert_reduce_fusion.1
  7.8 1.2 select_select_fusion
  9.1 1.1 and_select_fusion.refs_3_.refs_2_
  10.2 4.7 %gather_fusion = bf16[3,750,768]{2,1,0:T(8,128)(2,1)} fusion(bf16[3,750,768]{2,1,0:T(8,128)(2,1)} %bitcast.29, s32[1024]{0:T(1024)S(1)} %pad_clamp_fusion), kind=kCustom, calls=%fused_computation | custom fusion | bytes 6912012 | tf_op jit(solution)/shard_map/jit(_take)/gather | solution.py:1413
  14.8 112.4 %fused_forward.1 = (bf16[32,16,128]{2,1,0:T(8,128)(2,1)}, bf16[768,1536]{1,0:T(8,128)(2,1)}, bf16[768,3072]{1,0:T(8,128)(2,1)}, bf16[768,1536]{1,0:T(8,128)(2,1)...) custom-call(s32[2,128]{1,0:T(2,128)} %broadcast_in_dim.73.refs_0_, ...), custom_call_target="tpu_custom_call" | custom-call | tf_op jit(solution)/shard_map/fused_forward/pallas_call | solution.py:600
  127.2 0.9 convert_reduce_fusion
  128.2 1.1 copy-done
  129.3 1.0 copy-done.3
  130.3 0.8 copy-done.4
  131.1 18.0 %ffn.1 = (bf16[256,768]{1,0:T(8,128)(2,1)}, f32[256,768]{1,0:T(8,128)S(1)}, bf16[768,3072]{1,0:T(8,128)(2,1)}, bf16[3072,768]{1,0:T(8,128)(2,1)}, f32[1,3072]{1,0:T(1,128)S(1)}, /*index=5*/f32[16,768]{1,0:T(8,128)S(1)}) custom-call(bf16[256,768]{1,0:T(8,128)(2,1)S(1)} %copy-done.3, bf16[256,768]{1,0:T(8,128)(2,1)S(1)} %bitcast.25, f32[256,768]{1,0:T(8,128)S(1)} %copy-done, ...), custom_call_target="tpu_custom_call" | custom-call | tf_op jit(solution)/shard_map/ffn/pallas_call | solution.py:1137
  149.1 0.9 copy-done.1
  150.0 0.6 copy-done.5
  150.6 0.5 broadcast.130
  151.1 0.7 reduce.26
  151.9 0.6 pad.19.refs_17_
  152.5 131.9 %fused_backward.1 = (f32[256,768]{1,0:T(8,128)}, f32[3,750,768]{2,1,0:T(8,128)}, f32[24,3072]{1,0:T(8,128)}, f32[96,768]{1,0:T(8,128)}, f32[24,3072]{1,0:T(8,128...) custom-call(s32[2,128]{1,0:T(2,128)} %broadcast_in_dim.73.refs_0_, ...), custom_call_target="tpu_custom_call" | custom-call | tf_op jit(solution)/shard_map/fused_backward/pallas_call | solution.py:1065
  284.3 1.2 slice_bitcast_fusion.1
  285.5 1.2 slice_bitcast_fusion.2
  286.7 1.3 slice_bitcast_fusion
  288.0 9.3 %place_clips.1 = f32[13500,1,128]{2,1,0:T(1,128)} custom-call(s32[3]{0:T(128)S(1)} %pad_add_fusion.1.order, f32[3,750,768]{2,1,0:T(8,128)} %get-tuple-element.72.in_ref), custom_call_target="tpu_custom_call" | custom-call | tf_op jit(solution)/shard_map/place_clips/pallas_call | solution.py:1162
  297.3 0.9 copy.29
  298.2 0.7 copy.30
  298.9 0.7 copy.31
  299.6 0.7 copy.32
  300.3 0.7 copy.33
  (25 shorter events, 0.3 us)
Async XLA Ops:
  10.2 118.0 %copy-start.2 = (bf16[1,256,768]{2,1,0:T(8,128)(2,1)S(1)}, bf16[1,256,768]{2,1,0:T(8,128)(2,1)}, u32[]{:S(2)}) copy-start(bf16[1,256,768]{2,1,0:T(8,128)(2,1)} %param.14) | copy-start | bytes 1179652
  128.2 1.1 copy-start
  129.3 1.0 copy-start.3
  130.3 0.8 copy-start.4
  149.1 0.9 copy-start.1
  150.0 0.6 copy-start.5
  288.0 9.3 %copy-start.6 = (f32[256,768]{1,0:T(8,128)S(1)}, f32[256,768]{1,0:T(8,128)}, u32[]{:S(2)}) copy-start(f32[256,768]{1,0:T(8,128)} %get-tuple-element.71) | copy-start | bytes 2359300
  288.0 10.2 %copy-start.10 = (f32[24,3072]{1,0:T(8,128)S(1)}, f32[24,3072]{1,0:T(8,128)}, u32[]{:S(2)}) copy-start(f32[24,3072]{1,0:T(8,128)} %get-tuple-element.125) | copy-start | bytes 884740
  288.0 10.9 %copy-start.9 = (f32[24,3072]{1,0:T(8,128)S(1)}, f32[24,3072]{1,0:T(8,128)}, u32[]{:S(2)}) copy-start(f32[24,3072]{1,0:T(8,128)} %get-tuple-element.126) | copy-start | bytes 884740
  288.0 11.6 %copy-start.8 = (f32[24,3072]{1,0:T(8,128)S(1)}, f32[24,3072]{1,0:T(8,128)}, u32[]{:S(2)}) copy-start(f32[24,3072]{1,0:T(8,128)} %get-tuple-element.127) | copy-start | bytes 884740
  288.0 12.3 %copy-start.7 = (f32[96,768]{1,0:T(8,128)S(1)}, f32[96,768]{1,0:T(8,128)}, u32[]{:S(2)}) copy-start(f32[96,768]{1,0:T(8,128)} %get-tuple-element.128) | copy-start | bytes 884740

commit v2 on v1

--- a/solution.py
+++ b/solution.py
@@ -377,16 +377,24 @@
 
 
 def forward_kernel(*refs):
-    (group_ref, x_ref, frames_ref, bias_ref, seg_ref, small_in, self_in, cross_in, up_in, down_in) = refs[:10]
+    (length_ref, x_ref, vectors_in, up_bias_in, down_bias_in, self_in, cross_in, up_in, frames_hbm, down_in) = refs[:10]
     (small_out, ckv_out, self_out, cqo_out, up_out, down_out, kv_out, vec_ref, normed_one_ref, query_ref, kv_row_ref,
      attended_ref, self_lse_ref, after_self_ref, normed_two_ref, row_query_ref, cross_lse_ref, mixed_ref,
-     after_cross_ref, normed_three_ref) = refs[10:30]
-    (half_wide, half_narrow, pair_wide, pair_narrow, small_vm, ckv_vm, self_vm, cqo_vm, kv_vm, acc_ref, stat_ref, part_ref, part_stat_ref, give_ref,
-     give_stat_ref, take_ref, take_stat_ref, send_sem, recv_sem, own_sem, half_sems, mate_sems, load_sem) = refs[30:]
+     after_cross_ref, normed_three_ref, bias_ref, seg_ref, info_ref, ranked_hbm) = refs[10:34]
+    (frames_in, frames_ref, small_f32, small_in, half_wide, half_narrow, pair_wide, pair_narrow, small_vm, ckv_vm, self_vm, cqo_vm, kv_vm, acc_ref, stat_ref, part_ref, part_stat_ref, give_ref,
+     give_stat_ref, take_ref, take_stat_ref, send_sem, recv_sem, own_sem, half_sems, mate_sems, load_sem,
+     frame_sem) = refs[34:]
     me = Place()
     core = me.core
     width = x_ref.shape[1]
     toks = x_ref.shape[0]
+    frames_load = pltpu.make_async_copy(frames_hbm, frames_in, frame_sem.at[0])
+    frames_load.start()
+    small_f32[...] = jnp.zeros_like(small_f32)
+    small_f32[:12, :vectors_in.shape[1]] = vectors_in[...].astype(jnp.float32)
+    small_f32[12:13, :down_bias_in.shape[1]] = down_bias_in[...].astype(jnp.float32)
+    small_f32[13:14, :up_bias_in.shape[1]] = up_bias_in[...].astype(jnp.float32)
+    small_in[...] = small_f32[...].astype(jnp.bfloat16)
     me.greet()
 
     def to_mate(src, dst, k):
@@ -425,6 +433,39 @@
         copy.start()
         copy.wait()
 
+    lengths = [length_ref[0, clip] for clip in range(3)]
+    ends = [lengths[0], lengths[0] + lengths[1], lengths[0] + lengths[1] + lengths[2]]
+
+    def clip_at(position):
+        return sum((position >= end).astype(jnp.int32) for end in ends)
+
+    def number_row(value):
+        return jnp.zeros((1, width), jnp.int32) + value
+
+    length_rows = [number_row(length) for length in lengths]
+    big = jnp.where(length_rows[1] > length_rows[0], 1, 0)
+    big = jnp.where(length_rows[2] > jnp.maximum(length_rows[0], length_rows[1]), 2, big)
+    order = [big, jnp.where(big == 0, 1, 0), jnp.where(big == 2, 1, 2)]
+    info_ref[...] = jnp.zeros_like(info_ref)
+    for k in (1, 2):
+        info_ref[k - 1:k] = jnp.where(order[k] < big, 0, 3)
+    for clip in range(3):
+        info_ref[2 + clip:3 + clip] = jnp.where(order[0] == clip, 0, jnp.where(order[1] == clip, 1, 2))
+    group_ref = info_ref.at[:, pl.ds(0, 128)]
+    places = clip_at(lax.broadcasted_iota(jnp.int32, (1, 2 * toks), 1))
+    seg_ref[...] = jnp.where(
+        places == order[0][:, :2 * toks], 0,
+        jnp.where(places == order[1][:, :2 * toks], 1, jnp.where(places == order[2][:, :2 * toks], 2, 3)))
+    key_at = core * toks - toks + lax.broadcasted_iota(jnp.int32, bias_ref.shape, 0)
+    query_at = core * toks + lax.broadcasted_iota(jnp.int32, bias_ref.shape, 1)
+    allowed = (clip_at(key_at) == clip_at(query_at)) & (key_at <= query_at) & (key_at >= 0)
+    bias_ref[...] = jnp.where(allowed, 0.0, -1e30)
+    frames_load.wait()
+    for k in range(3):
+        frames_ref[k] = jnp.where(
+            order[k] == 0, frames_in[0], jnp.where(order[k] == 1, frames_in[1], frames_in[2]))
+    ranked_store = pltpu.make_async_copy(frames_ref, ranked_hbm, frame_sem.at[0])
+    ranked_store.start()
     gather.run_until(15)
     gather.need(0)
     fetch(small_out, small_vm, 0)
@@ -576,10 +617,11 @@
     gather.need(4)
     gather.need(5)
     kv_store.wait()
+    ranked_store.wait()
     gather.finish()
 
 
-def fused_forward(group, x, frames, bias, seg, small, self_w, cross_w, up_w, down_w):
+def fused_forward(lengths, x, vectors, up_bias, down_bias, self_w, cross_w, up_w, frames, down_w):
     toks, width = x.shape
     clips, count = frames.shape[:2]
     low, full = jnp.bfloat16, jnp.float32
@@ -596,14 +638,17 @@
         (vmem, shape((pairs, 2, toks), full)), (vmem, shape((toks, width), full)), (vmem, shape((toks, width), low)),
         (vmem, shape((2 * toks, width), low)), (vmem, shape((pairs, 2, toks), full)), (vmem, shape((toks, width), full)),
         (vmem, shape((toks, width), full)), (vmem, shape((toks, width), low)),
+        (vmem, shape((2 * toks, toks), full)), (vmem, shape((1, 2 * toks), jnp.int32)), (vmem, shape((8, width), jnp.int32)),
+        (hbm, shape(frames.shape, low)),
     ]
     return pl.pallas_call(
         forward_kernel,
-        in_specs=[vmem] * 5 + [hbm] + [vmem] * 3 + [hbm],
+        in_specs=[pl.BlockSpec(memory_space=pltpu.SMEM)] + [vmem] * 7 + [hbm] * 2,
         out_specs=tuple(spec for spec, _ in outs),
         out_shape=tuple(s for _, s in outs),
         scratch_shapes=[
-            pltpu.VMEM((2, 24, 2 * width), low), pltpu.VMEM((2, 24, width), low), pltpu.VMEM((2, 48, 2 * width), low),
+            pltpu.VMEM(frames.shape, low), pltpu.VMEM(frames.shape, low), pltpu.VMEM((16, 128), full),
+            pltpu.VMEM((16, 128), low), pltpu.VMEM((2, 24, 2 * width), low), pltpu.VMEM((2, 24, width), low), pltpu.VMEM((2, 48, 2 * width), low),
             pltpu.VMEM((2, 48, width), low), pltpu.VMEM((32, 16, 128), low),
             pltpu.VMEM((width, 2 * width), low), pltpu.VMEM((width, 4 * width), low), pltpu.VMEM((width, 2 * width), low),
             pltpu.VMEM((clips, width, 2 * width), low), pltpu.VMEM((128, 2 * toks), full), pltpu.VMEM((4, 2 * toks), full),
@@ -612,10 +657,11 @@
             pltpu.VMEM((pairs, 128, toks), low), pltpu.VMEM((pairs, 4, toks), full),
             pltpu.SemaphoreType.DMA((400,)), pltpu.SemaphoreType.DMA((6, 32)), pltpu.SemaphoreType.DMA((6,)),
             pltpu.SemaphoreType.DMA((2, 5)), pltpu.SemaphoreType.DMA((2, 4)), pltpu.SemaphoreType.DMA((2,)),
+            pltpu.SemaphoreType.DMA((1,)),
         ],
         compiler_params=pltpu.CompilerParams(collective_id=0, has_side_effects=True, vmem_limit_bytes=60 * 2**20),
         name="fused_forward",
-    )(group, x, frames, bias, seg, small, self_w, cross_w, up_w, down_w)
+    )(lengths, x, vectors, up_bias, down_bias, self_w, cross_w, up_w, frames, down_w)
 
 
 class Scatter:
@@ -755,9 +801,9 @@
 BACK_TIMES = (
     (0, 8, 9, 20, 32, 44),
     (1, 20, 21, 34, 46, 58),
-    (44, 54, 55, 68, 78, 88),
-    (80, 85, 86, 94, 102, 110),
-    (80.5, 86.0, 87.0, 95.0, 103.0, 111.5),
+    (44, 52, 53, 62, 68, 78),
+    (66, 71, 72, 80, 88, 97),
+    (70, 73, 74, 82, 89, 98),
 )
 
 
@@ -774,7 +820,7 @@
 
 
 def backward_kernel(*refs):
-    (group_ref, x_ref, bias_ref, seg_ref, vec_ref, gac_ref, mixed_ref, cross_lse_ref, row_query_ref, after_self_ref,
+    (info_ref, x_ref, bias_ref, seg_ref, vec_ref, gac_ref, mixed_ref, cross_lse_ref, row_query_ref, after_self_ref,
      attended_ref, self_lse_ref, query_ref, kv_row_ref, normed_one_ref, normed_two_ref, rows_ref, up_bias_ref, cqo_hbm,
      ckv_hbm, self_hbm, kv_hbm, frames_hbm, up_hbm, down_hbm) = refs[:25]
     (input_grad_ref, encoder_hbm, up_out, down_out, cross_out, self_out, small_out, dkv_hbm, cross_hbm,
@@ -785,6 +831,7 @@
     (cross_vm, kv_vm, frame_ref, turned_ref, tile_ref, stage_ref, small_ref, row_grad_ref, row_stat_ref, acc_ref,
      own_ref, give_ref, take_ref, take_query_ref, cq_ref, qkv_ref, vec_grad_ref, load_sem, mate_sems, tile_sem,
      stage_sem) = scratch
+    group_ref = info_ref.at[:, pl.ds(0, 128)]
     me = Place()
     core = me.core
     toks, width = x_ref.shape
@@ -918,10 +965,10 @@
     vec_grad_ref[10:11] = sum(
         jnp.sum(kv_vm[clip, :frames, width:].astype(full), 0, keepdims=True) for clip in range(clips))
     for clip in range(clips):
-        copy = pltpu.make_async_copy(frames_hbm.at[clip], frame_ref, load_sem.at[3])
+        copy = pltpu.make_async_copy(frames_hbm.at[clip], frame_ref.at[:, pl.ds(0, width)], load_sem.at[3])
         copy.start()
         copy.wait()
-        turned_ref[clip] = frame_ref[...].T
+        turned_ref[clip] = frame_ref[:, :width].T
     scatter.run_until(37)
 
     def frames_tile(cols):
@@ -996,6 +1043,7 @@
     row_copy.wait()
     qkv_ref[:, width:] = (own_ref[...] + take_ref[...].astype(full)).astype(low)
     product_tiles(self_grad_hbm, 0, normed_one_ref[...], qkv_ref)
+    scatter.run_until(66)
     sums = jnp.sum(qkv_ref[...].astype(full), 0, keepdims=True)
     vec_grad_ref[6:7] = sums[:, :width]
     vec_grad_ref[7:8] = sums[:, 2 * width:]
@@ -1020,32 +1068,35 @@
     for k in range(2):
         pltpu.make_async_copy(ckv_hbm.at[:, pl.ds(k * width, width)], cross_vm.at[k], load_sem.at[k]).wait()
     kv_load.wait()
-    tiles = width // 256
-
-    def encoder_store(slot, t):
-        return pltpu.make_async_copy(
-            stage_ref.at[slot], encoder_hbm.at[t // tiles, :, columns(t % tiles, 256)], stage_sem.at[slot])
-
-    def encoder_tile(t, tick):
-        tick(0)
-        clip, tile, slot = t // tiles, t % tiles, t % 2
-
-        @pl.when(t >= 2)
-        def _():
-            encoder_store(slot, t - 2).wait()
-
-        cols = columns(tile, 256)
-        stage_ref[slot] = dot(kv_vm[clip, :frames, :width], cross_vm[0, cols], NT) + dot(
-            kv_vm[clip, :frames, width:], cross_vm[1, cols], NT)
-        encoder_store(slot, t).start()
-
-    loop_with(scatter, clips * tiles, 71, 0.8, encoder_tile)
-    for t in range(clips * tiles - 2, clips * tiles):
-        encoder_store(t % 2, t).wait()
+    blocks = width // 128
+
+    def encoder_store(clip):
+        rows = pl.ds(clip * frames * blocks, frames * blocks)
+        return pltpu.make_async_copy(stage_ref, encoder_hbm.at[rows], stage_sem.at[0])
+
+    for clip in range(clips):
+        place = info_ref[2 + clip:3 + clip]
+        for part in (slice(0, width), slice(width, 2 * width)):
+            frame_ref[:, part] = jnp.where(
+                place == 0, kv_vm[0, :frames, part],
+                jnp.where(place == 1, kv_vm[1, :frames, part], kv_vm[2, :frames, part]))
+
+        def encoder_tile(t, tick, clip=clip):
+            tick(0)
+            rows = columns(t, 256)
+            value = dot(frame_ref[:, :width], cross_vm[0, rows], NT) + dot(frame_ref[:, width:], cross_vm[1, rows], NT)
+            if clip > 0:
+                pl.when(t == 0)(encoder_store(clip - 1).wait)
+            for k in range(2):
+                stage_ref[pl.ds(2 * t + k, frames, stride=blocks), 0] = value[:, k * 128:(k + 1) * 128]
+
+        loop_with(scatter, width // 256, 71 + 3 * clip, 1, encoder_tile)
+        encoder_store(clip).start()
+    encoder_store(clips - 1).wait()
     scatter.finish()
 
 
-def fused_backward(group, x, bias, seg, vec, gac, mixed, cross_lse, row_query, after_self, attended, self_lse, query,
+def fused_backward(info, x, bias, seg, vec, gac, mixed, cross_lse, row_query, after_self, attended, self_lse, query,
                    kv_row, normed_one, normed_two, rows, up_bias, cqo_full, ckv_full, self_full, kv, frames, grad_up,
                    grad_down):
     toks, width = x.shape
@@ -1057,7 +1108,7 @@
     small = shape((32, 16, 128), full)
     wide = (4, 4, 2, width // 32, 4 * width)
     outs = [
-        (vmem, shape((toks, width), full)), (hbm, shape(frames.shape, full)), (vmem, shape(grad_up.shape[1:], full)),
+        (vmem, shape((toks, width), full)), (hbm, shape((clips * count * width // 128, 1, 128), full)), (vmem, shape(grad_up.shape[1:], full)),
         (vmem, shape(grad_down.shape[1:], full)), (vmem, shape(grad_up.shape[1:], full)),
         (vmem, shape(grad_up.shape[1:], full)), (vmem, shape(small.shape[1:], full)), (hbm, shape(kv.shape, low)),
         (hbm, shape(wide, low)), (hbm, shape(wide, low)),
@@ -1070,18 +1121,18 @@
         scratch_shapes=scatter_buffers(grad_up) + scatter_buffers(grad_down) + scatter_buffers(grad_up)
         + scatter_buffers(small) + scatter_sems(5) + [
             pltpu.VMEM((2, width, width), low), pltpu.VMEM((clips, width, 2 * width), low),
-            pltpu.VMEM((count, width), low), pltpu.VMEM((clips, width, count), low),
-            pltpu.VMEM((2,) + wide[:4] + (256,), low), pltpu.VMEM((2, count, 256), full),
+            pltpu.VMEM((count, 2 * width), low), pltpu.VMEM((clips, width, count), low),
+            pltpu.VMEM((2,) + wide[:4] + (256,), low), pltpu.VMEM((count * width // 128, 1, 128), full),
             pltpu.VMEM((4, 4, 2, 16, 128), full), pltpu.VMEM((2 * toks, width), low),
             pltpu.VMEM((pairs, 4, 2 * toks), full), pltpu.VMEM((128, 2 * toks), full),
             pltpu.VMEM((toks, 2 * width), full), pltpu.VMEM((toks, 2 * width), low),
             pltpu.VMEM((toks, 2 * width), low), pltpu.VMEM((toks, width), low), pltpu.VMEM((toks, width), low),
             pltpu.VMEM((toks, 3 * width), low), pltpu.VMEM((16, width), full), pltpu.SemaphoreType.DMA((4,)),
-            pltpu.SemaphoreType.DMA((2, 4)), pltpu.SemaphoreType.DMA((2,)), pltpu.SemaphoreType.DMA((2,)),
+            pltpu.SemaphoreType.DMA((2, 4)), pltpu.SemaphoreType.DMA((2,)), pltpu.SemaphoreType.DMA((1,)),
         ],
         compiler_params=pltpu.CompilerParams(collective_id=2, has_side_effects=True, vmem_limit_bytes=63 * 2**20),
         name="fused_backward",
-    )(group, x, bias, seg, vec, gac, mixed, cross_lse, row_query, after_self, attended, self_lse, query, kv_row,
+    )(info, x, bias, seg, vec, gac, mixed, cross_lse, row_query, after_self, attended, self_lse, query, kv_row,
       normed_one, normed_two, rows, up_bias, cqo_full, ckv_full, self_full, kv, frames, scatter_view(grad_up),
       scatter_view(grad_down))
 
@@ -1274,25 +1325,6 @@
     )
 
 
-def forward(which, layer_input, frames, mask_bias, row_segment, weights):
-    if lax.axis_size("dp") != 16:
-        return plain_forward(which, layer_input, frames, mask_bias, row_segment, weights)
-    self_weights, cross_weights, up_weights, down_weights, up_bias, down_bias, vectors = weights
-
-    def as_row(values):
-        return jnp.pad(values, ((0, 0), (0, 128 - values.shape[1])))
-
-    small = jnp.concatenate(
-        [as_row(vectors.T), as_row(down_bias[None]), as_row(up_bias[None]), jnp.zeros((2, 128), vectors.dtype)]
-    )
-    group = jnp.broadcast_to(which[:, None], (2, 128))
-    whole = fused_forward(
-        group, layer_input, frames, mask_bias, row_segment, small, self_weights, cross_weights, up_weights,
-        down_weights,
-    )
-    return (whole[0][:, 13, : up_bias.shape[0]].reshape(-1),) + tuple(whole[1:])
-
-
 def plain_backward(
     which, layer_input, mask_bias, row_segment, vec, grad_after_cross, mixed_full, cross_lse, row_query, after_self,
     attended, self_lse, query, kv_row, cqo_full, self_full, cross_kv
@@ -1370,7 +1402,43 @@
     return encoder_grad, (grads_self, grads_cross)
 
 
-def per_device(
+def fused_device(
+    layer_input,
+    encoder_states,
+    clip_lengths,
+    out_grad,
+    self_weights,
+    cross_weights,
+    up_weights,
+    down_weights,
+    up_bias,
+    down_bias,
+    vectors,
+):
+    small_blocks, ckv_full, self_full, cqo_full, up_full, down_full, cross_kv, vec, normed_one, query, kv_row, attended, \
+        self_lse, after_self, normed_two, row_query, cross_lse, mixed_full, after_cross, normed_three, mask_bias, \
+        row_segment, info, frames = fused_forward(
+            clip_lengths, layer_input[0], vectors.T, up_bias[None], down_bias[None], self_weights, cross_weights, up_weights,
+            encoder_states[0], down_weights,
+        )
+    bias_full = small_blocks[:, 13, : up_bias.shape[0]].reshape(-1).astype(jnp.float32)
+    layer_output, grad_after_cross, grad_up, grad_down, grad_up_bias, ffn_rows = ffn(
+        normed_three, out_grad[0], after_cross, vec, up_full, bias_full[None], down_full
+    )
+    large = [g.reshape(32, -1, g.shape[1]) for g in (grad_up, grad_down)]
+    bias_rows = jnp.pad(grad_up_bias.reshape(32, -1), ((0, 0), (0, 128 - up_bias.shape[0])))
+    input_grad, encoder_grad, up_share, down_share, cross_share, self_share, row, *_ = fused_backward(
+        info, layer_input[0], mask_bias, row_segment, vec, grad_after_cross, mixed_full, cross_lse, row_query, after_self,
+        attended, self_lse, query, kv_row, normed_one, normed_two, ffn_rows, bias_rows, cqo_full, ckv_full, self_full,
+        cross_kv, frames, *large
+    )
+    return (
+        layer_output[None], input_grad[None], encoder_grad.reshape((1,) + encoder_states.shape[1:]), self_share, cross_share,
+        up_share, down_share, row[13, : up_bias.shape[0]], row[12, : down_bias.shape[0]], row[:12, : vectors.shape[0]].T,
+    )
+
+
+def plain_device(
     layer_input,
     encoder_states,
     clip_lengths,
@@ -1386,7 +1454,6 @@
     model_width = layer_input.shape[2]
     tok_span = layer_input.shape[1]
     seq_half = lax.axis_index("seq")
-    source = layer_input[0].astype(jnp.float32)
     position = seq_half * tok_span + jnp.arange(tok_span, dtype=jnp.int32)
     clip_ends = jnp.cumsum(clip_lengths[0])
     segment = jnp.sum((position[:, None] >= clip_ends[None, :]).astype(jnp.int32), 1)
@@ -1414,7 +1481,7 @@
     (
         bias_full, ckv_full, self_full, cqo_full, up_full, down_full, cross_kv, vec, normed_one, query, kv_row, attended,
         self_lse, after_self, normed_two, row_query, cross_lse, mixed_full, after_cross, normed_three,
-    ) = forward(
+    ) = plain_forward(
         which, layer_input[0], frames, mask_bias, row_segment,
         (self_weights, cross_weights, up_weights, down_weights, up_bias, down_bias, vectors),
     )
@@ -1426,39 +1493,26 @@
         layer_input[0], mask_bias, row_segment, vec, grad_after_cross, mixed_full, cross_lse, row_query, after_self,
         attended, self_lse, query, kv_row,
     )
-    if lax.axis_size("dp") == 16:
-        group = jnp.broadcast_to(which[:, None], (2, 128))
-        large = [g.reshape(32, -1, g.shape[1]) for g in (grad_up, grad_down)]
-        bias_rows = jnp.pad(grad_up_bias.reshape(32, -1), ((0, 0), (0, 128 - up_bias.shape[0])))
-        input_grad, encoder_grad, up_share, down_share, cross_share, self_share, row, *_ = fused_backward(
-            group, *operands, normed_one, normed_two, ffn_rows, bias_rows, cqo_full, ckv_full, self_full, cross_kv, frames,
-            *large
-        )
-        shares = (
-            self_share, cross_share, up_share, down_share, row[13, : up_bias.shape[0]], row[12, : down_bias.shape[0]],
-            row[:12, : vectors.shape[0]].T,
-        )
-    else:
-        input_grad, grad_query_sum, grad_self_low, grad_qkv_low, vec_grads, cross_kv_grad = plain_backward(
-            which, *operands, cqo_full, self_full, cross_kv
-        )
-        encoder_grad, large = plain_finish(
-            normed_one, grad_qkv_low, attended.astype(jnp.bfloat16), grad_self_low, normed_two, grad_query_sum,
-            mixed_full.astype(jnp.bfloat16), grad_after_cross.astype(jnp.bfloat16), frames, cross_kv_grad, ckv_full,
-        )
-        vector_grads = vec_grads + ffn_rows
-        shares = tuple(
-            lax.psum_scatter(part, ("dp", "seq"), scatter_dimension=0, tiled=True)
-            for part in large
-            + (grad_up.astype(jnp.float32), grad_down.astype(jnp.float32), grad_up_bias[0], vector_grads[12],
-               vector_grads[:12].T)
-        )
+    input_grad, grad_query_sum, grad_self_low, grad_qkv_low, vec_grads, cross_kv_grad = plain_backward(
+        which, *operands, cqo_full, self_full, cross_kv
+    )
+    encoder_grad, large = plain_finish(
+        normed_one, grad_qkv_low, attended.astype(jnp.bfloat16), grad_self_low, normed_two, grad_query_sum,
+        mixed_full.astype(jnp.bfloat16), grad_after_cross.astype(jnp.bfloat16), frames, cross_kv_grad, ckv_full,
+    )
+    vector_grads = vec_grads + ffn_rows
+    shares = tuple(
+        lax.psum_scatter(part, ("dp", "seq"), scatter_dimension=0, tiled=True)
+        for part in large
+        + (grad_up.astype(jnp.float32), grad_down.astype(jnp.float32), grad_up_bias[0], vector_grads[12],
+           vector_grads[:12].T)
+    )
     return (layer_output[None], input_grad[None], place_clips(order, encoder_grad)) + shares
 
 
 def solution(mesh):
     return jax.shard_map(
-        per_device,
+        fused_device if mesh.shape["dp"] == 16 else plain_device,
         mesh=mesh,
         in_specs=(
             P("dp", "seq", None),

time: 302 us -> 277 us (0.917)
  Pallas kernels: 271 us -> 252 us
  other arithmetic: 9.05 us -> 1.57 us
    pallas_call x2 -> x1, Pallas kernels: 122 us -> 112 us  [fused_forward(): pl.pallas_call(forward_kernel, in_specs=[pl.BlockSpec(memory_space=pltpu....]
    pallas_call x1, Pallas kernels: 132 us -> 122 us  [fused_backward(): pl.pallas_call(backward_kernel, in_specs=[vmem] * 18 + [hbm] * 7, out_spe...]
    unnamed x27 -> x26, local copies, waits for them, and re-layouts: 8.17 us -> 16.6 us
    gather x1 -> x0, local copies, waits for them, and re-layouts: 4.65 us -> none  [per_device(): frames = jnp.take(encoder_states[0], order, axis=0, mode='clip')]
    select_n x3 -> x0, other arithmetic: 3.04 us -> none  [the longest x1 1.23 us: per_device(): jnp.where(row_segment == order[0], 0, jnp.where(row_segment == order[1],...]
where the time goes in v2:
time: 277 us; the launch traced here: 276 us
  Pallas kernels  252 us (91%)
  local copies, waits for them, and re-layouts  21.5 us (8%)
    pallas_call x1, Pallas kernels, fused_backward(): pl.pallas_call(backward_kernel, in_specs=[vmem] * 18 + [hbm] * 7, out_spe...  122 us
    pallas_call x1, Pallas kernels, fused_forward(): pl.pallas_call(forward_kernel, in_specs=[pl.BlockSpec(memory_space=pltpu....  112 us
    pallas_call x1, Pallas kernels, ffn(): pl.pallas_call(ffn_kernel, grid=(hidden // size,), in_specs=[rows, rows,...  17.9 us
    unnamed x26, local copies, waits for them, and re-layouts  16.6 us

profile of v2, /device:TPU:0, one launch (start us, length us, event | category | flops | bytes accessed | tf_op | source)
XLA Modules:
  0.0 275.8 jit_solution(17338770371895345995)
XLA Ops:
  0.6 0.0 copy-start.2
  0.7 111.6 %fused_forward.1 = (bf16[32,16,128]{2,1,0:T(8,128)(2,1)}, bf16[768,1536]{1,0:T(8,128)(2,1)}, bf16[768,3072]{1,0:T(8,128)(2,1)}, bf16[768,1536]{1,0:T(8,128)(2,1)...) custom-call(s32[1,3]{1,0:T(1,128)} %refs_0_.1, ...), custom_call_target="tpu_custom_call" | custom-call | tf_op jit(solution)/shard_map/fused_forward/pallas_call | solution.py:644
  112.2 0.9 convert_reduce_fusion
  113.1 0.1 reshape.40.bias_ref
  113.2 0.0 copy-done.2
  113.2 0.0 copy-start
  113.2 1.1 copy-done
  114.4 0.0 copy-start.3
  114.4 1.0 copy-done.3
  115.4 0.0 copy-start.4
  115.4 0.8 copy-done.4
  116.2 17.9 %ffn.1 = (bf16[256,768]{1,0:T(8,128)(2,1)}, f32[256,768]{1,0:T(8,128)S(1)}, bf16[768,3072]{1,0:T(8,128)(2,1)}, bf16[3072,768]{1,0:T(8,128)(2,1)}, f32[1,3072]{1,0:T(1,128)S(1)}, /*index=5*/f32[16,768]{1,0:T(8,128)S(1)}) custom-call(bf16[256,768]{1,0:T(8,128)(2,1)S(1)} %copy-done.3, bf16[256,768]{1,0:T(8,128)(2,1)S(1)} %bitcast.17, f32[256,768]{1,0:T(8,128)S(1)} %copy-done, ...), custom_call_target="tpu_custom_call" | custom-call | tf_op jit(solution)/shard_map/ffn/pallas_call | solution.py:1188
  134.1 0.9 copy-done.1
  134.9 0.6 copy-done.5
  135.6 0.5 broadcast.8
  136.1 0.7 reduce.7
  136.8 0.1 reshape.38
  136.8 0.6 pad.4.refs_17_
  137.4 122.5 %fused_backward.1 = (f32[256,768]{1,0:T(8,128)}, f32[13500,1,128]{2,1,0:T(1,128)}, f32[24,3072]{1,0:T(8,128)}, f32[96,768]{1,0:T(8,128)}, f32[24,3072]{1,0:T(8,1...) custom-call(s32[8,768]{1,0:T(8,128)} %get-tuple-element.54.refs_0_, ...), custom_call_target="tpu_custom_call" | custom-call | tf_op jit(solution)/shard_map/fused_backward/pallas_call | solution.py:1116
  259.9 1.2 slice_bitcast_fusion.1
  261.1 1.2 slice_bitcast_fusion.2
  262.3 1.3 slice_bitcast_fusion
  263.6 2.1 copy.29
  265.7 7.2 %copy.30 = f32[1,3,750,768]{3,0,2,1:T(1,128)} copy(f32[1,3,750,768]{3,0,2,1:T(1,128)} %bitcast.18) | data formatting | bytes 13824000
  272.9 0.0 copy-done.9
  272.9 0.7 copy.31
  273.6 0.0 copy-done.8
  273.6 0.7 copy.32
  274.3 0.0 copy-done.7
  274.3 0.7 copy.33
  275.0 0.0 copy-done.6
  275.0 0.7 copy.34
  (6 shorter events, 0.0 us)
Async XLA Ops:
  0.6 112.6 %copy-start.2 = (bf16[1,256,768]{2,1,0:T(8,128)(2,1)S(1)}, bf16[1,256,768]{2,1,0:T(8,128)(2,1)}, u32[]{:S(2)}) copy-start(bf16[1,256,768]{2,1,0:T(8,128)(2,1)} %param.14) | copy-start | bytes 1179652
  113.2 1.1 copy-start
  114.4 1.0 copy-start.3
  115.4 0.8 copy-start.4
  134.1 0.9 copy-start.1
  134.9 0.6 copy-start.5
  265.7 7.2 %copy-start.9 = (f32[24,3072]{1,0:T(8,128)S(1)}, f32[24,3072]{1,0:T(8,128)}, u32[]{:S(2)}) copy-start(f32[24,3072]{1,0:T(8,128)} %get-tuple-element.117) | copy-start | bytes 884740
  265.7 7.9 %copy-start.8 = (f32[24,3072]{1,0:T(8,128)S(1)}, f32[24,3072]{1,0:T(8,128)}, u32[]{:S(2)}) copy-start(f32[24,3072]{1,0:T(8,128)} %get-tuple-element.118) | copy-start | bytes 884740
  265.7 8.7 %copy-start.7 = (f32[24,3072]{1,0:T(8,128)S(1)}, f32[24,3072]{1,0:T(8,128)}, u32[]{:S(2)}) copy-start(f32[24,3072]{1,0:T(8,128)} %get-tuple-element.119) | copy-start | bytes 884740
  265.7 9.4 %copy-start.6 = (f32[96,768]{1,0:T(8,128)S(1)}, f32[96,768]{1,0:T(8,128)}, u32[]{:S(2)}) copy-start(f32[96,768]{1,0:T(8,128)} %get-tuple-element.120) | copy-start | bytes 884740

commit v3 on v2

--- a/solution.py
+++ b/solution.py
@@ -469,14 +469,12 @@
     gather.run_until(15)
     gather.need(0)
     fetch(small_out, small_vm, 0)
-    row = lax.broadcasted_iota(jnp.int32, (128, width), 0)
-    spot = lax.broadcasted_iota(jnp.int32, (128, width), 1) - row
-
-    def place_small(d, total):
-        chosen = jnp.where((spot == d * 24) & (row < 24), 1.0, 0.0).astype(jnp.bfloat16)
-        return total + dot(small_vm[d], chosen, NN)
-
-    vec_ref[...] = lax.fori_loop(0, 32, place_small, jnp.zeros(vec_ref.shape, jnp.float32))
+    total = jnp.zeros(vec_ref.shape, jnp.float32)
+    for d in range(32):
+        block = jnp.concatenate(
+            [small_vm[d].astype(jnp.float32), jnp.zeros((16, width - 128), jnp.float32)], 1)
+        total = total + (block if d == 0 else pltpu.roll(block, d * 24, 1))
+    vec_ref[...] = total
 
     def vec(k):
         return vec_ref[k:k + 1]
@@ -496,9 +494,8 @@
         shift = vec_ref[10:11, columns(tile % 3, 256)] * is_value
         kv_vm[clip, :frames_ref.shape[1], columns(tile, 256)] = (result + shift).astype(jnp.bfloat16)
 
-    loop_with(gather, clips * tiles, 20, 0.65, project)
-    kv_store = pltpu.make_async_copy(kv_vm, kv_out, load_sem.at[1])
-    kv_store.start()
+    early, middle = 9, 13
+    loop_with(gather, early, 20, 0.65, project)
     gather.run_until(31)
     gather.need(2)
     fetch(self_out, self_vm, 0)
@@ -511,6 +508,7 @@
     kv_copy.start()
     query = (dot(normed, self_vm[:, :width], NN) + vec(6)).astype(jnp.bfloat16)
     query_ref[...] = query * jnp.bfloat16(0.125)
+    lax.fori_loop(early, middle, lambda t, carry: (project(t, lambda k: None), carry)[1], 0)
     gather.run_until(35)
     kv_copy.wait()
 
@@ -542,6 +540,9 @@
     row_query_ref[my_rows] = cross_query * jnp.bfloat16(0.125)
     query_copy = to_mate(row_query_ref.at[my_rows], row_query_ref.at[my_rows], 1)
     query_copy.start()
+    lax.fori_loop(middle, clips * tiles, lambda t, carry: (project(t, lambda k: None), carry)[1], 0)
+    kv_store = pltpu.make_async_copy(kv_vm, kv_out, load_sem.at[1])
+    kv_store.start()
     gather.run_until(48)
     query_copy.wait()
 
@@ -801,8 +802,8 @@
 BACK_TIMES = (
     (0, 8, 9, 20, 32, 44),
     (1, 20, 21, 34, 46, 58),
-    (44, 52, 53, 62, 68, 78),
-    (66, 71, 72, 80, 88, 97),
+    (45, 53, 54, 63, 70, 80),
+    (66, 71, 72, 79, 86, 95),
     (70, 73, 74, 82, 89, 98),
 )
 
@@ -830,7 +831,7 @@
     sems, scratch = scratch[24:30], scratch[30:]
     (cross_vm, kv_vm, frame_ref, turned_ref, tile_ref, stage_ref, small_ref, row_grad_ref, row_stat_ref, acc_ref,
      own_ref, give_ref, take_ref, take_query_ref, cq_ref, qkv_ref, vec_grad_ref, load_sem, mate_sems, tile_sem,
-     stage_sem) = scratch
+     stage_sem, frame_sem) = scratch
     group_ref = info_ref.at[:, pl.ds(0, 128)]
     me = Place()
     core = me.core
@@ -841,12 +842,20 @@
     halves = [pltpu.make_async_copy(cqo_hbm.at[:, pl.ds(k * width, width)], cross_vm.at[k], load_sem.at[k])
               for k in range(2)]
     kv_load = pltpu.make_async_copy(kv_hbm, kv_vm, load_sem.at[2])
-    for copy in (halves[1], kv_load, halves[0]):
+    frame_loads = [
+        pltpu.make_async_copy(
+            frames_hbm.at[clip], frame_ref.at[:, pl.ds(clip % 2 * width, width)], frame_sem.at[clip % 2])
+        for clip in range(clips)
+    ]
+    for copy in [halves[1], kv_load, halves[0]] + frame_loads[:2]:
         copy.start()
     me.greet()
+    self_buffers = [
+        ref.at[(slice(None),) * (len(ref.shape) - 1) + (pl.ds(0, 3 * width),)] for ref in up_buffers
+    ]
     scatter = Scatter(
         me, (up_hbm, down_hbm, cross_hbm, self_grad_hbm, small_ref), (up_out, down_out, cross_out, self_out, small_out),
-        (up_buffers, down_buffers, cross_buffers, up_buffers, small_buffers), sems, BACK_TIMES, {3: 0})
+        (up_buffers, down_buffers, cross_buffers, self_buffers, small_buffers), sems, BACK_TIMES, {3: 0})
     scatter.run_until(1)
 
     def to_mate(src, dst, k):
@@ -905,6 +914,14 @@
     stat_copy.start()
     cq_ref[...] = grad_cross
     product_tiles(cross_hbm, 9, mixed_ref[...].astype(low), cq_ref)
+
+    def turn_frames(clip):
+        frame_loads[clip].wait()
+        turned_ref[clip] = frame_ref[:, clip % 2 * width:(clip % 2 + 1) * width].T
+
+    turn_frames(0)
+    frame_loads[2].start()
+    turn_frames(1)
     kv_load.wait()
     scatter.run_until(5)
     grad_copy.wait()
@@ -964,11 +981,7 @@
     vec_grad_ref[...] = rows_ref[...]
     vec_grad_ref[10:11] = sum(
         jnp.sum(kv_vm[clip, :frames, width:].astype(full), 0, keepdims=True) for clip in range(clips))
-    for clip in range(clips):
-        copy = pltpu.make_async_copy(frames_hbm.at[clip], frame_ref.at[:, pl.ds(0, width)], load_sem.at[3])
-        copy.start()
-        copy.wait()
-        turned_ref[clip] = frame_ref[:, :width].T
+    turn_frames(2)
     scatter.run_until(37)
 
     def frames_tile(cols):
@@ -990,7 +1003,6 @@
     ]
     for copy in self_loads:
         copy.start()
-    scatter.run_until(46)
     vec_grad_ref[9:10] = jnp.sum(grad_query.astype(full), 0, keepdims=True)
     grad_part, gain, shift = norm_rows_back(after_self_ref[...], vec_ref[2:3], dot(grad_query, cross_vm[0], NT))
     vec_grad_ref[2:3] = gain
@@ -999,6 +1011,9 @@
     input_grad_ref[...] = grad_after_self
     grad_low = grad_after_self.astype(low)
     vec_grad_ref[8:9] = jnp.sum(grad_low.astype(full), 0, keepdims=True)
+    cq_ref[...] = grad_low
+    product_tiles(cross_hbm, 12, attended_ref[...].astype(low), cq_ref)
+    scatter.run_until(46)
     for copy in self_loads:
         copy.wait()
     grad_attended = dot(grad_low, kv_vm[1, :width, width:], NT).astype(low)
@@ -1037,8 +1052,6 @@
     loop_with(scatter, 6, 52, 1.4, self_pair)
     row_copy = to_mate(give_ref, take_ref, 3)
     row_copy.start()
-    cq_ref[...] = grad_low
-    product_tiles(self_grad_hbm, 9, attended_ref[...].astype(low), cq_ref)
     scatter.run_until(62)
     row_copy.wait()
     qkv_ref[:, width:] = (own_ref[...] + take_ref[...].astype(full)).astype(low)
@@ -1106,29 +1119,31 @@
     vmem, hbm = pl.BlockSpec(memory_space=pltpu.VMEM), pl.BlockSpec(memory_space=pl.ANY)
     shape = jax.ShapeDtypeStruct
     small = shape((32, 16, 128), full)
-    wide = (4, 4, 2, width // 32, 4 * width)
+    places = (4, 4, 2, width // 32)
+    cross = shape((32, width // 32, 5 * width), low)
     outs = [
         (vmem, shape((toks, width), full)), (hbm, shape((clips * count * width // 128, 1, 128), full)), (vmem, shape(grad_up.shape[1:], full)),
-        (vmem, shape(grad_down.shape[1:], full)), (vmem, shape(grad_up.shape[1:], full)),
-        (vmem, shape(grad_up.shape[1:], full)), (vmem, shape(small.shape[1:], full)), (hbm, shape(kv.shape, low)),
-        (hbm, shape(wide, low)), (hbm, shape(wide, low)),
+        (vmem, shape(grad_down.shape[1:], full)), (vmem, shape(cross.shape[1:], full)),
+        (vmem, shape((width // 32, 3 * width), full)), (vmem, shape(small.shape[1:], full)), (hbm, shape(kv.shape, low)),
+        (hbm, shape(places + (5 * width,), low)), (hbm, shape(places + (3 * width,), low)),
     ]
     return pl.pallas_call(
         backward_kernel,
         in_specs=[vmem] * 18 + [hbm] * 7,
         out_specs=tuple(spec for spec, _ in outs),
         out_shape=tuple(s for _, s in outs),
-        scratch_shapes=scatter_buffers(grad_up) + scatter_buffers(grad_down) + scatter_buffers(grad_up)
+        scratch_shapes=scatter_buffers(grad_up) + scatter_buffers(grad_down) + scatter_buffers(cross)
         + scatter_buffers(small) + scatter_sems(5) + [
             pltpu.VMEM((2, width, width), low), pltpu.VMEM((clips, width, 2 * width), low),
             pltpu.VMEM((count, 2 * width), low), pltpu.VMEM((clips, width, count), low),
-            pltpu.VMEM((2,) + wide[:4] + (256,), low), pltpu.VMEM((count * width // 128, 1, 128), full),
+            pltpu.VMEM((2,) + places + (256,), low), pltpu.VMEM((count * width // 128, 1, 128), full),
             pltpu.VMEM((4, 4, 2, 16, 128), full), pltpu.VMEM((2 * toks, width), low),
             pltpu.VMEM((pairs, 4, 2 * toks), full), pltpu.VMEM((128, 2 * toks), full),
             pltpu.VMEM((toks, 2 * width), full), pltpu.VMEM((toks, 2 * width), low),
             pltpu.VMEM((toks, 2 * width), low), pltpu.VMEM((toks, width), low), pltpu.VMEM((toks, width), low),
             pltpu.VMEM((toks, 3 * width), low), pltpu.VMEM((16, width), full), pltpu.SemaphoreType.DMA((4,)),
             pltpu.SemaphoreType.DMA((2, 4)), pltpu.SemaphoreType.DMA((2,)), pltpu.SemaphoreType.DMA((1,)),
+            pltpu.SemaphoreType.DMA((2,)),
         ],
         compiler_params=pltpu.CompilerParams(collective_id=2, has_side_effects=True, vmem_limit_bytes=63 * 2**20),
         name="fused_backward",
@@ -1195,7 +1210,7 @@
             shape(down_full.shape, low), shape((1, hidden), full), shape((16, width), full),
         ],
         scratch_shapes=[pltpu.VMEM((width, toks), low), pltpu.VMEM((toks, width), full), pltpu.VMEM((toks, width), full)],
-        compiler_params=pltpu.CompilerParams(vmem_limit_bytes=48 * 2**20),
+        compiler_params=pltpu.CompilerParams(vmem_limit_bytes=63 * 2**20),
         name="ffn",
     )(normed, grad, after, vec, up_full, bias, down_full)
 
@@ -1432,6 +1447,9 @@
         attended, self_lse, query, kv_row, normed_one, normed_two, ffn_rows, bias_rows, cqo_full, ckv_full, self_full,
         cross_kv, frames, *large
     )
+    width = layer_input.shape[2]
+    self_share = jnp.concatenate([self_share, cross_share[:, 4 * width :]], 1)
+    cross_share = cross_share[:, : 4 * width]
     return (
         layer_output[None], input_grad[None], encoder_grad.reshape((1,) + encoder_states.shape[1:]), self_share, cross_share,
         up_share, down_share, row[13, : up_bias.shape[0]], row[12, : down_bias.shape[0]], row[:12, : vectors.shape[0]].T,

time: 277 us -> 265 us (0.957)
  Pallas kernels: 252 us -> 241 us
    pallas_call x1, Pallas kernels: 122 us -> 116 us  [fused_backward(): pl.pallas_call(backward_kernel, in_specs=[vmem] * 18 + [hbm] * 7, out_spe...]
    unnamed x26 -> x8, local copies, waits for them, and re-layouts: 16.6 us -> 10.7 us
    pallas_call x1, Pallas kernels: 112 us -> 106 us  [fused_forward(): pl.pallas_call(forward_kernel, in_specs=[pl.BlockSpec(memory_space=pltpu....]
where the time goes in v3:
time: 265 us; the launch traced here: 264 us
  Pallas kernels  241 us (91%)
  local copies, waits for them, and re-layouts  18.8 us (7%)
  other arithmetic  3.95 us (1%)
    pallas_call x1, Pallas kernels, fused_backward(): pl.pallas_call(backward_kernel, in_specs=[vmem] * 18 + [hbm] * 7, out_spe...  116 us
    pallas_call x1, Pallas kernels, fused_forward(): pl.pallas_call(forward_kernel, in_specs=[pl.BlockSpec(memory_space=pltpu....  106 us
    pallas_call x1, Pallas kernels, ffn(): pl.pallas_call(ffn_kernel, grid=(hidden // size,), in_specs=[rows, rows,...  18.8 us
    unnamed x8, local copies, waits for them, and re-layouts  10.7 us

profile of v3, /device:TPU:0, one launch (start us, length us, event | category | flops | bytes accessed | tf_op | source)
XLA Modules:
  0.0 264.5 jit_solution(1517495616159376185)
XLA Ops:
  0.6 105.8 %fused_forward.1 = (bf16[32,16,128]{2,1,0:T(8,128)(2,1)}, bf16[768,1536]{1,0:T(8,128)(2,1)}, bf16[768,3072]{1,0:T(8,128)(2,1)}, bf16[768,1536]{1,0:T(8,128)(2,1)...) custom-call(s32[1,3]{1,0:T(1,128)} %refs_0_.1, ...), custom_call_target="tpu_custom_call" | custom-call | tf_op jit(solution)/shard_map/fused_forward/pallas_call | solution.py:645
  106.5 0.9 convert_reduce_fusion
  107.4 0.7 reshape.40.bias_ref
  108.0 18.8 %ffn.1 = (bf16[256,768]{1,0:T(8,128)(2,1)}, f32[256,768]{1,0:T(8,128)}, bf16[768,3072]{1,0:T(8,128)(2,1)}, bf16[3072,768]{1,0:T(8,128)(2,1)}, f32[1,3072]{1,0:T(1,128)}, /*index=5*/f32[16,768]{1,0:T(8,128)}) custom-call(bf16[256,768]{1,0:T(8,128)(2,1)} %get-tuple-element.47.normed_ref, bf16[256,768]{1,0:T(8,128)(2,1)} %bitcast.24, ...), custom_call_target="tpu_custom_call" | custom-call | tf_op jit(solution)/shard_map/ffn/pallas_call | solution.py:1203
  126.9 0.5 broadcast.8
  127.4 1.4 reduce.7
  128.8 0.1 reshape.38
  128.8 0.6 pad.4.refs_17_
  129.4 116.4 %fused_backward.1 = (f32[256,768]{1,0:T(8,128)}, f32[13500,1,128]{2,1,0:T(1,128)}, f32[24,3072]{1,0:T(8,128)}, f32[96,768]{1,0:T(8,128)}, f32[24,3840]{1,0:T(8,1...) custom-call(s32[8,768]{1,0:T(8,128)} %get-tuple-element.54.refs_0_, ...), custom_call_target="tpu_custom_call" | custom-call | tf_op jit(solution)/shard_map/fused_backward/pallas_call | solution.py:1130
  245.8 1.2 slice_bitcast_fusion.1
  247.0 1.2 slice_bitcast_fusion.2
  248.2 1.3 slice_bitcast_fusion
  249.5 0.9 slice.19
  250.4 1.7 slice.20
  252.1 1.7 pad_maximum_fusion
  253.8 2.1 copy.27
  255.8 0.0 copy-start.1
  255.8 0.0 copy-start
  255.8 7.2 %copy.28 = f32[1,3,750,768]{3,0,2,1:T(1,128)} copy(f32[1,3,750,768]{3,0,2,1:T(1,128)} %bitcast.17) | data formatting | bytes 13824000
  263.0 0.0 copy-done.1
  263.0 0.7 copy.29
  263.7 0.0 copy-done
  263.7 0.7 copy.30
Async XLA Ops:
  255.8 7.2 %copy-start.1 = (f32[24,3072]{1,0:T(8,128)S(1)}, f32[24,3072]{1,0:T(8,128)}, u32[]{:S(2)}) copy-start(f32[24,3072]{1,0:T(8,128)} %get-tuple-element.119) | copy-start | bytes 884740
  255.8 7.9 %copy-start = (f32[96,768]{1,0:T(8,128)S(1)}, f32[96,768]{1,0:T(8,128)}, u32[]{:S(2)}) copy-start(f32[96,768]{1,0:T(8,128)} %get-tuple-element.120) | copy-start | bytes 884740

commit v4 on v3

--- a/solution.py
+++ b/solution.py
@@ -800,8 +800,8 @@
 
 
 BACK_TIMES = (
-    (0, 8, 9, 20, 32, 44),
-    (1, 20, 21, 34, 46, 58),
+    (0, 6.5, 8, 18, 30, 43),
+    (1, 17, 19, 32, 43.5, 60),
     (45, 53, 54, 63, 70, 80),
     (66, 71, 72, 79, 86, 95),
     (70, 73, 74, 82, 89, 98),
@@ -824,9 +824,9 @@
     (info_ref, x_ref, bias_ref, seg_ref, vec_ref, gac_ref, mixed_ref, cross_lse_ref, row_query_ref, after_self_ref,
      attended_ref, self_lse_ref, query_ref, kv_row_ref, normed_one_ref, normed_two_ref, rows_ref, up_bias_ref, cqo_hbm,
      ckv_hbm, self_hbm, kv_hbm, frames_hbm, up_hbm, down_hbm) = refs[:25]
-    (input_grad_ref, encoder_hbm, up_out, down_out, cross_out, self_out, small_out, dkv_hbm, cross_hbm,
-     self_grad_hbm) = refs[25:35]
-    scratch = refs[35:]
+    (input_grad_ref, encoder_hbm, up_out, down_out, cross_out, self_out, up_bias_out, down_bias_out, vectors_out,
+     dkv_hbm, cross_hbm, self_grad_hbm) = refs[25:37]
+    cross_sum, small_out, *scratch = refs[37:]
     up_buffers, down_buffers, cross_buffers, small_buffers = (scratch[k * 6:(k + 1) * 6] for k in range(4))
     sems, scratch = scratch[24:30], scratch[30:]
     (cross_vm, kv_vm, frame_ref, turned_ref, tile_ref, stage_ref, small_ref, row_grad_ref, row_stat_ref, acc_ref,
@@ -854,7 +854,7 @@
         ref.at[(slice(None),) * (len(ref.shape) - 1) + (pl.ds(0, 3 * width),)] for ref in up_buffers
     ]
     scatter = Scatter(
-        me, (up_hbm, down_hbm, cross_hbm, self_grad_hbm, small_ref), (up_out, down_out, cross_out, self_out, small_out),
+        me, (up_hbm, down_hbm, cross_hbm, self_grad_hbm, small_ref), (up_out, down_out, cross_sum, self_out.at[:, pl.ds(0, 3 * width)], small_out),
         (up_buffers, down_buffers, cross_buffers, self_buffers, small_buffers), sems, BACK_TIMES, {3: 0})
     scatter.run_until(1)
 
@@ -1076,7 +1076,8 @@
         place = (d // 8, d // 2 % 4, d % 2)
         turned_rows = rows if d == 0 else pltpu.roll(rows, width - d * 24, 1)
         small_ref[place] = turned_rows[:, :128]
-        small_ref[place + (slice(13, 14),)] = up_bias_ref[d:d + 1]
+        bias_row = up_bias_ref[...] if d == 0 else pltpu.roll(up_bias_ref[...], up_bias_ref.shape[1] * (32 - d) // 32, 1)
+        small_ref[place + (slice(13, 14),)] = bias_row[:, :128]
     scatter.run_until(70)
     for k in range(2):
         pltpu.make_async_copy(ckv_hbm.at[:, pl.ds(k * width, width)], cross_vm.at[k], load_sem.at[k]).wait()
@@ -1107,6 +1108,11 @@
         encoder_store(clip).start()
     encoder_store(clips - 1).wait()
     scatter.finish()
+    cross_out[...] = cross_sum[:, :4 * width]
+    self_out[:, 3 * width:] = cross_sum[:, 4 * width:]
+    up_bias_out[...] = small_out[13:14, :up_bias_out.shape[1]]
+    down_bias_out[...] = small_out[12:13, :down_bias_out.shape[1]]
+    vectors_out[...] = small_out[:12, :vectors_out.shape[1]]
 
 
 def fused_backward(info, x, bias, seg, vec, gac, mixed, cross_lse, row_query, after_self, attended, self_lse, query,
@@ -1123,8 +1129,9 @@
     cross = shape((32, width // 32, 5 * width), low)
     outs = [
         (vmem, shape((toks, width), full)), (hbm, shape((clips * count * width // 128, 1, 128), full)), (vmem, shape(grad_up.shape[1:], full)),
-        (vmem, shape(grad_down.shape[1:], full)), (vmem, shape(cross.shape[1:], full)),
-        (vmem, shape((width // 32, 3 * width), full)), (vmem, shape(small.shape[1:], full)), (hbm, shape(kv.shape, low)),
+        (vmem, shape(grad_down.shape[1:], full)), (vmem, shape((width // 32, 4 * width), full)),
+        (vmem, shape((width // 32, 4 * width), full)), (vmem, shape((1, up_bias.shape[1] // 32), full)),
+        (vmem, shape((1, width // 32), full)), (vmem, shape((12, width // 32), full)), (hbm, shape(kv.shape, low)),
         (hbm, shape(places + (5 * width,), low)), (hbm, shape(places + (3 * width,), low)),
     ]
     return pl.pallas_call(
@@ -1132,7 +1139,8 @@
         in_specs=[vmem] * 18 + [hbm] * 7,
         out_specs=tuple(spec for spec, _ in outs),
         out_shape=tuple(s for _, s in outs),
-        scratch_shapes=scatter_buffers(grad_up) + scatter_buffers(grad_down) + scatter_buffers(cross)
+        scratch_shapes=[pltpu.VMEM(cross.shape[1:], full), pltpu.VMEM(small.shape[1:], full)]
+        + scatter_buffers(grad_up) + scatter_buffers(grad_down) + scatter_buffers(cross)
         + scatter_buffers(small) + scatter_sems(5) + [
             pltpu.VMEM((2, width, width), low), pltpu.VMEM((clips, width, 2 * width), low),
             pltpu.VMEM((count, 2 * width), low), pltpu.VMEM((clips, width, count), low),
@@ -1192,7 +1200,7 @@
 def ffn(normed, grad, after, vec, up_full, bias, down_full):
     toks, width = normed.shape
     hidden = up_full.shape[1]
-    size = 256
+    size = 768
     low, full = jnp.bfloat16, jnp.float32
     shape = jax.ShapeDtypeStruct
     rows = pl.BlockSpec((toks, width), lambda t: (0, 0))
@@ -1441,18 +1449,14 @@
         normed_three, out_grad[0], after_cross, vec, up_full, bias_full[None], down_full
     )
     large = [g.reshape(32, -1, g.shape[1]) for g in (grad_up, grad_down)]
-    bias_rows = jnp.pad(grad_up_bias.reshape(32, -1), ((0, 0), (0, 128 - up_bias.shape[0])))
-    input_grad, encoder_grad, up_share, down_share, cross_share, self_share, row, *_ = fused_backward(
+    input_grad, encoder_grad, up_share, down_share, cross_share, self_share, up_row, down_row, vector_rows, *_ = fused_backward(
         info, layer_input[0], mask_bias, row_segment, vec, grad_after_cross, mixed_full, cross_lse, row_query, after_self,
-        attended, self_lse, query, kv_row, normed_one, normed_two, ffn_rows, bias_rows, cqo_full, ckv_full, self_full,
+        attended, self_lse, query, kv_row, normed_one, normed_two, ffn_rows, grad_up_bias, cqo_full, ckv_full, self_full,
         cross_kv, frames, *large
     )
-    width = layer_input.shape[2]
-    self_share = jnp.concatenate([self_share, cross_share[:, 4 * width :]], 1)
-    cross_share = cross_share[:, : 4 * width]
     return (
         layer_output[None], input_grad[None], encoder_grad.reshape((1,) + encoder_states.shape[1:]), self_share, cross_share,
-        up_share, down_share, row[13, : up_bias.shape[0]], row[12, : down_bias.shape[0]], row[:12, : vectors.shape[0]].T,
+        up_share, down_share, up_row[0], down_row[0], vector_rows.T,
     )
 
 

time: 265 us -> 252 us (0.951)
  Pallas kernels: 241 us -> 235 us
  local copies, waits for them, and re-layouts: 18.8 us -> 14.5 us
  other arithmetic: 3.95 us -> 0.9 us
    pallas_call x1, Pallas kernels: 18.8 us -> 14.1 us  [ffn(): pl.pallas_call(ffn_kernel, grid=(hidden // size,), in_specs=[rows, rows,...]
    unnamed x8 -> x23, local copies, waits for them, and re-layouts: 10.7 us -> 13.8 us
where the time goes in v4:
time: 252 us; the launch traced here: 251 us
  Pallas kernels  235 us (93%)
  local copies, waits for them, and re-layouts  14.5 us (6%)
    pallas_call x1, Pallas kernels, fused_backward(): pl.pallas_call(backward_kernel, in_specs=[vmem] * 18 + [hbm] * 7, out_spe...  115 us
    pallas_call x1, Pallas kernels, fused_forward(): pl.pallas_call(forward_kernel, in_specs=[pl.BlockSpec(memory_space=pltpu....  106 us
    pallas_call x1, Pallas kernels, ffn(): pl.pallas_call(ffn_kernel, grid=(hidden // size,), in_specs=[rows, rows,...  14.1 us
    unnamed x23, local copies, waits for them, and re-layouts  13.8 us

profile of v4, /device:TPU:0, one launch (start us, length us, event | category | flops | bytes accessed | tf_op | source)
XLA Modules:
  0.0 251.1 jit_solution(1029726413751420811)
XLA Ops:
  0.6 105.9 %fused_forward.1 = (bf16[32,16,128]{2,1,0:T(8,128)(2,1)}, bf16[768,1536]{1,0:T(8,128)(2,1)}, bf16[768,3072]{1,0:T(8,128)(2,1)}, bf16[768,1536]{1,0:T(8,128)(2,1)...) custom-call(s32[1,3]{1,0:T(1,128)} %refs_0_.1, ...), custom_call_target="tpu_custom_call" | custom-call | tf_op jit(solution)/shard_map/fused_forward/pallas_call | solution.py:645
  106.5 0.9 convert_reduce_fusion
  107.4 0.7 reshape.36.bias_ref
  108.1 14.1 %ffn.1 = (bf16[256,768]{1,0:T(8,128)(2,1)}, f32[256,768]{1,0:T(8,128)}, bf16[768,3072]{1,0:T(8,128)(2,1)}, bf16[3072,768]{1,0:T(8,128)(2,1)}, f32[1,3072]{1,0:T(1,128)}, /*index=5*/f32[16,768]{1,0:T(8,128)}) custom-call(bf16[256,768]{1,0:T(8,128)(2,1)} %get-tuple-element.49.normed_ref, bf16[256,768]{1,0:T(8,128)(2,1)} %bitcast.21, ...), custom_call_target="tpu_custom_call" | custom-call | tf_op jit(solution)/shard_map/ffn/pallas_call | solution.py:1211
  122.2 115.1 %fused_backward.1 = (f32[256,768]{1,0:T(8,128)}, f32[13500,1,128]{2,1,0:T(1,128)}, f32[24,3072]{1,0:T(8,128)}, f32[96,768]{1,0:T(8,128)}, f32[24,3072]{1,0:T(8,1...) custom-call(s32[8,768]{1,0:T(8,128)} %get-tuple-element.56.refs_0_, ...), custom_call_target="tpu_custom_call" | custom-call | tf_op jit(solution)/shard_map/fused_backward/pallas_call | solution.py:1137
  237.3 2.1 copy.32
  239.3 0.0 copy-start.3
  239.3 0.0 copy-start.2
  239.3 0.0 copy-start.1
  239.3 0.0 copy-start
  239.3 0.0 copy-start.6
  239.4 0.0 copy-start.5
  239.4 0.0 copy-start.4
  239.4 7.2 %copy.33 = f32[1,3,750,768]{3,0,2,1:T(1,128)} copy(f32[1,3,750,768]{3,0,2,1:T(1,128)} %bitcast.14) | data formatting | bytes 13824000
  246.6 0.0 copy-done.3
  246.6 0.7 copy.34
  247.3 0.0 copy-done.2
  247.3 0.7 copy.35
  248.0 0.0 copy-done.1
  248.0 0.7 copy.36
  248.7 0.0 copy-done
  248.7 0.7 copy.37
  249.5 0.0 copy-done.6
  249.5 0.5 copy.38
  250.0 0.0 copy-done.5
  250.0 0.5 copy.39
  250.5 0.0 copy-done.4
  250.5 0.6 copy.40
Async XLA Ops:
  239.3 7.2 %copy-start.3 = (f32[24,3072]{1,0:T(8,128)S(1)}, f32[24,3072]{1,0:T(8,128)}, u32[]{:S(2)}) copy-start(f32[24,3072]{1,0:T(8,128)} %get-tuple-element.121) | copy-start | bytes 884740
  239.3 8.0 %copy-start.2 = (f32[24,3072]{1,0:T(8,128)S(1)}, f32[24,3072]{1,0:T(8,128)}, u32[]{:S(2)}) copy-start(f32[24,3072]{1,0:T(8,128)} %get-tuple-element.122) | copy-start | bytes 884740
  239.3 8.7 %copy-start.1 = (f32[24,3072]{1,0:T(8,128)S(1)}, f32[24,3072]{1,0:T(8,128)}, u32[]{:S(2)}) copy-start(f32[24,3072]{1,0:T(8,128)} %get-tuple-element.123) | copy-start | bytes 884740
  239.3 9.4 %copy-start = (f32[96,768]{1,0:T(8,128)S(1)}, f32[96,768]{1,0:T(8,128)}, u32[]{:S(2)}) copy-start(f32[96,768]{1,0:T(8,128)} %get-tuple-element.124) | copy-start | bytes 884740
  239.3 10.1 %copy-start.6 = (f32[1,96]{1,0:T(1,128)S(1)}, f32[1,96]{1,0:T(1,128)}, u32[]{:S(2)}) copy-start(f32[1,96]{1,0:T(1,128)} %get-tuple-element.85) | copy-start | bytes 1156
  239.4 10.6 %copy-start.5 = (f32[1,24]{1,0:T(1,128)S(1)}, f32[1,24]{1,0:T(1,128)}, u32[]{:S(2)}) copy-start(f32[1,24]{1,0:T(1,128)} %get-tuple-element.86) | copy-start | bytes 292
  239.4 11.1 %copy-start.4 = (f32[12,24]{1,0:T(8,128)S(1)}, f32[12,24]{1,0:T(8,128)}, u32[]{:S(2)}) copy-start(f32[12,24]{1,0:T(8,128)} %get-tuple-element.87) | copy-start | bytes 3460

commit v5 on v4

--- a/solution.py
+++ b/solution.py
@@ -380,10 +380,11 @@
     (length_ref, x_ref, vectors_in, up_bias_in, down_bias_in, self_in, cross_in, up_in, frames_hbm, down_in) = refs[:10]
     (small_out, ckv_out, self_out, cqo_out, up_out, down_out, kv_out, vec_ref, normed_one_ref, query_ref, kv_row_ref,
      attended_ref, self_lse_ref, after_self_ref, normed_two_ref, row_query_ref, cross_lse_ref, mixed_ref,
-     after_cross_ref, normed_three_ref, bias_ref, seg_ref, info_ref, ranked_hbm) = refs[10:34]
+     after_cross_ref, normed_three_ref, bias_ref, seg_ref, info_ref, ranked_hbm,
+     up_bias_ref) = refs[10:35]
     (frames_in, frames_ref, small_f32, small_in, half_wide, half_narrow, pair_wide, pair_narrow, small_vm, ckv_vm, self_vm, cqo_vm, kv_vm, acc_ref, stat_ref, part_ref, part_stat_ref, give_ref,
      give_stat_ref, take_ref, take_stat_ref, send_sem, recv_sem, own_sem, half_sems, mate_sems, load_sem,
-     frame_sem) = refs[34:]
+     frame_sem) = refs[35:]
     me = Place()
     core = me.core
     width = x_ref.shape[1]
@@ -475,6 +476,13 @@
             [small_vm[d].astype(jnp.float32), jnp.zeros((16, width - 128), jnp.float32)], 1)
         total = total + (block if d == 0 else pltpu.roll(block, d * 24, 1))
     vec_ref[...] = total
+    hidden = up_bias_ref.shape[1]
+    bias = jnp.zeros((1, hidden), jnp.float32)
+    for d in range(32):
+        block = jnp.concatenate(
+            [small_vm[d].astype(jnp.float32)[13:14], jnp.zeros((1, hidden - 128), jnp.float32)], 1)
+        bias = bias + (block if d == 0 else pltpu.roll(block, d * hidden // 32, 1))
+    up_bias_ref[...] = bias
 
     def vec(k):
         return vec_ref[k:k + 1]
@@ -494,7 +502,7 @@
         shift = vec_ref[10:11, columns(tile % 3, 256)] * is_value
         kv_vm[clip, :frames_ref.shape[1], columns(tile, 256)] = (result + shift).astype(jnp.bfloat16)
 
-    early, middle = 9, 13
+    early, middle = 6, 12
     loop_with(gather, early, 20, 0.65, project)
     gather.run_until(31)
     gather.need(2)
@@ -640,7 +648,7 @@
         (vmem, shape((2 * toks, width), low)), (vmem, shape((pairs, 2, toks), full)), (vmem, shape((toks, width), full)),
         (vmem, shape((toks, width), full)), (vmem, shape((toks, width), low)),
         (vmem, shape((2 * toks, toks), full)), (vmem, shape((1, 2 * toks), jnp.int32)), (vmem, shape((8, width), jnp.int32)),
-        (hbm, shape(frames.shape, low)),
+        (hbm, shape(frames.shape, low)), (vmem, shape((1, 4 * width), full)),
     ]
     return pl.pallas_call(
         forward_kernel,
@@ -1438,15 +1446,14 @@
     down_bias,
     vectors,
 ):
-    small_blocks, ckv_full, self_full, cqo_full, up_full, down_full, cross_kv, vec, normed_one, query, kv_row, attended, \
+    _, ckv_full, self_full, cqo_full, up_full, down_full, cross_kv, vec, normed_one, query, kv_row, attended, \
         self_lse, after_self, normed_two, row_query, cross_lse, mixed_full, after_cross, normed_three, mask_bias, \
-        row_segment, info, frames = fused_forward(
+        row_segment, info, frames, bias_row = fused_forward(
             clip_lengths, layer_input[0], vectors.T, up_bias[None], down_bias[None], self_weights, cross_weights, up_weights,
             encoder_states[0], down_weights,
         )
-    bias_full = small_blocks[:, 13, : up_bias.shape[0]].reshape(-1).astype(jnp.float32)
     layer_output, grad_after_cross, grad_up, grad_down, grad_up_bias, ffn_rows = ffn(
-        normed_three, out_grad[0], after_cross, vec, up_full, bias_full[None], down_full
+        normed_three, out_grad[0], after_cross, vec, up_full, bias_row, down_full
     )
     large = [g.reshape(32, -1, g.shape[1]) for g in (grad_up, grad_down)]
     input_grad, encoder_grad, up_share, down_share, cross_share, self_share, up_row, down_row, vector_rows, *_ = fused_backward(

time: 252 us -> 249 us (0.988)
  no operation moved by 1% of the time
where the time goes in v5:
time: 249 us
  Pallas kernels  234 us (94%)
  local copies, waits for them, and re-layouts  13.8 us (6%)
    pallas_call x1, Pallas kernels, fused_backward(): pl.pallas_call(backward_kernel, in_specs=[vmem] * 18 + [hbm] * 7, out_spe...  115 us
    pallas_call x1, Pallas kernels, fused_forward(): pl.pallas_call(forward_kernel, in_specs=[pl.BlockSpec(memory_space=pltpu....  105 us
    pallas_call x1, Pallas kernels, ffn(): pl.pallas_call(ffn_kernel, grid=(hidden // size,), in_specs=[rows, rows,...  14.1 us
    unnamed x23, local copies, waits for them, and re-layouts  13.8 us

profile of v5, /device:TPU:0, one launch (start us, length us, event | category | flops | bytes accessed | tf_op | source)
XLA Modules:
  0.0 248.6 jit_solution(3233939856991970203)
XLA Ops:
  0.6 104.8 %fused_forward.1 = (bf16[32,16,128]{2,1,0:T(8,128)(2,1)}, bf16[768,1536]{1,0:T(8,128)(2,1)}, bf16[768,3072]{1,0:T(8,128)(2,1)}, bf16[768,1536]{1,0:T(8,128)(2,1)...) custom-call(s32[1,3]{1,0:T(1,128)} %refs_0_.1, ...), custom_call_target="tpu_custom_call" | custom-call | tf_op jit(solution)/shard_map/fused_forward/pallas_call | solution.py:653
  105.5 14.1 %ffn.1 = (bf16[256,768]{1,0:T(8,128)(2,1)}, f32[256,768]{1,0:T(8,128)}, bf16[768,3072]{1,0:T(8,128)(2,1)}, bf16[3072,768]{1,0:T(8,128)(2,1)}, f32[1,3072]{1,0:T(1,128)}, /*index=5*/f32[16,768]{1,0:T(8,128)}) custom-call(bf16[256,768]{1,0:T(8,128)(2,1)} %get-tuple-element.49.normed_ref, bf16[256,768]{1,0:T(8,128)(2,1)} %bitcast.21, ...), custom_call_target="tpu_custom_call" | custom-call | tf_op jit(solution)/shard_map/ffn/pallas_call | solution.py:1219
  119.5 115.3 %fused_backward.1 = (f32[256,768]{1,0:T(8,128)}, f32[13500,1,128]{2,1,0:T(1,128)}, f32[24,3072]{1,0:T(8,128)}, f32[96,768]{1,0:T(8,128)}, f32[24,3072]{1,0:T(8,1...) custom-call(s32[8,768]{1,0:T(8,128)} %get-tuple-element.56.refs_0_, ...), custom_call_target="tpu_custom_call" | custom-call | tf_op jit(solution)/shard_map/fused_backward/pallas_call | solution.py:1145
  234.8 2.1 copy.32
  236.9 0.0 copy-start.3
  236.9 0.0 copy-start.2
  236.9 0.0 copy-start.1
  236.9 0.0 copy-start
  236.9 0.0 copy-start.6
  236.9 0.0 copy-start.5
  236.9 0.0 copy-start.4
  236.9 7.2 %copy.33 = f32[1,3,750,768]{3,0,2,1:T(1,128)} copy(f32[1,3,750,768]{3,0,2,1:T(1,128)} %bitcast.14) | data formatting | bytes 13824000
  244.1 0.0 copy-done.3
  244.1 0.7 copy.34
  244.8 0.0 copy-done.2
  244.8 0.7 copy.35
  245.6 0.0 copy-done.1
  245.6 0.7 copy.36
  246.3 0.0 copy-done
  246.3 0.7 copy.37
  247.0 0.0 copy-done.6
  247.0 0.5 copy.38
  247.5 0.0 copy-done.5
  247.5 0.5 copy.39
  248.0 0.0 copy-done.4
  248.0 0.6 copy.40
Async XLA Ops:
  236.9 7.2 %copy-start.3 = (f32[24,3072]{1,0:T(8,128)S(1)}, f32[24,3072]{1,0:T(8,128)}, u32[]{:S(2)}) copy-start(f32[24,3072]{1,0:T(8,128)} %get-tuple-element.121) | copy-start | bytes 884740
  236.9 8.0 %copy-start.2 = (f32[24,3072]{1,0:T(8,128)S(1)}, f32[24,3072]{1,0:T(8,128)}, u32[]{:S(2)}) copy-start(f32[24,3072]{1,0:T(8,128)} %get-tuple-element.122) | copy-start | bytes 884740
  236.9 8.7 %copy-start.1 = (f32[24,3072]{1,0:T(8,128)S(1)}, f32[24,3072]{1,0:T(8,128)}, u32[]{:S(2)}) copy-start(f32[24,3072]{1,0:T(8,128)} %get-tuple-element.123) | copy-start | bytes 884740
  236.9 9.4 %copy-start = (f32[96,768]{1,0:T(8,128)S(1)}, f32[96,768]{1,0:T(8,128)}, u32[]{:S(2)}) copy-start(f32[96,768]{1,0:T(8,128)} %get-tuple-element.124) | copy-start | bytes 884740
  236.9 10.1 %copy-start.6 = (f32[1,96]{1,0:T(1,128)S(1)}, f32[1,96]{1,0:T(1,128)}, u32[]{:S(2)}) copy-start(f32[1,96]{1,0:T(1,128)} %get-tuple-element.85) | copy-start | bytes 1156
  236.9 10.6 %copy-start.5 = (f32[1,24]{1,0:T(1,128)S(1)}, f32[1,24]{1,0:T(1,128)}, u32[]{:S(2)}) copy-start(f32[1,24]{1,0:T(1,128)} %get-tuple-element.86) | copy-start | bytes 292
  236.9 11.1 %copy-start.4 = (f32[12,24]{1,0:T(8,128)S(1)}, f32[12,24]{1,0:T(8,128)}, u32[]{:S(2)}) copy-start(f32[12,24]{1,0:T(8,128)} %get-tuple-element.87) | copy-start | bytes 3460
